TPU v7x, 128 devices: a whole 4x4x4 slice. The times are simulated.
128 devices in a mesh: pipe: 2 (over x_hi), expert: 16 (over x_lo, y, core), tensor: 4 (over z).
Axes of the slice: x: 4 (x_hi: 2, x_lo: 2; x = x_hi * 2 + x_lo), y: 4, z: 4, core: 2. Of those that a mesh axis runs over, the one named last changes fastest.
Arguments:
- fwd_in: bfloat16 [2, 1024, 3072], P('pipe', 'expert', 'tensor'), may hold values from -6 to 6
- bwd_in: bfloat16 [2, 1024, 3072], P('pipe', 'expert', 'tensor'), may hold values from -6 to 6
- cotangent: bfloat16 [2, 1024, 3072], P('pipe', 'expert', 'tensor'), may hold values from -6 to 6
- route_fwd: int32 [2, 1024, 4], P('pipe', 'expert'), may hold values from 0 to 15, as said below
- gate_fwd: int32 [2, 1024, 4], P('pipe', 'expert'), may hold values from 4096 to 32767
- route_bwd: int32 [2, 1024, 4], P('pipe', 'expert'), may hold values from 0 to 15, as said below
- gate_bwd: int32 [2, 1024, 4], P('pipe', 'expert'), may hold values from 4096 to 32767
- w_gate: bfloat16 [2, 16, 5376, 3072], P('pipe', 'expert', 'tensor'), may hold values from -0.109375 to 0.109375
- w_up: bfloat16 [2, 16, 5376, 3072], P('pipe', 'expert', 'tensor'), may hold values from -0.109375 to 0.109375
- w_down: bfloat16 [2, 16, 5376, 3072], P('pipe', 'expert', 'tensor'), may hold values from -0.078125 to 0.078125
Outputs:
- next_inputs: bfloat16 [2, 1024, 3072], P('pipe', 'expert', 'tensor')
- next_grads: bfloat16 [2, 1024, 3072], P('pipe', 'expert', 'tensor')
Inputs may be any that keep to these rules, and one draw needn't show every extreme that they name: `route_fwd`: each row names 4 different experts. Within each aligned block of 64 rows of a section no expert is named by more than 24 rows, and in each section one expert is named by exactly 24 rows of every block. `route_bwd`: each row names 4 different experts. Within each aligned block of 64 rows of a section no expert is named by more than 24 rows, and in each section one expert is named by exactly 24 rows of every block.
All inputs are finite; a program needn't handle non-finite values.
Results may differ from a plain program's by a relative error of at most 0.004.
Values may be sent and summed in bfloat16 or wider, within the bound.
No kernel may reach another device: no remote copies, remote signals or barrier semaphores. Data moves between devices by JAX's collectives and lax.ppermute only.
A program may use at most 128 MiB of HBM per device.

v0:
```python
import jax
import jax.numpy as jnp
from jax import lax
from jax.sharding import PartitionSpec as P


def passed_along(shard, axis, by):
    length = lax.axis_size(axis)
    return lax.ppermute(shard, axis, [(i, (i + by) % length) for i in range(length)])


def slot_targets(route_rows, experts, capacity):
    flat_ids = route_rows.reshape(-1)
    one_hot = (flat_ids[:, None] == jnp.arange(experts, dtype=jnp.int32)[None, :]).astype(jnp.int32)
    earlier = jnp.cumsum(one_hot, axis=0) - one_hot
    slot_rank = jnp.sum(earlier * one_hot, axis=1)
    return (flat_ids * capacity + slot_rank, jnp.sum(one_hot, axis=0))


def scatter_slots(features, targets, experts, capacity, fanout):
    repeated = jnp.repeat(features, fanout, axis=0)
    buffer_rows = jnp.zeros((experts * capacity, features.shape[1]), features.dtype)
    return buffer_rows.at[targets].set(repeated).reshape(experts, capacity, features.shape[1])


def gather_slots(returned, targets, gate_ints, residual):
    tokens_here, fanout = gate_ints.shape
    gate_values = gate_ints.astype(jnp.float32) / 65536.0
    picked = returned.reshape(-1, returned.shape[-1])[targets].reshape(tokens_here, fanout, -1)
    mixed = jnp.sum(gate_values[:, :, None] * picked.astype(jnp.float32), axis=1)
    return (residual.astype(jnp.float32) + mixed).astype(jnp.bfloat16)


def contract_model(activations, weight):
    return lax.dot_general(
        activations, weight, (((1,), (1,)), ((), ())), preferred_element_type=jnp.float32
    )


def expert_forward(activations, gate_weight, up_weight, down_weight):
    pre_gate = contract_model(activations, gate_weight)
    pre_up = contract_model(activations, up_weight)
    hidden = (jax.nn.silu(pre_gate) * pre_up).astype(jnp.bfloat16)
    return jnp.dot(hidden, down_weight, preferred_element_type=jnp.float32)


def expert_backward(activations, upstream, gate_weight, up_weight, down_weight):
    pre_gate = contract_model(activations, gate_weight)
    pre_up = contract_model(activations, up_weight)
    sigmoid_gate = jax.nn.sigmoid(pre_gate)
    hidden_grad = contract_model(upstream, down_weight)
    gate_grad = (
        hidden_grad * pre_up * sigmoid_gate * (1.0 + pre_gate * (1.0 - sigmoid_gate))
    ).astype(jnp.bfloat16)
    up_grad = (hidden_grad * pre_gate * sigmoid_gate).astype(jnp.bfloat16)
    return jnp.dot(gate_grad, gate_weight, preferred_element_type=jnp.float32) + jnp.dot(
        up_grad, up_weight, preferred_element_type=jnp.float32
    )


def local(
    fwd_in, bwd_in, cotangent, route_fwd, gate_fwd, route_bwd, gate_bwd, w_gate, w_up, w_down
):
    experts = lax.axis_size("expert")
    tokens_here = fwd_in.shape[1]
    fanout = route_fwd.shape[2]
    capacity = min(tokens_here, max(2, tokens_here * fanout * 3 // (2 * experts)))
    slot_total = experts * capacity
    gate_mat = w_gate[0, 0]
    up_mat = w_up[0, 0]
    down_mat = w_down[0, 0]
    targets_fwd, load_fwd = slot_targets(route_fwd[0], experts, capacity)
    targets_bwd, load_bwd = slot_targets(route_bwd[0], experts, capacity)
    send_fwd = scatter_slots(fwd_in[0], targets_fwd, experts, capacity, fanout)
    send_bwd = scatter_slots(bwd_in[0], targets_bwd, experts, capacity, fanout)
    send_upstream = scatter_slots(cotangent[0], targets_bwd, experts, capacity, fanout)
    recv_fwd, recv_bwd, recv_upstream = (
        lax.all_to_all(send_fwd, "expert", split_axis=0, concat_axis=0, tiled=True),
        lax.all_to_all(send_bwd, "expert", split_axis=0, concat_axis=0, tiled=True),
        lax.all_to_all(send_upstream, "expert", split_axis=0, concat_axis=0, tiled=True),
    )
    quarter = recv_fwd.shape[2]
    rows_fwd, rows_bwd, rows_upstream = (
        lax.all_gather(recv_fwd.reshape(slot_total, quarter), "tensor", axis=1, tiled=True),
        lax.all_gather(recv_bwd.reshape(slot_total, quarter), "tensor", axis=1, tiled=True),
        lax.all_gather(recv_upstream.reshape(slot_total, quarter), "tensor", axis=1, tiled=True),
    )
    partial_fwd = expert_forward(rows_fwd, gate_mat, up_mat, down_mat)
    partial_bwd = expert_backward(rows_bwd, rows_upstream, gate_mat, up_mat, down_mat)
    total_fwd, total_bwd = lax.psum((partial_fwd, partial_bwd), "tensor")
    offset = lax.axis_index("tensor") * quarter
    share_fwd = lax.dynamic_slice_in_dim(total_fwd, offset, quarter, 1)
    share_bwd = lax.dynamic_slice_in_dim(total_bwd, offset, quarter, 1)
    back_fwd, back_bwd = (
        lax.all_to_all(
            share_fwd.astype(jnp.bfloat16).reshape(experts, capacity, quarter),
            "expert",
            split_axis=0,
            concat_axis=0,
            tiled=True,
        ),
        lax.all_to_all(
            share_bwd.astype(jnp.bfloat16).reshape(experts, capacity, quarter),
            "expert",
            split_axis=0,
            concat_axis=0,
            tiled=True,
        ),
    )
    out_fwd = gather_slots(back_fwd, targets_fwd, gate_fwd[0], fwd_in[0])
    out_bwd = gather_slots(back_bwd, targets_bwd, gate_bwd[0], cotangent[0])
    next_inputs = passed_along(out_fwd[None], "pipe", 1)
    next_grads = passed_along(out_bwd[None], "pipe", -1)
    return (next_inputs, next_grads)


def solution(mesh):
    placed = (
        P("pipe", "expert", "tensor"),
        P("pipe", "expert", "tensor"),
        P("pipe", "expert", "tensor"),
        P("pipe", "expert", None),
        P("pipe", "expert", None),
        P("pipe", "expert", None),
        P("pipe", "expert", None),
        P("pipe", "expert", "tensor", None),
        P("pipe", "expert", "tensor", None),
        P("pipe", "expert", "tensor", None),
    )
    return jax.shard_map(
        local,
        mesh=mesh,
        in_specs=placed,
        out_specs=(P("pipe", "expert", "tensor"), P("pipe", "expert", "tensor")),
        check_vma=False,
    )
```

profile of v0, /device:TPU:0, one launch (start us, length us, event | category | flops | bytes accessed | tf_op | source)
XLA Modules:
  0.0 379.3 jit_solution(4849225312204875735)
XLA Ops:
  7.2 0.8 copy.21
  8.2 0.7 broadcast_multiply_fusion
  9.9 1.0 broadcast_in_dim.8
  11.1 1.8 scatter_custom_fusion.2
  12.9 17.1 %all_to_all.25 = bf16[16,24,768]{2,1,0:T(8,128)(2,1)} all-to-all(bf16[16,24,768]{2,1,0:T(8,128)(2,1)S(1)} %bitcast.114), channel_id=1, replica_groups=mesh['pipe'=2,'expert'=16,'tensor'=4] {'expert'}, dimensions={0} | all-to-all | bytes 1179648 | tf_op jit(solution)/shard_map/all_to_all | solution.py:79
  30.3 1.8 scatter_custom_fusion.1
  32.1 14.8 %all_to_all.26 = bf16[16,24,768]{2,1,0:T(8,128)(2,1)} all-to-all(bf16[16,24,768]{2,1,0:T(8,128)(2,1)S(1)} %bitcast.115), channel_id=1, replica_groups=mesh['pipe'=2,'expert'=16,'tensor'=4] {'expert'}, dimensions={0} | all-to-all | bytes 1179648 | tf_op jit(solution)/shard_map/all_to_all | solution.py:80
  48.7 2.5 scatter_custom_fusion
  51.2 3.6 all-to-all-start
  55.0 11.3 %all-to-all-done = bf16[16,24,768]{2,1,0:T(8,128)(2,1)S(1)} async-done(((bf16[16,24,768]{2,1,0:T(8,128)(2,1)}), bf16[16,24,768]{2,1,0:T(8,128)(2,1)S(1)}, u32[]{:S(2)}, u32[]{:S(2)}) %all-to-all-start) | async-done | bytes 589856 | tf_op jit(solution)/shard_map/all_to_all | solution.py:78
  66.3 0.8 copy-done
  67.2 9.8 %fusion.12 = f32[384,1344]{0,1:T(8,128)} fusion(bf16[384,3072]{1,0:T(8,128)(2,1)} %all-gather.8.cloned.1.call-done, bf16[1,1,1344,3072]{3,2,1,0:T(8,128)(2,1)} %param.17), kind=kOutput, calls=%fused_computation.17 | convolution fusion | flops 3170893824 | bytes 12681216 | tf_op jit(solution)/shard_map/dot_general | solution.py:35
  77.0 21.4 %all-gather.6.cloned.1.call-done = bf16[384,3072]{1,0:T(8,128)(2,1)} async-done(((bf16[384,768]{1,0:T(8,128)(2,1)}), bf16[384,3072]{1,0:T(8,128)(2,1)}) %all-gather.6.cloned.1.call-update) | async-done | bytes 2359312 | tf_op jit(solution)/shard_map/all_gather | solution.py:86
  98.4 7.9 %fusion = f32[384,1344]{0,1:T(8,128)S(1)} fusion(bf16[384,3072]{1,0:T(8,128)(2,1)} %all-gather.6.cloned.1.call-done, bf16[1,1,1344,3072]{3,2,1,0:T(8,128)(2,1)} %param.19), kind=kOutput, calls=%fused_computation.5 | convolution fusion | flops 3170893824 | bytes 12681216 | tf_op jit(solution)/shard_map/dot_general | solution.py:35
  106.4 1.4 copy-done.9
  107.8 10.2 %fusion.4 = f32[384,3072]{1,0:T(8,128)} fusion(bf16[1,1,1344,3072]{3,2,1,0:T(8,128)(2,1)} %param.18, f32[384,1344]{0,1:T(8,128)S(1)} %fusion, f32[384,1344]{0,1:T(8,128)S(1)} %copy-done.8), kind=kOutput, calls=%fused_computation.9 | convolution fusion | flops 3173990400 | bytes 17104896 | tf_op jit(solution)/shard_map/dot_general | solution.py:56
  118.0 19.2 %fusion.16 = f32[384,3072]{1,0:T(8,128)} fusion(f32[384,3072]{1,0:T(8,128)} %fusion.4, bf16[1,1,1344,3072]{3,2,1,0:T(8,128)(2,1)} %param.17, f32[384,1344]{0,1:T(8,128)} %copy-done.9, bf16[384,3072]{1,0:T(8,128)(2,1)S(1)} %copy-done.6, bf16[1,1,1344,3072]{3,2,1,0:T(8,128)(2,1)} %param.18, f32[384,1344]{0,1:T(8,128)} %fusion.12), kind=kOutput, calls=%fused_computation.21 | convolution fusion | flops 6348128256 | bytes 32440320 | tf_op jit(solution)/shard_map/dot_general | solution.py:56
  137.2 10.3 %fusion.14 = f32[384,1344]{0,1:T(8,128)} fusion(bf16[384,3072]{1,0:T(8,128)(2,1)} %all-gather.4.cloned.1.call-done, bf16[1,1,1344,3072]{3,2,1,0:T(8,128)(2,1)} %param.17), kind=kOutput, calls=%fused_computation.19 | convolution fusion | flops 3170893824 | bytes 12681216 | tf_op jit(solution)/shard_map/dot_general | solution.py:35
  147.5 16.8 %fusion.2 = f32[384,3072]{1,0:T(8,128)} fusion(bf16[1,1,1344,3072]{3,2,1,0:T(8,128)(2,1)} %param.19, bf16[384,3072]{1,0:T(8,128)(2,1)S(1)} %copy-done.7, bf16[1,1,1344,3072]{3,2,1,0:T(8,128)(2,1)} %param.18, f32[384,1344]{0,1:T(8,128)} %fusion.14), kind=kOutput, calls=%fused_computation.7 | convolution fusion | flops 6344884224 | bytes 25657344 | tf_op jit(solution)/shard_map/dot_general | solution.py:44
  164.2 164.2 %all-reduce.2 = (bf16[384,3072]{1,0:T(8,128)(2,1)S(1)}, bf16[384,3072]{1,0:T(8,128)(2,1)}) all-reduce(f32[384,3072]{1,0:T(8,128)} %fusion.2, f32[384,3072]{1,0:T(8,128)} %fusion.16), channel_id=1, replica_groups=mesh['pipe'=2,'expert'=16,'tensor'=4] {'tensor'}, use_global_device_ids=true, to_apply=%region_4.5 | all-reduce | flops 2359296 | bytes 14155776 | tf_op jit(solution)/shard_map/psum | solution.py:90
  328.4 1.9 dynamic-slice_convert_fusion
  330.3 5.3 %all-to-all-start.4 = ((bf16[16,24,768]{2,1,0:T(8,128)(2,1)}), bf16[16,24,768]{2,1,0:T(8,128)(2,1)S(1)}, u32[]{:S(2)}, u32[]{:S(2)}) async-start(bf16[16,24,768]{2,1,0:T(8,128)(2,1)} %bitcast.23), calls=%async_computation.4 | async-start | bytes 1179648 | tf_op jit(solution)/shard_map/all_to_all | solution.py:102
  335.7 0.9 dynamic-slice_convert_fusion.1
  336.6 10.7 %all-to-all-done.4 = bf16[16,24,768]{2,1,0:T(8,128)(2,1)S(1)} async-done(((bf16[16,24,768]{2,1,0:T(8,128)(2,1)}), bf16[16,24,768]{2,1,0:T(8,128)(2,1)S(1)}, u32[]{:S(2)}, u32[]{:S(2)}) %all-to-all-start.4) | async-done | bytes 589856 | tf_op jit(solution)/shard_map/all_to_all | solution.py:102
  347.3 3.9 %all-to-all-start.1 = ((bf16[16,24,768]{2,1,0:T(8,128)(2,1)}), bf16[16,24,768]{2,1,0:T(8,128)(2,1)S(1)}, u32[]{:S(2)}, u32[]{:S(2)}) async-start(bf16[16,24,768]{2,1,0:T(8,128)(2,1)} %bitcast.10), calls=%async_computation.1 | async-start | bytes 1179648 | tf_op jit(solution)/shard_map/all_to_all | solution.py:95
  351.3 1.2 gather_fusion.1
  353.3 2.8 collective-permute-start.1
  356.0 6.8 %all-to-all-done.1 = bf16[16,24,768]{2,1,0:T(8,128)(2,1)S(1)} async-done(((bf16[16,24,768]{2,1,0:T(8,128)(2,1)}), bf16[16,24,768]{2,1,0:T(8,128)(2,1)S(1)}, u32[]{:S(2)}, u32[]{:S(2)}) %all-to-all-start.1) | async-done | bytes 589856 | tf_op jit(solution)/shard_map/all_to_all | solution.py:95
  362.9 1.2 gather_fusion
  364.8 2.8 collective-permute-start
  367.6 3.4 collective-permute-done
  371.0 0.6 copy.34
  (69 shorter events, 6.0 us)
Async XLA Ops:
  7.2 22.9 %copy-start.1 = (bf16[1,64,768]{2,1,0:T(8,128)(2,1)S(1)}, bf16[1,64,768]{2,1,0:T(8,128)(2,1)}, u32[]{:S(2)}) copy-start(bf16[1,64,768]{2,1,0:T(8,128)(2,1)} %param.12) | copy-start | bytes 294916
  7.2 60.0 %all-gather.8.cloned.1.call-start = ((), (), s32[]{:S(2)}) async-start(), calls=%async_computation.7 | async-start | bytes 2949120 | tf_op jit(solution)/shard_map/all_gather | solution.py:85
  30.0 17.0 %copy-start.3 = (s32[1,64,4]{1,2,0:T(4,128)S(1)}, s32[1,64,4]{1,2,0:T(4,128)}, u32[]{:S(2)}) copy-start(s32[1,64,4]{1,2,0:T(4,128)} %param.13) | copy-start | bytes 3076
  30.0 18.4 %copy-start.2 = (bf16[1,64,768]{2,1,0:T(8,128)(2,1)S(1)}, bf16[1,64,768]{2,1,0:T(8,128)(2,1)}, u32[]{:S(2)}) copy-start(bf16[1,64,768]{2,1,0:T(8,128)(2,1)} %param.10) | copy-start | bytes 294916
  30.0 68.4 %all-gather.6.cloned.1.call-start = ((), (), s32[]{:S(2)}) async-start(), calls=%async_computation.6 | async-start | bytes 2949120 | tf_op jit(solution)/shard_map/all_gather | solution.py:86
  51.2 15.2 %all-to-all-start = ((bf16[16,24,768]{2,1,0:T(8,128)(2,1)}), bf16[16,24,768]{2,1,0:T(8,128)(2,1)S(1)}, u32[]{:S(2)}, u32[]{:S(2)}) async-start(bf16[16,24,768]{2,1,0:T(8,128)(2,1)} %bitcast.5), calls=%async_computation | async-start | bytes 1179648 | tf_op jit(solution)/shard_map/all_to_all | solution.py:78
  54.8 82.5 %all-gather.4.cloned.1.call-start = ((), (), s32[]{:S(2)}) async-start(), calls=%async_computation.5 | async-start | bytes 2949120 | tf_op jit(solution)/shard_map/all_gather | solution.py:84
  66.3 0.8 copy-start
  98.4 9.3 %copy-start.8 = (f32[384,1344]{0,1:T(8,128)S(1)}, f32[384,1344]{0,1:T(8,128)}, u32[]{:S(2)}) copy-start(f32[384,1344]{0,1:T(8,128)} %fusion.12) | copy-start | bytes 6193156
  106.4 1.4 copy-start.9
  107.8 10.2 %copy-start.6 = (bf16[384,3072]{1,0:T(8,128)(2,1)S(1)}, bf16[384,3072]{1,0:T(8,128)(2,1)}, u32[]{:S(2)}) copy-start(bf16[384,3072]{1,0:T(8,128)(2,1)} %all-gather.8.cloned.1.call-done) | copy-start | bytes 7077892
  137.2 10.3 %copy-start.7 = (bf16[384,3072]{1,0:T(8,128)(2,1)S(1)}, bf16[384,3072]{1,0:T(8,128)(2,1)}, u32[]{:S(2)}) copy-start(bf16[384,3072]{1,0:T(8,128)(2,1)} %all-gather.4.cloned.1.call-done) | copy-start | bytes 7077892
  328.4 7.3 %copy-start.4 = (s32[1,64,4]{1,2,0:T(4,128)S(1)}, s32[1,64,4]{1,2,0:T(4,128)}, u32[]{:S(2)}) copy-start(s32[1,64,4]{1,2,0:T(4,128)} %param.16) | copy-start | bytes 3076
  328.4 7.3 %copy-start.5 = (s32[1,64,4]{1,2,0:T(4,128)S(1)}, s32[1,64,4]{1,2,0:T(4,128)}, u32[]{:S(2)}) copy-start(s32[1,64,4]{1,2,0:T(4,128)} %param.14) | copy-start | bytes 3076
  330.3 16.9 %all-to-all-start.4 = ((bf16[16,24,768]{2,1,0:T(8,128)(2,1)}), bf16[16,24,768]{2,1,0:T(8,128)(2,1)S(1)}, u32[]{:S(2)}, u32[]{:S(2)}) async-start(bf16[16,24,768]{2,1,0:T(8,128)(2,1)} %bitcast.23), calls=%async_computation.4 | async-start | bytes 1179648 | tf_op jit(solution)/shard_map/all_to_all | solution.py:102
  347.3 15.6 %all-to-all-start.1 = ((bf16[16,24,768]{2,1,0:T(8,128)(2,1)}), bf16[16,24,768]{2,1,0:T(8,128)(2,1)S(1)}, u32[]{:S(2)}, u32[]{:S(2)}) async-start(bf16[16,24,768]{2,1,0:T(8,128)(2,1)} %bitcast.10), calls=%async_computation.1 | async-start | bytes 1179648 | tf_op jit(solution)/shard_map/all_to_all | solution.py:95
  353.3 14.3 %collective-permute-start.1 = (bf16[1,64,768]{2,1,0:T(8,128)(2,1)S(1)}, bf16[1,64,768]{2,1,0:T(8,128)(2,1)S(1)}, u32[]{:S(2)}, u32[]{:S(2)}) collective-permute-start(bf16[1,64,768]{2,1,0:T(8,128)(2,1)S(1)} %fusion.50), channel_id=1, source_target_pairs={{0,64},{64,0},{1,65},{65,1},{2,66},{66,2},{3,67},{67,3},{4,68},{68... | collective-permute-start | bytes 294920 | tf_op jit(solution)/shard_map/ppermute | solution.py:9
  364.8 6.2 %collective-permute-start = (bf16[1,64,768]{2,1,0:T(8,128)(2,1)S(1)}, bf16[1,64,768]{2,1,0:T(8,128)(2,1)S(1)}, u32[]{:S(2)}, u32[]{:S(2)}) collective-permute-start(bf16[1,64,768]{2,1,0:T(8,128)(2,1)S(1)} %fusion.51), channel_id=1, source_target_pairs={{0,64},{64,0},{1,65},{65,1},{2,66},{66,2},{3,67},{67,3},{4,68},{68... | collective-permute-start | bytes 294920 | tf_op jit(solution)/shard_map/ppermute | solution.py:9
Sparse Core Ops, SparseCore 0:
  30.2 33.3 all-gather.7
  65.2 33.1 all-gather.5
  100.1 33.1 all-gather.3
where the time goes:
time: 385 us; the launch traced here: 379 us
  blocking collectives  196 us (51%)
  matrix products  74.2 us (19%)
  waiting for transfers between devices  53.8 us (14%)
  local copies, waits for them, and re-layouts  18.9 us (5%)
  starting transfers between devices  18.6 us (5%)
  between operations  14.5 us (4%)
    psum x1, blocking collectives, local(): total_fwd, total_bwd = lax.psum((partial_fwd, partial_bwd), 'tensor')  164 us
    dot_general x3, matrix products, contract_model(): lax.dot_general(activations, weight, (((1,), (1,)), ((), ())), preferred_...  28 us
    all_gather x1, waiting for transfers between devices, local(): lax.all_gather(recv_upstream.reshape(slot_total, quarter), 'tensor', axis...  21.4 us
    dot_general x1, matrix products, expert_backward(): jnp.dot(gate_grad, gate_weight, preferred_element_type=jnp.float32)  19.2 us
    all_to_all x1, blocking collectives, local(): lax.all_to_all(send_bwd, 'expert', split_axis=0, concat_axis=0, tiled=True)  17.1 us
    dot_general x1, matrix products, expert_forward(): return jnp.dot(hidden, down_weight, preferred_element_type=jnp.float32)  16.8 us
    all_to_all x1, blocking collectives, local(): lax.all_to_all(send_upstream, 'expert', split_axis=0, concat_axis=0, tile...  14.8 us
    all_to_all x1, waiting for transfers between devices, local(): lax.all_to_all(send_fwd, 'expert', split_axis=0, concat_axis=0, tiled=True)  11.3 us
  transfers between devices with their start and end apart: 8, of which 5 were waited for; matrix products, arithmetic and copies ran while one was open for 15% of the time, Pallas kernels for 0%

commit v1 on v0

v1 whole, which is shorter than its diff:
```python
import functools

import jax
import jax.numpy as jnp
from jax import lax
from jax.experimental import pallas as pl
from jax.experimental.pallas import tpu as pltpu
from jax.sharding import PartitionSpec as P

F32 = jnp.float32
BF16 = jnp.bfloat16
VMEM_LIMIT = 56 * 1024 * 1024


def params():
    return pltpu.CompilerParams(vmem_limit_bytes=VMEM_LIMIT)


def contract_last(rows, weight):
    return lax.dot_general(rows, weight, (((1,), (1,)), ((), ())), preferred_element_type=F32)


def contract_first(table, rows):
    return lax.dot_general(table, rows, (((0,), (0,)), ((), ())), preferred_element_type=F32)


def shift(shard, axis, by):
    length = lax.axis_size(axis)
    return lax.ppermute(shard, axis, [(i, (i + by) % length) for i in range(length)])


def after(value, *earlier):
    return lax.optimization_barrier((value, *earlier))[0]


def slot_tables(route, gate, experts, capacity):
    tokens, fanout = route.shape
    slots = experts * capacity
    labels = lax.broadcasted_iota(jnp.int32, (tokens, experts), 1)
    picks = [(route[:, k : k + 1] == labels).astype(F32) for k in range(fanout)]
    member = functools.reduce(jnp.add, picks)
    row = lax.broadcasted_iota(jnp.int32, (tokens, tokens), 0)
    column = lax.broadcasted_iota(jnp.int32, (tokens, tokens), 1)
    earlier = (column < row).astype(BF16)
    rank = jnp.dot(earlier, member.astype(BF16), preferred_element_type=F32)
    place = rank + (labels * capacity).astype(F32)
    slot_ids = lax.broadcasted_iota(jnp.int32, (tokens, slots), 1)
    table = jnp.zeros((tokens, slots), F32)
    high = jnp.zeros((tokens, slots), F32)
    low = jnp.zeros((tokens, slots), F32)
    for k in range(fanout):
        target = jnp.sum(picks[k] * place, axis=1, keepdims=True).astype(jnp.int32)
        hit = (slot_ids == target).astype(F32)
        gate_k = gate[:, k : k + 1]
        high_k = ((gate_k >> 7) << 7).astype(F32) * (1.0 / 65536.0)
        low_k = (gate_k & 127).astype(F32) * (1.0 / 65536.0)
        table += hit
        high += hit * high_k
        low += hit * low_k
    return table.astype(BF16), jnp.concatenate([high, low], axis=0).astype(BF16)


def dispatch_kernel(experts, capacity, rf, gf, rb, gb, f, c, send, table_b, mix_f, mix_b):
    quarter = f.shape[1]
    table, mix_f[...] = slot_tables(rf[...], gf[...], experts, capacity)
    send[:, :quarter] = contract_first(table, f[...]).astype(BF16)
    table, mix_b[...] = slot_tables(rb[...], gb[...], experts, capacity)
    table_b[...] = table
    send[:, quarter:] = contract_first(table, c[...]).astype(BF16)


def dispatch(rf, gf, rb, gb, f, c, experts, capacity):
    tokens, quarter = f.shape
    slots = experts * capacity
    return pl.pallas_call(
        functools.partial(dispatch_kernel, experts, capacity),
        out_shape=(
            jax.ShapeDtypeStruct((slots, 2 * quarter), BF16),
            jax.ShapeDtypeStruct((tokens, slots), BF16),
            jax.ShapeDtypeStruct((2 * tokens, slots), BF16),
            jax.ShapeDtypeStruct((2 * tokens, slots), BF16),
        ),
        compiler_params=params(),
    )(rf, gf, rb, gb, f, c)


def place_pieces(order, pieces, whole):
    quarter = pieces[0].shape[1]
    for n, piece in enumerate(pieces):
        whole[:, pl.ds(pl.multiple_of(order[n] * quarter, quarter), quarter)] = piece[...]


def dispatch_whole_kernel(order, table, p0, p1, p2, p3, send):
    quarter = p0.shape[1]
    for n, piece in enumerate((p0, p1, p2, p3)):
        rows = contract_first(table[...], piece[...]).astype(BF16)
        send[:, pl.ds(pl.multiple_of(order[n] * quarter, quarter), quarter)] = rows


def dispatch_whole(order, table, pieces):
    slots = table.shape[1]
    features = 4 * pieces[0].shape[1]
    vmem = pl.BlockSpec(memory_space=pltpu.VMEM)
    return pl.pallas_call(
        dispatch_whole_kernel,
        in_specs=[pl.BlockSpec(memory_space=pltpu.SMEM)] + [vmem] * 5,
        out_specs=vmem,
        out_shape=jax.ShapeDtypeStruct((slots, features), BF16),
        compiler_params=params(),
    )(order, table, *pieces)


def hidden_kernel(order, p0, p1, p2, p3, wg, wu, hidden, whole):
    @pl.when(pl.program_id(0) == 0)
    def _():
        place_pieces(order, (p0, p1, p2, p3), whole)

    rows = whole[...]
    a = contract_last(rows, wg[...])
    b = contract_last(rows, wu[...])
    hidden[0] = (a * jax.nn.sigmoid(a) * b).astype(BF16)


def hidden_forward(order, pieces, wg, wu, tile):
    rows, quarter = pieces[0].shape
    units, features = wg.shape
    weight = pl.BlockSpec((tile, features), lambda i: (i, 0))
    piece = pl.BlockSpec((rows, quarter), lambda i: (0, 0))
    return pl.pallas_call(
        hidden_kernel,
        grid=(units // tile,),
        in_specs=[pl.BlockSpec(memory_space=pltpu.SMEM)] + [piece] * 4 + [weight] * 2,
        out_specs=pl.BlockSpec((1, rows, tile), lambda i: (i, 0, 0)),
        out_shape=jax.ShapeDtypeStruct((units // tile, rows, tile), BF16),
        scratch_shapes=[pltpu.VMEM((rows, features), BF16)],
        compiler_params=params(),
        cost_estimate=pl.CostEstimate(
            flops=4 * rows * features * units, bytes_accessed=4 * units * features, transcendentals=rows * units
        ),
    )(order, *pieces, wg, wu)


def grads_kernel(order, x, p0, p1, p2, p3, wg, wu, wd, da, db, whole):
    @pl.when(pl.program_id(0) == 0)
    def _():
        place_pieces(order, (p0, p1, p2, p3), whole)

    rows = x[...]
    a = contract_last(rows, wg[...])
    b = contract_last(rows, wu[...])
    dh = contract_last(whole[...], wd[...])
    q = jax.nn.sigmoid(a)
    scaled = dh * q
    da[0] = (scaled * b * (1.0 + a * (1.0 - q))).astype(BF16)
    db[0] = (scaled * a).astype(BF16)


def hidden_grads(order, x, pieces, wg, wu, wd, tile):
    rows, quarter = pieces[0].shape
    units, features = wg.shape
    weight = pl.BlockSpec((tile, features), lambda i: (i, 0))
    piece = pl.BlockSpec((rows, quarter), lambda i: (0, 0))
    result = pl.BlockSpec((1, rows, tile), lambda i: (i, 0, 0))
    return pl.pallas_call(
        grads_kernel,
        grid=(units // tile,),
        in_specs=[pl.BlockSpec(memory_space=pltpu.SMEM), pl.BlockSpec((rows, features), lambda i: (0, 0))]
        + [piece] * 4
        + [weight] * 3,
        out_specs=[result, result],
        out_shape=[jax.ShapeDtypeStruct((units // tile, rows, tile), BF16)] * 2,
        scratch_shapes=[pltpu.VMEM((rows, features), BF16)],
        compiler_params=params(),
        cost_estimate=pl.CostEstimate(
            flops=6 * rows * features * units, bytes_accessed=6 * units * features, transcendentals=rows * units
        ),
    )(order, x, *pieces, wg, wu, wd)


def slices_kernel(pairs, order, *refs):
    acts, weights = refs[:pairs], refs[pairs : 2 * pairs]
    out, total = refs[2 * pairs], refs[2 * pairs + 1]
    step, last = pl.program_id(1), pl.num_programs(1) - 1
    part = functools.reduce(
        jnp.add, [jnp.dot(a[0], w[...], preferred_element_type=F32) for a, w in zip(acts, weights)]
    )

    @pl.when(step == 0)
    def _():
        total[...] = part

    @pl.when(step > 0)
    def _():
        total[...] += part

    @pl.when(step == last)
    def _():
        out[0] = total[...].astype(out.dtype)


def result_slices(order, acts, weights, quarter, dtype):
    tiles, rows, tile = acts[0].shape
    units = tiles * tile
    count = order.shape[0]
    act = pl.BlockSpec((1, rows, tile), lambda j, i, order: (i, 0, 0))
    weight = pl.BlockSpec((tile, quarter), lambda j, i, order: (i, order[j]))
    return pl.pallas_call(
        functools.partial(slices_kernel, len(acts)),
        grid_spec=pltpu.PrefetchScalarGridSpec(
            num_scalar_prefetch=1,
            grid=(count, tiles),
            in_specs=[act] * len(acts) + [weight] * len(acts),
            out_specs=pl.BlockSpec((1, rows, quarter), lambda j, i, order: (j, 0, 0)),
            scratch_shapes=[pltpu.VMEM((rows, quarter), F32)],
        ),
        out_shape=jax.ShapeDtypeStruct((count, rows, quarter), dtype),
        compiler_params=params(),
        cost_estimate=pl.CostEstimate(
            flops=2 * count * len(acts) * rows * quarter * units,
            bytes_accessed=2 * count * len(acts) * units * quarter,
            transcendentals=0,
        ),
    )(order, *acts, *weights)


def summed_over_tensor(place, acts, weights, quarter):
    order = (place + jnp.array([2, 1, 3, 0], jnp.int32)) % 4
    rows = acts[0].shape[1]
    half = rows // 2
    opposite = result_slices(order[:1], acts, weights, quarter, BF16)[0]
    up = shift(opposite[:half], "tensor", 1)
    down = shift(opposite[half:], "tensor", -1)
    sides = result_slices(order[1:3], acts, weights, quarter, BF16)
    own = result_slices(order[3:], acts, weights, quarter, F32)[0]
    to_next = jnp.concatenate([(sides[0, :half].astype(F32) + up.astype(F32)).astype(BF16), sides[0, half:]])
    to_last = jnp.concatenate([sides[1, :half], (sides[1, half:].astype(F32) + down.astype(F32)).astype(BF16)])
    from_last = shift(to_next, "tensor", 1)
    from_next = shift(to_last, "tensor", -1)
    return (own + from_last.astype(F32) + from_next.astype(F32)).astype(BF16)


def mix_kernel(mix, back, residual, out):
    tokens = residual.shape[0]
    both = jnp.dot(mix[...], back[...], preferred_element_type=F32)
    out[...] = (residual[...].astype(F32) + (both[:tokens] + both[tokens:])).astype(BF16)


def mixed(mix, back, residual):
    return pl.pallas_call(
        mix_kernel, out_shape=jax.ShapeDtypeStruct(residual.shape, BF16), compiler_params=params()
    )(mix, back, residual)


def exchange(rows):
    return lax.all_to_all(rows, "expert", split_axis=0, concat_axis=0, tiled=True)


def local(fwd_in, bwd_in, cotangent, route_fwd, gate_fwd, route_bwd, gate_bwd, w_gate, w_up, w_down):
    experts = lax.axis_size("expert")
    f, x, c = fwd_in[0], bwd_in[0], cotangent[0]
    tokens, quarter = f.shape
    fanout = route_fwd.shape[2]
    capacity = min(tokens, max(2, tokens * fanout * 3 // (2 * experts)))
    wg, wu, wd = w_gate[0, 0], w_up[0, 0], w_down[0, 0]
    tile = wg.shape[0] // 3
    place = lax.axis_index("tensor").astype(jnp.int32)
    order = (place + jnp.array([0, 3, 1, 2], jnp.int32)) % 4

    send_fc, table_b, mix_f, mix_b = dispatch(
        route_fwd[0], gate_fwd[0], route_bwd[0], gate_bwd[0], f, c, experts, capacity
    )
    x_pieces = (x, shift(x, "tensor", 1), shift(x, "tensor", -1), shift(x, "tensor", 2))
    got_fc = exchange(send_fc)
    send_x = dispatch_whole(order, table_b, x_pieces)
    rows_x = exchange(after(send_x, got_fc))

    f0, c0 = got_fc[:, :quarter], got_fc[:, quarter:]
    f_last, f_next = shift(f0, "tensor", 1), shift(f0, "tensor", -1)
    f_opposite = shift(f_last, "tensor", 1)
    c1 = after(c0, f_next)
    c_next = shift(c1, "tensor", -1)
    c_opposite = shift(c_next, "tensor", -1)
    c_last = shift(after(c0, f_opposite), "tensor", 1)

    hidden = hidden_forward(order, (f0, f_last, f_next, f_opposite), wg, wu, tile)
    share_f = summed_over_tensor(place, (hidden,), (wd,), quarter)
    da, db = hidden_grads(order, rows_x, (c0, c_last, c_next, c_opposite), wg, wu, wd, tile)
    share_b = summed_over_tensor(place, (da, db), (wg, wu), quarter)
    out_f = mixed(mix_f, exchange(share_f), f)
    out_b = mixed(mix_b, exchange(share_b), c)
    return shift(out_f[None], "pipe", 1), shift(out_b[None], "pipe", -1)


def solution(mesh):
    rows = P("pipe", "expert", "tensor")
    routes = P("pipe", "expert", None)
    weights = P("pipe", "expert", "tensor", None)
    return jax.shard_map(
        local,
        mesh=mesh,
        in_specs=(rows, rows, rows, routes, routes, routes, routes, weights, weights, weights),
        out_specs=(rows, rows),
        check_vma=False,
    )
```

time: 385 us -> 212 us (0.55); the launches traced: 379 us -> 211 us
  blocking collectives: 196 us -> 23.5 us
  Pallas kernels: 0 us -> 82.6 us
  matrix products: 74.2 us -> 0 us
  starting transfers between devices: 18.6 us -> 39.3 us
  between operations: 14.5 us -> 0.84 us
  waiting for transfers between devices: 53.8 us -> 40.9 us
    psum x1 -> x0, blocking collectives: 164 us -> none  [local(): total_fwd, total_bwd = lax.psum((partial_fwd, partial_bwd), 'tensor')]
    pallas_call x0 -> x12, Pallas kernels: none -> 82.6 us  [the longest x6 41.4 us: result_slices(): pl.pallas_call(functools.partial(slices_kernel, len(acts)), grid_spec=plt...]
    dot_general x6 -> x0, matrix products: 74.2 us -> none  [the longest x3 28 us: contract_model(): lax.dot_general(activations, weight, (((1,), (1,)), ((), ())), preferred_...]
    ppermute x2 -> x19, waiting for transfers between devices: 3.44 us -> 31.1 us  [shift(): lax.ppermute(shard, axis, [(i, (i + by) % length) for i in range(length)])]
    ppermute x2 -> x19, starting transfers between devices: 5.51 us -> 28.3 us  [shift(): lax.ppermute(shard, axis, [(i, (i + by) % length) for i in range(length)])]
    all_gather x3 -> x0, waiting for transfers between devices: 21.4 us -> none  [the longest x1 21.4 us: local(): lax.all_gather(recv_upstream.reshape(slot_total, quarter), 'tensor', axis...]
    all_to_all x3, waiting for transfers between devices: 28.9 us -> 9.86 us  [exchange(): lax.all_to_all(rows, 'expert', split_axis=0, concat_axis=0, tiled=True)]
    all_to_all x2 -> x1, blocking collectives: 31.9 us -> 23.5 us  [exchange(): lax.all_to_all(rows, 'expert', split_axis=0, concat_axis=0, tiled=True)]
  transfers between devices with their start and end apart: 8 -> 22, of which waited for: 5 -> 8; matrix products, arithmetic and copies ran while one was open for 15% -> 6% of each run, Pallas kernels for 0% -> 38%
where the time goes in v1:
time: 212 us; the launch traced here: 211 us
  Pallas kernels  82.6 us (39%)
  waiting for transfers between devices  40.9 us (19%)
  starting transfers between devices  39.3 us (19%)
  blocking collectives  23.5 us (11%)
  local copies, waits for them, and re-layouts  17.3 us (8%)
  other arithmetic  6.11 us (3%)
    pallas_call x6, Pallas kernels, result_slices(): pl.pallas_call(functools.partial(slices_kernel, len(acts)), grid_spec=plt...  41.4 us
    ppermute x19, waiting for transfers between devices, shift(): lax.ppermute(shard, axis, [(i, (i + by) % length) for i in range(length)])  31.1 us
    ppermute x19, starting transfers between devices, shift(): lax.ppermute(shard, axis, [(i, (i + by) % length) for i in range(length)])  28.3 us
    all_to_all x1, blocking collectives, exchange(): lax.all_to_all(rows, 'expert', split_axis=0, concat_axis=0, tiled=True)  23.5 us
    pallas_call x1, Pallas kernels, hidden_grads(): pl.pallas_call(grads_kernel, grid=(units // tile,), in_specs=[pl.BlockSpe...  18.4 us
    pallas_call x1, Pallas kernels, hidden_forward(): pl.pallas_call(hidden_kernel, grid=(units // tile,), in_specs=[pl.BlockSp...  12.1 us
    all_to_all x3, starting transfers between devices, exchange(): lax.all_to_all(rows, 'expert', split_axis=0, concat_axis=0, tiled=True)  11 us
    unnamed x36, local copies, waits for them, and re-layouts  10.7 us
  transfers between devices with their start and end apart: 22, of which 8 were waited for; matrix products, arithmetic and copies ran while one was open for 6% of the time, Pallas kernels for 38%

profile of v1, /device:TPU:0, one launch (start us, length us, event | category | flops | bytes accessed | tf_op | source)
XLA Modules:
  0.0 210.6 jit_solution(8266273203312852541)
XLA Ops:
  6.1 3.3 %shard_map.140 = (bf16[384,1536]{1,0:T(8,128)(2,1)}, bf16[64,384]{1,0:T(8,128)(2,1)}, bf16[128,384]{1,0:T(8,128)(2,1)}, bf16[128,384]{1,0:T(8,128)(2,1)}) custom-call(s32[64,4]{1,0:T(8,128)} %bitcast.92, s32[64,4]{1,0:T(8,128)} %bitcast.93, s32[64,4]{1,0:T(8,128)} %bitcast.94, s32[64,4]{1,0:T(8,128)} %bitcast.95, bf16[64,768]{1,0:T(8,128)(2,1)} %bitcast.88, ...), custom_call_target="tpu_custom_call" | custom-call | tf_op jit(solution)/shard_map/pallas_call | solution.py:75
  9.4 23.5 %all_to_all.45 = bf16[16,24,1536]{2,1,0:T(8,128)(2,1)S(1)} all-to-all(bf16[16,24,1536]{2,1,0:T(8,128)(2,1)} %bitcast.87), channel_id=1, replica_groups=mesh['pipe'=2,'expert'=16,'tensor'=4] {'expert'}, dimensions={0} | all-to-all | bytes 2359296 | tf_op jit(solution)/shard_map/all_to_all | solution.py:255
  39.0 2.4 %collective-permute-start.10 = (bf16[64,768]{1,0:T(8,128)(2,1)S(1)}, bf16[64,768]{1,0:T(8,128)(2,1)S(1)}, u32[]{:S(2)}, u32[]{:S(2)}) collective-permute-start(bf16[64,768]{1,0:T(8,128)(2,1)S(1)} %bitcast.99), channel_id=1, source_target_pairs={{0,2},{1,3},{2,0},{3,1},{4,6},{5,7},{6,4},{7,5},{8,10},{9,11},{10,... | collective-permute-start | bytes 294920 | tf_op jit(solution)/shard_map/ppermute | solution.py:29
  42.4 9.7 %collective-permute-done.p1 = bf16[384,768]{1,0:T(8,128)(2,1)S(1)} collective-permute-done((bf16[384,768]{1,0:T(8,128)(2,1)S(1)}, bf16[384,768]{1,0:T(8,128)(2,1)S(1)}, u32[]{:S(2)}, u32[]{:S(2)}) %collective-permute-start) | collective-permute-done | bytes 589856 | tf_op jit(solution)/shard_map/ppermute | solution.py:29
  53.3 4.4 %collective-permute-done.10.p3 = bf16[64,768]{1,0:T(8,128)(2,1)S(1)} collective-permute-done((bf16[64,768]{1,0:T(8,128)(2,1)S(1)}, bf16[64,768]{1,0:T(8,128)(2,1)S(1)}, u32[]{:S(2)}, u32[]{:S(2)}) %collective-permute-start.10) | collective-permute-done | bytes 98336 | tf_op jit(solution)/shard_map/ppermute | solution.py:29
  58.4 3.3 %shard_map.146 = bf16[384,3072]{1,0:T(8,128)(2,1)} custom-call(s32[4]{0:T(128)} %and_select_fusion.order, bf16[64,384]{1,0:T(8,128)(2,1)} %get-tuple-element.14.table, bf16[64,768]{1,0:T(8,128)(2,1)} %bitcast.96, bf16[64,768]{1,0:T(8,128)(2,1)} %copy-done.7, bf16[64,768]{1,0:T(8,128)(2,1)} %copy-done.8, bf16[64,768]{1,0:T(8,128)(2,1)} %copy-done.9), custom_call_target="tpu_custom_call" | custom-call | tf_op jit(solution)/shard_map/pallas_call | solution.py:104
  61.7 3.7 %all-to-all-start.2 = ((bf16[16,24,3072]{2,1,0:T(8,128)(2,1)}), bf16[16,24,3072]{2,1,0:T(8,128)(2,1)S(1)}, u32[]{:S(2)}, u32[]{:S(2)}) async-start(bf16[16,24,3072]{2,1,0:T(8,128)(2,1)} %bitcast.82), calls=%async_computation.2 | async-start | bytes 4718592 | tf_op jit(solution)/shard_map/all_to_all | solution.py:255
  66.7 2.0 collective-permute-done.2.p3
  68.7 12.1 %shard_map.141.refs_0_ = bf16[3,384,448]{2,1,0:T(8,128)(2,1)} custom-call(s32[4]{0:T(128)} %and_select_fusion.order, bf16[384,768]{1,0:T(8,128)(2,1)} %copy-done.5, bf16[384,768]{1,0:T(8,128)(2,1)} %copy-done.11, bf16[384,768]{1,0:T(8,128)(2,1)} %collective-permute-done.1.p2, bf16[384,768]{1,0:T(8,128)(2,1)} %collective-permute-done.2.p3, ...), custom_call_target="tpu_custom_call" | custom-call | flops 6341787648 | bytes 16515072 | tf_op jit(solution)/shard_map/pallas_call | solution.py:129
  80.8 5.1 %shard_map.144 = bf16[1,384,768]{2,1,0:T(8,128)(2,1)} custom-call(s32[1]{0:T(128)} %get-tuple-element.34.order, bf16[3,384,448]{2,1,0:T(8,128)(2,1)} %shard_map.141.refs_0_, bf16[1344,3072]{1,0:T(8,128)(2,1)} %bitcast.68), custom_call_target="tpu_custom_call" | custom-call | flops 792723456 | bytes 2064384 | tf_op jit(solution)/shard_map/pallas_call | solution.py:207
  87.1 3.2 %collective-permute-start.5 = (bf16[192,768]{1,0:T(8,128)(2,1)S(1)}, bf16[192,768]{1,0:T(8,128)(2,1)S(1)}, u32[]{:S(2)}, u32[]{:S(2)}) collective-permute-start(bf16[192,768]{1,0:T(8,128)(2,1)S(1)} %get-tuple-element.33), channel_id=1, source_target_pairs={{0,3},{1,0},{2,1},{3,2},{4,7},{5,4},{6,5},{7,6},{8,11},{9,8},{10,9... | collective-permute-start | bytes 884744 | tf_op jit(solution)/shard_map/ppermute | solution.py:29
  90.3 7.9 %shard_map.143 = bf16[2,384,768]{2,1,0:T(8,128)(2,1)} custom-call(s32[2]{0:T(128)} %slice.74.order, bf16[3,384,448]{2,1,0:T(8,128)(2,1)} %shard_map.141.refs_0_, bf16[1344,3072]{1,0:T(8,128)(2,1)} %bitcast.69), custom_call_target="tpu_custom_call" | custom-call | flops 1585446912 | bytes 4128768 | tf_op jit(solution)/shard_map/pallas_call | solution.py:207
  98.2 3.2 %collective-permute-start.13 = (bf16[384,768]{1,0:T(8,128)(2,1)S(1)}, bf16[384,768]{1,0:T(8,128)(2,1)}, u32[]{:S(2)}, u32[]{:S(2)}) collective-permute-start(bf16[384,768]{1,0:T(8,128)(2,1)S(1)} %collective-permute-done.12.p2), channel_id=1, source_target_pairs={{0,3},{1,0},{2,1},{3,2},{4,7},{5,4},{6,5},{7,6},{8,11},{9,8},{10,9... | collective-permute-start | bytes 1769480 | tf_op jit(solution)/shard_map/ppermute | solution.py:29
  103.1 2.1 collective-permute-start.4
  105.1 10.7 %collective-permute-done.11.p1 = bf16[384,768]{1,0:T(8,128)(2,1)S(1)} collective-permute-done((bf16[384,768]{1,0:T(8,128)(2,1)}, bf16[384,768]{1,0:T(8,128)(2,1)S(1)}, u32[]{:S(2)}, u32[]{:S(2)}) %collective-permute-start.11) | collective-permute-done | bytes 589856 | tf_op jit(solution)/shard_map/ppermute | solution.py:29
  118.1 18.4 %shard_map.147 = (bf16[3,384,448]{2,1,0:T(8,128)(2,1)}, bf16[3,384,448]{2,1,0:T(8,128)(2,1)}) custom-call(s32[4]{0:T(128)} %and_select_fusion.order, bf16[384,3072]{1,0:T(8,128)(2,1)} %bitcast.84, bf16[384,768]{1,0:T(8,128)(2,1)} %get-tuple-element.17.p0, bf16[384,768]{1,0:T(8,128)(2,1)} %copy-done.12, bf16[384,768]{1,0:T(8,128)(2,1)} %copy-done.10, ...), custom_call_target="tpu_custom_call" | custom-call | flops 9512681472 | bytes 24772608 | tf_op jit(solution)/shard_map/pallas_call | solution.py:164
  136.6 6.4 %shard_map.150 = bf16[1,384,768]{2,1,0:T(8,128)(2,1)} custom-call(s32[1]{0:T(128)} %get-tuple-element.34.order, bf16[3,384,448]{2,1,0:T(8,128)(2,1)} %get-tuple-element.18.refs_0_, bf16[3,384,448]{2,1,0:T(8,128)(2,1)} %get-tuple-element.19.refs_1_, bf16[1344,3072]{1,0:T(8,128)(2,1)} %bitcast.74, bf16[1344,3072]{1,0:T(8,128)(2,1)} %bitcast.79), custom_call_target="tpu_custom_call" | custom-call | flops 1585446912 | bytes 4128768 | tf_op jit(solution)/shard_map/pallas_call | solution.py:207
  144.1 3.2 %collective-permute-start.16 = (bf16[192,768]{1,0:T(8,128)(2,1)S(1)}, bf16[192,768]{1,0:T(8,128)(2,1)S(1)}, u32[]{:S(2)}, u32[]{:S(2)}) collective-permute-start(bf16[192,768]{1,0:T(8,128)(2,1)S(1)} %get-tuple-element.31), channel_id=1, source_target_pairs={{0,3},{1,0},{2,1},{3,2},{4,7},{5,4},{6,5},{7,6},{8,11},{9,8},{10,9... | collective-permute-start | bytes 884744 | tf_op jit(solution)/shard_map/ppermute | solution.py:29
  147.3 10.2 %shard_map.149 = bf16[2,384,768]{2,1,0:T(8,128)(2,1)} custom-call(s32[2]{0:T(128)} %slice.74.order, bf16[3,384,448]{2,1,0:T(8,128)(2,1)} %get-tuple-element.18.refs_0_, bf16[3,384,448]{2,1,0:T(8,128)(2,1)} %get-tuple-element.19.refs_1_, bf16[1344,3072]{1,0:T(8,128)(2,1)} %bitcast.75, bf16[1344,3072]{1,0:T(8,128)(2,1)} %bitcast.80), custom_call_target="tpu_custom_call" | custom-call | flops 3170893824 | bytes 8257536 | tf_op jit(solution)/shard_map/pallas_call | solution.py:207
  161.4 5.3 %shard_map.142 = f32[1,384,768]{2,1,0:T(8,128)} custom-call(s32[1]{0:T(128)} %get-tuple-element.35.order, bf16[3,384,448]{2,1,0:T(8,128)(2,1)} %shard_map.141.refs_0_, bf16[1344,3072]{1,0:T(8,128)(2,1)} %bitcast.71), custom_call_target="tpu_custom_call" | custom-call | flops 792723456 | bytes 2064384 | tf_op jit(solution)/shard_map/pallas_call | solution.py:207
  166.7 2.6 %fusion.3 = bf16[384,768]{1,0:T(8,128)(2,1)} fusion(f32[1,384,768]{2,1,0:T(8,128)} %shard_map.142, bf16[384,768]{1,0:T(8,128)(2,1)} %collective-permute-done.6, bf16[384,768]{1,0:T(8,128)(2,1)} %collective-permute-done.4), kind=kLoop, calls=%fused_computation.5 | loop fusion | flops 1474560 | bytes 2949120 | tf_op jit(solution)/shard_map/convert_element_type | solution.py:239
  169.3 3.7 %all-to-all-start.1 = ((bf16[16,24,768]{2,1,0:T(8,128)(2,1)}), bf16[16,24,768]{2,1,0:T(8,128)(2,1)S(1)}, u32[]{:S(2)}, u32[]{:S(2)}) async-start(bf16[16,24,768]{2,1,0:T(8,128)(2,1)} %bitcast.18), calls=%async_computation.1 | async-start | bytes 1179648 | tf_op jit(solution)/shard_map/all_to_all | solution.py:255
  172.9 6.6 %shard_map.148 = f32[1,384,768]{2,1,0:T(8,128)} custom-call(s32[1]{0:T(128)} %get-tuple-element.35.order, bf16[3,384,448]{2,1,0:T(8,128)(2,1)} %get-tuple-element.18.refs_0_, bf16[3,384,448]{2,1,0:T(8,128)(2,1)} %get-tuple-element.19.refs_1_, bf16[1344,3072]{1,0:T(8,128)(2,1)} %bitcast.76, bf16[1344,3072]{1,0:T(8,128)(2,1)} %bitcast.81), custom_call_target="tpu_custom_call" | custom-call | flops 1585446912 | bytes 4128768 | tf_op jit(solution)/shard_map/pallas_call | solution.py:207
  179.6 2.4 %fusion.1 = bf16[384,768]{1,0:T(8,128)(2,1)} fusion(f32[1,384,768]{2,1,0:T(8,128)} %shard_map.148, bf16[384,768]{1,0:T(8,128)(2,1)S(1)} %collective-permute-done.17, bf16[384,768]{1,0:T(8,128)(2,1)} %collective-permute-done.15), kind=kLoop, calls=%fused_computation.2 | loop fusion | flops 1474560 | bytes 2949120 | tf_op jit(solution)/shard_map/convert_element_type | solution.py:239
  182.0 2.5 %all-to-all-done.1 = bf16[16,24,768]{2,1,0:T(8,128)(2,1)S(1)} async-done(((bf16[16,24,768]{2,1,0:T(8,128)(2,1)}), bf16[16,24,768]{2,1,0:T(8,128)(2,1)S(1)}, u32[]{:S(2)}, u32[]{:S(2)}) %all-to-all-start.1) | async-done | bytes 589856 | tf_op jit(solution)/shard_map/all_to_all | solution.py:255
  184.6 3.6 %all-to-all-start.3 = ((bf16[16,24,768]{2,1,0:T(8,128)(2,1)}), bf16[16,24,768]{2,1,0:T(8,128)(2,1)S(1)}, u32[]{:S(2)}, u32[]{:S(2)}) async-start(bf16[16,24,768]{2,1,0:T(8,128)(2,1)} %bitcast.31), calls=%async_computation.3 | async-start | bytes 1179648 | tf_op jit(solution)/shard_map/all_to_all | solution.py:255
  188.2 2.0 shard_map.145
  190.2 2.7 %collective-permute-start.7 = (bf16[1,64,768]{2,1,0:T(8,128)(2,1)}, bf16[1,64,768]{2,1,0:T(8,128)(2,1)S(1)}, u32[]{:S(2)}, u32[]{:S(2)}) collective-permute-start(bf16[1,64,768]{2,1,0:T(8,128)(2,1)} %bitcast.100), channel_id=1, source_target_pairs={{0,64},{64,0},{1,65},{65,1},{2,66},{66,2},{3,67},{67,3},{4,68},{68... | collective-permute-start | bytes 294920 | tf_op jit(solution)/shard_map/ppermute | solution.py:29
  192.9 7.3 %all-to-all-done.3 = bf16[16,24,768]{2,1,0:T(8,128)(2,1)S(1)} async-done(((bf16[16,24,768]{2,1,0:T(8,128)(2,1)}), bf16[16,24,768]{2,1,0:T(8,128)(2,1)S(1)}, u32[]{:S(2)}, u32[]{:S(2)}) %all-to-all-start.3) | async-done | bytes 589856 | tf_op jit(solution)/shard_map/all_to_all | solution.py:255
  201.0 2.0 shard_map.151
  203.0 2.7 %collective-permute-start.18 = (bf16[1,64,768]{2,1,0:T(8,128)(2,1)}, bf16[1,64,768]{2,1,0:T(8,128)(2,1)S(1)}, u32[]{:S(2)}, u32[]{:S(2)}) collective-permute-start(bf16[1,64,768]{2,1,0:T(8,128)(2,1)} %bitcast.101), channel_id=1, source_target_pairs={{0,64},{64,0},{1,65},{65,1},{2,66},{66,2},{3,67},{67,3},{4,68},{68... | collective-permute-start | bytes 294920 | tf_op jit(solution)/shard_map/ppermute | solution.py:29
  205.7 3.6 %collective-permute-done.18 = bf16[1,64,768]{2,1,0:T(8,128)(2,1)S(1)} collective-permute-done((bf16[1,64,768]{2,1,0:T(8,128)(2,1)}, bf16[1,64,768]{2,1,0:T(8,128)(2,1)S(1)}, u32[]{:S(2)}, u32[]{:S(2)}) %collective-permute-start.18) | collective-permute-done | bytes 98336 | tf_op jit(solution)/shard_map/ppermute | solution.py:29
  (78 shorter events, 27.8 us)
Async XLA Ops:
  32.9 2.8 %copy-start.6 = (bf16[1,64,768]{2,1,0:T(8,128)(2,1)S(1)}, bf16[1,64,768]{2,1,0:T(8,128)(2,1)}, u32[]{:S(2)}) copy-start(bf16[1,64,768]{2,1,0:T(8,128)(2,1)} %param.14) | copy-start | bytes 294916
  32.9 19.1 %copy-start.14 = (s32[4]{0:T(128)S(1)}, s32[4]{0:T(128)}, u32[]{:S(2)}) copy-start(s32[4]{0:T(128)} %constant.33.clone) | copy-start | bytes 52
  33.9 27.9 %copy-start.5 = (bf16[384,768]{1,0:T(8,128)(2,1)}, bf16[384,768]{1,0:T(8,128)(2,1)S(1)}, u32[]{:S(2)}) copy-start(bf16[384,768]{1,0:T(8,128)(2,1)S(1)} %get-tuple-element.25.p0) | copy-start | bytes 1769476
  33.9 18.2 %collective-permute-start = (bf16[384,768]{1,0:T(8,128)(2,1)S(1)}, bf16[384,768]{1,0:T(8,128)(2,1)S(1)}, u32[]{:S(2)}, u32[]{:S(2)}) collective-permute-start(bf16[384,768]{1,0:T(8,128)(2,1)S(1)} %get-tuple-element.25.p0), channel_id=1, source_target_pairs={{0,1},{1,2},{2,3},{3,0},{4,5},{5,6},{6,7},{7,4},{8,9},{9,10},{10,1... | collective-permute-start | bytes 1769480 | tf_op jit(solution)/shard_map/ppermute | solution.py:29
  35.8 17.6 %collective-permute-start.8 = (bf16[64,768]{1,0:T(8,128)(2,1)S(1)}, bf16[64,768]{1,0:T(8,128)(2,1)S(1)}, u32[]{:S(2)}, u32[]{:S(2)}) collective-permute-start(bf16[64,768]{1,0:T(8,128)(2,1)S(1)} %bitcast.97), channel_id=1, source_target_pairs={{0,1},{1,2},{2,3},{3,0},{4,5},{5,6},{6,7},{7,4},{8,9},{9,10},{10,1... | collective-permute-start | bytes 294920 | tf_op jit(solution)/shard_map/ppermute | solution.py:29
  37.7 15.6 %collective-permute-start.9 = (bf16[64,768]{1,0:T(8,128)(2,1)S(1)}, bf16[64,768]{1,0:T(8,128)(2,1)S(1)}, u32[]{:S(2)}, u32[]{:S(2)}) collective-permute-start(bf16[64,768]{1,0:T(8,128)(2,1)S(1)} %bitcast.98), channel_id=1, source_target_pairs={{0,3},{1,0},{2,1},{3,2},{4,7},{5,4},{6,5},{7,6},{8,11},{9,8},{10,9... | collective-permute-start | bytes 294920 | tf_op jit(solution)/shard_map/ppermute | solution.py:29
  39.0 18.7 %collective-permute-start.10 = (bf16[64,768]{1,0:T(8,128)(2,1)S(1)}, bf16[64,768]{1,0:T(8,128)(2,1)S(1)}, u32[]{:S(2)}, u32[]{:S(2)}) collective-permute-start(bf16[64,768]{1,0:T(8,128)(2,1)S(1)} %bitcast.99), channel_id=1, source_target_pairs={{0,2},{1,3},{2,0},{3,1},{4,6},{5,7},{6,4},{7,5},{8,10},{9,11},{10,... | collective-permute-start | bytes 294920 | tf_op jit(solution)/shard_map/ppermute | solution.py:29
  41.4 25.3 %collective-permute-start.1 = (bf16[384,768]{1,0:T(8,128)(2,1)S(1)}, bf16[384,768]{1,0:T(8,128)(2,1)}, u32[]{:S(2)}, u32[]{:S(2)}) collective-permute-start(bf16[384,768]{1,0:T(8,128)(2,1)S(1)} %get-tuple-element.25.p0), channel_id=1, source_target_pairs={{0,3},{1,0},{2,1},{3,2},{4,7},{5,4},{6,5},{7,6},{8,11},{9,8},{10,9... | collective-permute-start | bytes 1769480 | tf_op jit(solution)/shard_map/ppermute | solution.py:29
  52.0 9.7 %copy-start.11 = (bf16[384,768]{1,0:T(8,128)(2,1)}, bf16[384,768]{1,0:T(8,128)(2,1)S(1)}, u32[]{:S(2)}) copy-start(bf16[384,768]{1,0:T(8,128)(2,1)S(1)} %collective-permute-done.p1) | copy-start | bytes 1769476
  52.1 16.6 %collective-permute-start.2 = (bf16[384,768]{1,0:T(8,128)(2,1)S(1)}, bf16[384,768]{1,0:T(8,128)(2,1)}, u32[]{:S(2)}, u32[]{:S(2)}) collective-permute-start(bf16[384,768]{1,0:T(8,128)(2,1)S(1)} %collective-permute-done.p1), channel_id=1, source_target_pairs={{0,1},{1,2},{2,3},{3,0},{4,5},{5,6},{6,7},{7,4},{8,9},{9,10},{10,1... | collective-permute-start | bytes 1769480 | tf_op jit(solution)/shard_map/ppermute | solution.py:29
  53.3 4.4 %copy-start.7 = (bf16[64,768]{1,0:T(8,128)(2,1)}, bf16[64,768]{1,0:T(8,128)(2,1)S(1)}, u32[]{:S(2)}) copy-start(bf16[64,768]{1,0:T(8,128)(2,1)S(1)} %collective-permute-done.8.p1) | copy-start | bytes 294916
  53.3 4.4 %copy-start.8 = (bf16[64,768]{1,0:T(8,128)(2,1)}, bf16[64,768]{1,0:T(8,128)(2,1)S(1)}, u32[]{:S(2)}) copy-start(bf16[64,768]{1,0:T(8,128)(2,1)S(1)} %collective-permute-done.9.p2) | copy-start | bytes 294916
  61.7 3.8 %copy-start.13 = (s32[4]{0:T(128)S(1)}, s32[4]{0:T(128)}, u32[]{:S(2)}) copy-start(s32[4]{0:T(128)} %constant.34.clone) | copy-start | bytes 52
  61.7 55.0 %all-to-all-start.2 = ((bf16[16,24,3072]{2,1,0:T(8,128)(2,1)}), bf16[16,24,3072]{2,1,0:T(8,128)(2,1)S(1)}, u32[]{:S(2)}, u32[]{:S(2)}) async-start(bf16[16,24,3072]{2,1,0:T(8,128)(2,1)} %bitcast.82), calls=%async_computation.2 | async-start | bytes 4718592 | tf_op jit(solution)/shard_map/all_to_all | solution.py:255
  66.7 31.5 %collective-permute-start.12 = (bf16[384,768]{1,0:T(8,128)(2,1)}, bf16[384,768]{1,0:T(8,128)(2,1)S(1)}, u32[]{:S(2)}, u32[]{:S(2)}) collective-permute-start(bf16[384,768]{1,0:T(8,128)(2,1)} %get-tuple-element.17.p0), channel_id=1, source_target_pairs={{0,3},{1,0},{2,1},{3,2},{4,7},{5,4},{6,5},{7,6},{8,11},{9,8},{10,9... | collective-permute-start | bytes 1769480 | tf_op jit(solution)/shard_map/ppermute | solution.py:29
  87.0 15.5 %collective-permute-start.3 = (bf16[192,768]{1,0:T(8,128)(2,1)S(1)}, bf16[192,768]{1,0:T(8,128)(2,1)S(1)}, u32[]{:S(2)}, u32[]{:S(2)}) collective-permute-start(bf16[192,768]{1,0:T(8,128)(2,1)S(1)} %get-tuple-element.32), channel_id=1, source_target_pairs={{0,1},{1,2},{2,3},{3,0},{4,5},{5,6},{6,7},{7,4},{8,9},{9,10},{10,1... | collective-permute-start | bytes 884744 | tf_op jit(solution)/shard_map/ppermute | solution.py:29
  87.1 15.5 %collective-permute-start.5 = (bf16[192,768]{1,0:T(8,128)(2,1)S(1)}, bf16[192,768]{1,0:T(8,128)(2,1)S(1)}, u32[]{:S(2)}, u32[]{:S(2)}) collective-permute-start(bf16[192,768]{1,0:T(8,128)(2,1)S(1)} %get-tuple-element.33), channel_id=1, source_target_pairs={{0,3},{1,0},{2,1},{3,2},{4,7},{5,4},{6,5},{7,6},{8,11},{9,8},{10,9... | collective-permute-start | bytes 884744 | tf_op jit(solution)/shard_map/ppermute | solution.py:29
  98.2 4.4 %copy-start.1 = (bf16[2,384,768]{2,1,0:T(8,128)(2,1)S(1)}, bf16[2,384,768]{2,1,0:T(8,128)(2,1)}, u32[]{:S(2)}) copy-start(bf16[2,384,768]{2,1,0:T(8,128)(2,1)} %shard_map.143) | copy-start | bytes 3538948
  98.2 17.7 %collective-permute-start.11 = (bf16[384,768]{1,0:T(8,128)(2,1)}, bf16[384,768]{1,0:T(8,128)(2,1)S(1)}, u32[]{:S(2)}, u32[]{:S(2)}) collective-permute-start(bf16[384,768]{1,0:T(8,128)(2,1)} %get-tuple-element.17.p0), channel_id=1, source_target_pairs={{0,1},{1,2},{2,3},{3,0},{4,5},{5,6},{6,7},{7,4},{8,9},{9,10},{10,1... | collective-permute-start | bytes 1769480 | tf_op jit(solution)/shard_map/ppermute | solution.py:29
  98.2 4.5 %copy-start.10 = (bf16[384,768]{1,0:T(8,128)(2,1)}, bf16[384,768]{1,0:T(8,128)(2,1)S(1)}, u32[]{:S(2)}) copy-start(bf16[384,768]{1,0:T(8,128)(2,1)S(1)} %collective-permute-done.12.p2) | copy-start | bytes 1769476
  98.2 18.5 %collective-permute-start.13 = (bf16[384,768]{1,0:T(8,128)(2,1)S(1)}, bf16[384,768]{1,0:T(8,128)(2,1)}, u32[]{:S(2)}, u32[]{:S(2)}) collective-permute-start(bf16[384,768]{1,0:T(8,128)(2,1)S(1)} %collective-permute-done.12.p2), channel_id=1, source_target_pairs={{0,3},{1,0},{2,1},{3,2},{4,7},{5,4},{6,5},{7,6},{8,11},{9,8},{10,9... | collective-permute-start | bytes 1769480 | tf_op jit(solution)/shard_map/ppermute | solution.py:29
  102.8 63.9 %collective-permute-start.6 = (bf16[384,768]{1,0:T(8,128)(2,1)S(1)}, bf16[384,768]{1,0:T(8,128)(2,1)}, u32[]{:S(2)}, u32[]{:S(2)}) collective-permute-start(bf16[384,768]{1,0:T(8,128)(2,1)S(1)} %pad_maximum_fusion.1), channel_id=1, source_target_pairs={{0,3},{1,0},{2,1},{3,2},{4,7},{5,4},{6,5},{7,6},{8,11},{9,8},{10,9... | collective-permute-start | bytes 1769480 | tf_op jit(solution)/shard_map/ppermute | solution.py:29
  103.1 63.6 %collective-permute-start.4 = (bf16[384,768]{1,0:T(8,128)(2,1)S(1)}, bf16[384,768]{1,0:T(8,128)(2,1)}, u32[]{:S(2)}, u32[]{:S(2)}) collective-permute-start(bf16[384,768]{1,0:T(8,128)(2,1)S(1)} %pad_maximum_fusion), channel_id=1, source_target_pairs={{0,1},{1,2},{2,3},{3,0},{4,5},{5,6},{6,7},{7,4},{8,9},{9,10},{10,1... | collective-permute-start | bytes 1769480 | tf_op jit(solution)/shard_map/ppermute | solution.py:29
  144.0 14.7 %collective-permute-start.14 = (bf16[192,768]{1,0:T(8,128)(2,1)S(1)}, bf16[192,768]{1,0:T(8,128)(2,1)S(1)}, u32[]{:S(2)}, u32[]{:S(2)}) collective-permute-start(bf16[192,768]{1,0:T(8,128)(2,1)S(1)} %get-tuple-element.30), channel_id=1, source_target_pairs={{0,1},{1,2},{2,3},{3,0},{4,5},{5,6},{6,7},{7,4},{8,9},{9,10},{10,1... | collective-permute-start | bytes 884744 | tf_op jit(solution)/shard_map/ppermute | solution.py:29
  144.1 14.6 %collective-permute-start.16 = (bf16[192,768]{1,0:T(8,128)(2,1)S(1)}, bf16[192,768]{1,0:T(8,128)(2,1)S(1)}, u32[]{:S(2)}, u32[]{:S(2)}) collective-permute-start(bf16[192,768]{1,0:T(8,128)(2,1)S(1)} %get-tuple-element.31), channel_id=1, source_target_pairs={{0,3},{1,0},{2,1},{3,2},{4,7},{5,4},{6,5},{7,6},{8,11},{9,8},{10,9... | collective-permute-start | bytes 884744 | tf_op jit(solution)/shard_map/ppermute | solution.py:29
  159.2 20.4 %collective-permute-start.17 = (bf16[384,768]{1,0:T(8,128)(2,1)S(1)}, bf16[384,768]{1,0:T(8,128)(2,1)S(1)}, u32[]{:S(2)}, u32[]{:S(2)}) collective-permute-start(bf16[384,768]{1,0:T(8,128)(2,1)S(1)} %pad_maximum_fusion.3), channel_id=1, source_target_pairs={{0,3},{1,0},{2,1},{3,2},{4,7},{5,4},{6,5},{7,6},{8,11},{9,8},{10,9... | collective-permute-start | bytes 1769480 | tf_op jit(solution)/shard_map/ppermute | solution.py:29
  160.4 19.2 %collective-permute-start.15 = (bf16[384,768]{1,0:T(8,128)(2,1)S(1)}, bf16[384,768]{1,0:T(8,128)(2,1)}, u32[]{:S(2)}, u32[]{:S(2)}) collective-permute-start(bf16[384,768]{1,0:T(8,128)(2,1)S(1)} %pad_maximum_fusion.2), channel_id=1, source_target_pairs={{0,1},{1,2},{2,3},{3,0},{4,5},{5,6},{6,7},{7,4},{8,9},{9,10},{10,1... | collective-permute-start | bytes 1769480 | tf_op jit(solution)/shard_map/ppermute | solution.py:29
  169.3 15.3 %all-to-all-start.1 = ((bf16[16,24,768]{2,1,0:T(8,128)(2,1)}), bf16[16,24,768]{2,1,0:T(8,128)(2,1)S(1)}, u32[]{:S(2)}, u32[]{:S(2)}) async-start(bf16[16,24,768]{2,1,0:T(8,128)(2,1)} %bitcast.18), calls=%async_computation.1 | async-start | bytes 1179648 | tf_op jit(solution)/shard_map/all_to_all | solution.py:255
  184.6 3.6 %copy-start.3 = (bf16[16,24,768]{2,1,0:T(8,128)(2,1)}, bf16[16,24,768]{2,1,0:T(8,128)(2,1)S(1)}, u32[]{:S(2)}) copy-start(bf16[16,24,768]{2,1,0:T(8,128)(2,1)S(1)} %all-to-all-done.1) | copy-start | bytes 1769476
  184.6 15.6 %all-to-all-start.3 = ((bf16[16,24,768]{2,1,0:T(8,128)(2,1)}), bf16[16,24,768]{2,1,0:T(8,128)(2,1)S(1)}, u32[]{:S(2)}, u32[]{:S(2)}) async-start(bf16[16,24,768]{2,1,0:T(8,128)(2,1)} %bitcast.31), calls=%async_computation.3 | async-start | bytes 1179648 | tf_op jit(solution)/shard_map/all_to_all | solution.py:255
  190.2 15.6 %collective-permute-start.7 = (bf16[1,64,768]{2,1,0:T(8,128)(2,1)}, bf16[1,64,768]{2,1,0:T(8,128)(2,1)S(1)}, u32[]{:S(2)}, u32[]{:S(2)}) collective-permute-start(bf16[1,64,768]{2,1,0:T(8,128)(2,1)} %bitcast.100), channel_id=1, source_target_pairs={{0,64},{64,0},{1,65},{65,1},{2,66},{66,2},{3,67},{67,3},{4,68},{68... | collective-permute-start | bytes 294920 | tf_op jit(solution)/shard_map/ppermute | solution.py:29
  203.0 6.3 %collective-permute-start.18 = (bf16[1,64,768]{2,1,0:T(8,128)(2,1)}, bf16[1,64,768]{2,1,0:T(8,128)(2,1)S(1)}, u32[]{:S(2)}, u32[]{:S(2)}) collective-permute-start(bf16[1,64,768]{2,1,0:T(8,128)(2,1)} %bitcast.101), channel_id=1, source_target_pairs={{0,64},{64,0},{1,65},{65,1},{2,66},{66,2},{3,67},{67,3},{4,68},{68... | collective-permute-start | bytes 294920 | tf_op jit(solution)/shard_map/ppermute | solution.py:29
  (5 other events, 5.1 us)

commit v2 on v1

v2 whole, which is shorter than its diff:
```python
import functools

import jax
import jax.numpy as jnp
from jax import lax
from jax.experimental import pallas as pl
from jax.experimental.pallas import tpu as pltpu
from jax.sharding import PartitionSpec as P

F32 = jnp.float32
BF16 = jnp.bfloat16
VMEM = pl.BlockSpec(memory_space=pltpu.VMEM)
SMEM = pl.BlockSpec(memory_space=pltpu.SMEM)
ANY = pl.BlockSpec(memory_space=pl.ANY)


def params(mebibytes=12):
    return pltpu.CompilerParams(vmem_limit_bytes=mebibytes * 1024 * 1024)


def near(array):
    return pltpu.with_memory_space_constraint(array, pltpu.VMEM)


def far(array):
    return pltpu.with_memory_space_constraint(array, pltpu.HBM)


def contract_last(rows, weight):
    return lax.dot_general(rows, weight, (((1,), (1,)), ((), ())), preferred_element_type=F32)


def shift(shard, axis, by):
    length = lax.axis_size(axis)
    return lax.ppermute(shard, axis, [(i, (i + by) % length) for i in range(length)])


def after(value, *earlier):
    return lax.optimization_barrier((value, *earlier))[0]


def slot_tables(route, gate, experts, capacity):
    fanout, tokens = route.shape
    slots = experts * capacity
    labels = lax.broadcasted_iota(jnp.int32, (experts, tokens), 0)
    picks = [(route[k : k + 1, :] == labels).astype(F32) for k in range(fanout)]
    member = functools.reduce(jnp.add, picks)
    row = lax.broadcasted_iota(jnp.int32, (tokens, tokens), 0)
    column = lax.broadcasted_iota(jnp.int32, (tokens, tokens), 1)
    earlier = (row < column).astype(BF16)
    rank = jnp.dot(member.astype(BF16), earlier, preferred_element_type=F32)
    place = rank + (labels * capacity).astype(F32)
    slot_ids = lax.broadcasted_iota(jnp.int32, (slots, tokens), 0)
    table = jnp.zeros((slots, tokens), F32)
    high = jnp.zeros((slots, tokens), F32)
    low = jnp.zeros((slots, tokens), F32)
    for k in range(fanout):
        target = jnp.sum(picks[k] * place, axis=0, keepdims=True).astype(jnp.int32)
        hit = (slot_ids == target).astype(F32)
        gate_k = gate[k : k + 1, :]
        high_k = ((gate_k >> 7) << 7).astype(F32) * (1.0 / 65536.0)
        low_k = (gate_k & 127).astype(F32) * (1.0 / 65536.0)
        table += hit
        high += hit * high_k
        low += hit * low_k
    return table.astype(BF16), jnp.concatenate([high, low], axis=1).astype(BF16)


def dispatch_kernel(experts, capacity, rf, gf, rb, gb, f, x, send, table_b, mix_f, mix_b):
    quarter = f.shape[1]
    table, mix_f[...] = slot_tables(rf[...], gf[...], experts, capacity)
    send[:, :quarter] = jnp.dot(table, f[...], preferred_element_type=F32).astype(BF16)
    table, mix_b[...] = slot_tables(rb[...], gb[...], experts, capacity)
    table_b[...] = table
    send[:, quarter:] = jnp.dot(table, x[...], preferred_element_type=F32).astype(BF16)


def dispatch(rf, gf, rb, gb, f, x, experts, capacity):
    tokens, quarter = f.shape
    slots = experts * capacity
    return pl.pallas_call(
        functools.partial(dispatch_kernel, experts, capacity),
        out_shape=(
            pltpu.HBM((slots, 2 * quarter), BF16),
            pltpu.HBM((slots, tokens), BF16),
            pltpu.HBM((slots, 2 * tokens), BF16),
            pltpu.HBM((slots, 2 * tokens), BF16),
        ),
        compiler_params=params(),
    )(*[far(array) for array in (rf, gf, rb, gb, f, x)])


def dispatch_whole_kernel(order, table, p0, p1, p2, p3, send):
    quarter = p0.shape[1]
    for n, piece in enumerate((p0, p1, p2, p3)):
        rows = jnp.dot(table[...], piece[...], preferred_element_type=F32).astype(BF16)
        send[:, pl.ds(pl.multiple_of(order[n] * quarter, quarter), quarter)] = rows


def dispatch_whole(order, table, pieces):
    slots = table.shape[0]
    features = 4 * pieces[0].shape[1]
    return pl.pallas_call(
        dispatch_whole_kernel,
        in_specs=[SMEM] + [VMEM] * 5,
        out_specs=VMEM,
        out_shape=pltpu.HBM((slots, features), BF16),
        compiler_params=params(),
    )(order, table, *pieces)


def tiles(units, tile=256):
    return [(start, min(tile, units - start)) for start in range(0, units, tile)]


def columns(number, quarter):
    return pl.ds(pl.multiple_of(number * quarter, quarter), quarter)


def load_kernel(*refs):
    count = (len(refs) - 2) // 2
    mark, semaphores = refs[-2:]
    copies = [pltpu.make_async_copy(refs[n], refs[count + n], semaphores.at[n]) for n in range(count)]
    for copy in copies:
        copy.start()
    mark[...] = jnp.zeros_like(mark)
    for copy in copies:
        copy.wait()


def load_weights(weights):
    return pl.pallas_call(
        load_kernel,
        in_specs=[ANY] * len(weights),
        out_specs=[VMEM] * (len(weights) + 1),
        out_shape=[pltpu.VMEM(weight.shape, weight.dtype) for weight in weights]
        + [jax.ShapeDtypeStruct((8, 128), F32)],
        scratch_shapes=[pltpu.SemaphoreType.DMA((len(weights),))],
        compiler_params=params(2),
        cost_estimate=pl.CostEstimate(
            flops=0, bytes_accessed=sum(weight.size * 2 for weight in weights), transcendentals=0
        ),
    )(*[far(weight) for weight in weights])


def held_kernel(*refs):
    pass


def held(array, *earlier):
    return pl.pallas_call(
        held_kernel,
        in_specs=[ANY] * (1 + len(earlier)),
        out_specs=ANY,
        out_shape=jax.ShapeDtypeStruct(array.shape, array.dtype),
        input_output_aliases={0: 0},
        compiler_params=params(2),
        cost_estimate=pl.CostEstimate(flops=0, bytes_accessed=16 * 1024 * 1024, transcendentals=0),
    )(array, *earlier)


def halves_kernel(from_last, from_next, *refs):
    top, bottom = refs[-2:]
    half = top.shape[0]
    top[...] = from_last[:half]
    bottom[...] = from_next[half:]


def halves(from_last, from_next, *earlier):
    rows, quarter = from_last.shape
    return pl.pallas_call(
        halves_kernel,
        in_specs=[VMEM] * 2 + [ANY] * len(earlier),
        out_specs=[VMEM] * 2,
        out_shape=[jax.ShapeDtypeStruct((rows // 2, quarter), from_last.dtype)] * 2,
        compiler_params=params(4),
    )(from_last, from_next, *earlier)


def piece_sums(order, first_entry, pieces, wg, wu, part):
    quarter = pieces[0].shape[1]
    sums = []
    for weight in (wg, wu):
        terms = [
            contract_last(piece[...], weight[part, columns(order[first_entry + n], quarter)])
            for n, piece in enumerate(pieces)
        ]
        sums.append(functools.reduce(jnp.add, terms))
    return sums


def begin_kernel(order, p0, p1, p2, wg, wu, sum_a, sum_b):
    for start, size in tiles(wg.shape[0]):
        part = slice(start, start + size)
        sum_a[:, part], sum_b[:, part] = piece_sums(order, 0, (p0, p1, p2), wg, wu, part)


def begin_loading_kernel(order, p0, p1, p2, wg, wu, wd, sum_a, sum_b, near_g, near_u, near_d, semaphores):
    spans = load_spans(wg.shape[0])
    copies = []
    for p, (start, size) in enumerate(spans):
        span = pl.ds(start, size)
        copies.append(
            [
                pltpu.make_async_copy(wg.at[span, :], near_g.at[span, :], semaphores.at[p, 0]),
                pltpu.make_async_copy(wu.at[span, :], near_u.at[span, :], semaphores.at[p, 1]),
            ]
        )
    copies.append([pltpu.make_async_copy(wd, near_d, semaphores.at[len(spans), 0])])
    for copy in copies[0] + copies[1]:
        copy.start()
    for p, (begin, length) in enumerate(spans):
        for copy in copies[p]:
            copy.wait()
        if p + 2 < len(copies):
            for copy in copies[p + 2]:
                copy.start()
        for start, size in tiles(length):
            part = slice(begin + start, begin + start + size)
            sum_a[:, part], sum_b[:, part] = piece_sums(order, 0, (p0, p1, p2), near_g, near_u, part)
    copies[-1][0].wait()


def begin(order, pieces, weights):
    loading = len(weights) == 3
    rows, quarter = pieces[0].shape
    units = weights[0].shape[0]
    return pl.pallas_call(
        begin_loading_kernel if loading else begin_kernel,
        in_specs=[SMEM] + [VMEM] * 3 + [ANY if loading else VMEM] * len(weights),
        out_specs=[VMEM] * (5 if loading else 2),
        out_shape=[pltpu.VMEM((rows, units), F32)] * 2
        + ([pltpu.VMEM(w.shape, w.dtype) for w in weights] if loading else []),
        scratch_shapes=[pltpu.SemaphoreType.DMA((len(load_spans(units)) + 1, 2))] if loading else [],
        compiler_params=params(),
        cost_estimate=pl.CostEstimate(
            flops=12 * rows * quarter * units, bytes_accessed=12 * units * quarter, transcendentals=0
        ),
    )(order, *pieces, *[(far if loading else near)(w) for w in weights])


def finish_kernel(forward, order, top, bottom, sum_a, sum_b, wg, wu, *outs):
    rows = outs[-1]
    half = top.shape[0]
    rows[:half] = top[...]
    rows[half:] = bottom[...]
    for start, size in tiles(wg.shape[0]):
        part = slice(start, start + size)
        a, b = piece_sums(order, 3, (rows,), wg, wu, part)
        a += sum_a[:, part]
        b += sum_b[:, part]
        q = jax.nn.sigmoid(a)
        if forward:
            outs[0][:, part] = (a * q * b).astype(BF16)
        else:
            outs[0][:, part] = b * q * (1.0 + a * (1.0 - q))
            outs[1][:, part] = a * q


def finish(forward, order, halves, sums, wg, wu):
    rows, units = sums[0].shape
    quarter = halves[0].shape[1]
    outs = [pltpu.VMEM((rows, units), BF16)] if forward else [pltpu.VMEM((rows, units), F32)] * 2
    return pl.pallas_call(
        functools.partial(finish_kernel, forward),
        in_specs=[SMEM] + [VMEM] * 6,
        out_specs=[VMEM] * len(outs),
        out_shape=outs,
        scratch_shapes=[pltpu.VMEM((rows, quarter), BF16)],
        compiler_params=params(),
        cost_estimate=pl.CostEstimate(
            flops=4 * rows * quarter * units, bytes_accessed=4 * units * quarter, transcendentals=rows * units
        ),
    )(order, *halves, *[near(array) for array in (*sums, wg, wu)])


def load_spans(units):
    cuts = [0, min(256, units), min(768, units), units]
    return [(low, high - low) for low, high in zip(cuts, cuts[1:]) if high > low]


def grads_kernel(c, for_gate, for_up, wd, da, db):
    for start, size in tiles(wd.shape[0]):
        part = slice(start, start + size)
        dh = contract_last(c[...], wd[part, :])
        da[:, part] = (dh * for_gate[:, part]).astype(BF16)
        db[:, part] = (dh * for_up[:, part]).astype(BF16)


def hidden_grads(c, for_gate, for_up, wd):
    rows, features = c.shape
    units = wd.shape[0]
    return pl.pallas_call(
        grads_kernel,
        in_specs=[VMEM] * 4,
        out_specs=[VMEM] * 2,
        out_shape=[pltpu.VMEM((rows, units), BF16)] * 2,
        compiler_params=params(),
        cost_estimate=pl.CostEstimate(
            flops=2 * rows * features * units, bytes_accessed=2 * units * features, transcendentals=0
        ),
    )(c, near(for_gate), near(for_up), near(wd))


def down_kernel(which, pairs, order, *refs):
    acts, weights, outs = refs[:pairs], refs[pairs : 2 * pairs], refs[2 * pairs :]
    quarter = weights[0].shape[1] // 4
    for n, entry in enumerate(which):
        slots = columns(order[entry], quarter)
        total = functools.reduce(
            jnp.add, [jnp.dot(a[...], w[:, slots], preferred_element_type=F32) for a, w in zip(acts, weights)]
        )
        if len(which) == 4:
            outs[0][:, slots] = total.astype(outs[0].dtype)
        elif len(which) == 1:
            half = outs[0].shape[0]
            outs[0][...] = total[:half].astype(outs[0].dtype)
            outs[1][...] = total[half:].astype(outs[1].dtype)
        else:
            outs[n][...] = total.astype(outs[n].dtype)


def down_projections(order, which, acts, weights, outs):
    rows, units = acts[0].shape
    quarter = weights[0].shape[1] // 4
    pairs = len(acts)
    return pl.pallas_call(
        functools.partial(down_kernel, which, pairs),
        in_specs=[SMEM] + [VMEM] * (2 * pairs),
        out_specs=[VMEM] * len(outs),
        out_shape=outs,
        compiler_params=params(),
        cost_estimate=pl.CostEstimate(
            flops=2 * len(which) * pairs * rows * units * quarter,
            bytes_accessed=2 * len(which) * pairs * units * quarter,
            transcendentals=0,
        ),
    )(order, *[near(array) for array in (*acts, *weights)])


def passed_kernel(to_next, to_last, up, down, next_sum, last_sum):
    half = up.shape[0]
    next_sum[:half] = (to_next[:half].astype(F32) + up[...].astype(F32)).astype(BF16)
    next_sum[half:] = to_next[half:]
    last_sum[:half] = to_last[:half]
    last_sum[half:] = (to_last[half:].astype(F32) + down[...].astype(F32)).astype(BF16)


def total_kernel(own, from_last, from_next, out):
    out[...] = (own[...] + from_last[...].astype(F32) + from_next[...].astype(F32)).astype(BF16)


def summed_over_tensor(order, acts, weights, earlier):
    rows = acts[0].shape[0]
    quarter = weights[0].shape[1] // 4
    whole = jax.ShapeDtypeStruct((rows, quarter), BF16)
    half = jax.ShapeDtypeStruct((rows // 2, quarter), BF16)
    top, bottom = down_projections(order, (3,), acts, weights, [half, half])
    up = shift(top, "tensor", 1)
    down = shift(bottom, "tensor", -1)
    kept = [pltpu.VMEM(whole.shape, BF16)] * 2 + [pltpu.VMEM(whole.shape, F32)]
    to_next, to_last, own = down_projections(order, (2, 1, 0), acts, weights, kept)
    to_next, to_last = pl.pallas_call(passed_kernel, out_shape=[whole, whole], compiler_params=params())(
        near(to_next), near(to_last), up, down
    )
    from_last = shift(to_next, "tensor", 1)
    from_next = shift(to_last, "tensor", -1)
    from_next = after(from_next, *earlier)
    return pl.pallas_call(total_kernel, out_shape=whole, compiler_params=params())(near(own), from_last, from_next)


def mix(table, back):
    both = lax.dot_general(table, back, (((0,), (0,)), ((), ())), preferred_element_type=F32)
    tokens = both.shape[0] // 2
    return both[:tokens] + both[tokens:]


def mix_kernel(table, back, residual, out):
    out[...] = (residual[...].astype(F32) + mix(table[...], back[...])).astype(BF16)


def mixed(table, back, residual):
    return pl.pallas_call(
        mix_kernel, out_shape=jax.ShapeDtypeStruct(residual.shape, BF16), compiler_params=params()
    )(table, back, residual)


def mix_parts_kernel(order, table, back, residual, own, to_last, to_next, to_opposite):
    quarter = residual.shape[1]
    own[...] = residual[...].astype(F32) + mix(table[...], back[:, columns(order[0], quarter)])
    for entry, out in ((1, to_last), (2, to_next), (3, to_opposite)):
        out[...] = mix(table[...], back[:, columns(order[entry], quarter)]).astype(BF16)


def mixed_over_tensor(order, table, back, residual):
    part = jax.ShapeDtypeStruct(residual.shape, BF16)
    own, to_last, to_next, to_opposite = pl.pallas_call(
        mix_parts_kernel,
        in_specs=[SMEM] + [VMEM] * 3,
        out_specs=[VMEM] * 4,
        out_shape=[jax.ShapeDtypeStruct(residual.shape, F32), part, part, part],
        compiler_params=params(),
    )(order, table, back, residual)
    return own, to_last, to_next, to_opposite


def total_over_tensor(own, to_last, to_next, to_opposite):
    received = (shift(to_last, "tensor", -1), shift(to_next, "tensor", 1), shift(to_opposite, "tensor", 2))
    return (own + sum(piece.astype(F32) for piece in received)).astype(BF16)


def exchange(rows):
    return lax.all_to_all(rows, "expert", split_axis=0, concat_axis=0, tiled=True)


def local(fwd_in, bwd_in, cotangent, route_fwd, gate_fwd, route_bwd, gate_bwd, w_gate, w_up, w_down):
    experts = lax.axis_size("expert")
    f, x, c = fwd_in[0], bwd_in[0], cotangent[0]
    tokens, quarter = f.shape
    fanout = route_fwd.shape[2]
    capacity = min(tokens, max(2, tokens * fanout * 3 // (2 * experts)))
    place = lax.axis_index("tensor").astype(jnp.int32)
    order = (place + jnp.array([0, 3, 1, 2], jnp.int32)) % 4

    c_pieces = (c, shift(c, "tensor", 1), shift(c, "tensor", -1), shift(c, "tensor", 2))
    send, table_b, mix_f, mix_b = dispatch(
        route_fwd[0].T, gate_fwd[0].T, route_bwd[0].T, gate_bwd[0].T, f, x, experts, capacity
    )
    wg, wu, wd = w_gate[0, 0], w_up[0, 0], w_down[0, 0]
    got = exchange(send)
    send_c = dispatch_whole(order, table_b, c_pieces)
    got, send_c = lax.optimization_barrier((got, send_c))
    f0, x0 = got[:, :quarter], got[:, quarter:]
    rows_c = exchange(after(send_c, f0, x0))
    f_last, f_next = shift(f0, "tensor", 1), shift(f0, "tensor", -1)
    near_g, near_u, near_d, loaded = load_weights((wg, wu, wd))
    f_top, f_bottom = halves(f_last, f_next, loaded)
    f_opposite = shift(f_top, "tensor", 1), shift(f_bottom, "tensor", -1)
    x0 = held(x0, f_top, f_bottom)
    x_next, x_last = shift(x0, "tensor", -1), shift(x0, "tensor", 1)
    x_top, x_bottom = halves(x_last, x_next)
    x_opposite = shift(x_top, "tensor", 1), shift(x_bottom, "tensor", -1)

    sums = begin(order, (f0, f_last, f_next), (near_g, near_u))
    (hidden,) = finish(True, order, f_opposite, sums, near_g, near_u)
    whole = pltpu.HBM((hidden.shape[0], wd.shape[1]), BF16)
    (part_f,) = down_projections(order, (0, 1, 2, 3), (hidden,), (near_d,), [whole])
    back_f = exchange(part_f)
    *sums, near_g, near_u, near_d = begin(order, (held(x0, part_f), x_last, x_next), (wg, wu, wd))
    for_gate, for_up = finish(False, order, x_opposite, sums, near_g, near_u)
    da, db = hidden_grads(rows_c, for_gate, for_up, near_d)
    mixed_f = mixed_over_tensor(order, mix_f, back_f, f)
    share_b = summed_over_tensor(order, (da, db), (near_g, near_u), mixed_f)
    out_f = total_over_tensor(*mixed_f)
    out_b = mixed(mix_b, exchange(share_b), c)
    return shift(out_f[None], "pipe", 1), shift(out_b[None], "pipe", -1)


def solution(mesh):
    rows = P("pipe", "expert", "tensor")
    routes = P("pipe", "expert", None)
    weights = P("pipe", "expert", "tensor", None)
    return jax.shard_map(
        local,
        mesh=mesh,
        in_specs=(rows, rows, rows, routes, routes, routes, routes, weights, weights, weights),
        out_specs=(rows, rows),
        check_vma=False,
    )
```

time: 212 us -> 159 us (0.75)
  blocking collectives: 23.5 us -> 0 us
  Pallas kernels: 82.6 us -> 60 us
  local copies, waits for them, and re-layouts: 17.3 us -> 3.73 us
  starting transfers between devices: 39.3 us -> 52.8 us
  other arithmetic: 6.11 us -> 0.06 us
    all_to_all x1 -> x0, blocking collectives: 23.5 us -> none  [exchange(): lax.all_to_all(rows, 'expert', split_axis=0, concat_axis=0, tiled=True)]
    pallas_call x9 -> x17, Pallas kernels: 75.3 us -> 56.6 us  [the longest x2 16.3 us: begin(): pl.pallas_call(begin_loading_kernel if loading else begin_kernel, in_spec...]
    all_to_all x3 -> x4, starting transfers between devices: 11 us -> 20.2 us  [exchange(): lax.all_to_all(rows, 'expert', split_axis=0, concat_axis=0, tiled=True)]
    unnamed x36 -> x26, local copies, waits for them, and re-layouts: 10.7 us -> 3.65 us
    convert_element_type x4 -> x0, other arithmetic: 5.29 us -> none  [the longest x2 5.01 us: summed_over_tensor(): return (own + from_last.astype(F32) + from_next.astype(F32)).astype(BF16)]
    all_to_all x3 -> x4, waiting for transfers between devices: 9.86 us -> 4.86 us  [exchange(): lax.all_to_all(rows, 'expert', split_axis=0, concat_axis=0, tiled=True)]
    ppermute x19 -> x20, waiting for transfers between devices: 31.1 us -> 35.5 us  [shift(): lax.ppermute(shard, axis, [(i, (i + by) % length) for i in range(length)])]
    ppermute x19 -> x20, starting transfers between devices: 28.3 us -> 32.6 us  [shift(): lax.ppermute(shard, axis, [(i, (i + by) % length) for i in range(length)])]
  transfers between devices with their start and end apart: 22 -> 24, of which waited for: 8 -> 14; matrix products, arithmetic and copies ran while one was open for 6% -> 0% of each run, Pallas kernels for 38% -> 35%
where the time goes in v2:
time: 159 us; the launch traced here: 158 us
  Pallas kernels  60 us (38%)
  starting transfers between devices  52.8 us (33%)
  waiting for transfers between devices  40.4 us (25%)
  local copies, waits for them, and re-layouts  3.73 us (2%)
    ppermute x20, waiting for transfers between devices, shift(): lax.ppermute(shard, axis, [(i, (i + by) % length) for i in range(length)])  35.5 us
    ppermute x20, starting transfers between devices, shift(): lax.ppermute(shard, axis, [(i, (i + by) % length) for i in range(length)])  32.6 us
    all_to_all x4, starting transfers between devices, exchange(): lax.all_to_all(rows, 'expert', split_axis=0, concat_axis=0, tiled=True)  20.2 us
    pallas_call x2, Pallas kernels, begin(): pl.pallas_call(begin_loading_kernel if loading else begin_kernel, in_spec...  16.3 us
    pallas_call x3, Pallas kernels, down_projections(): pl.pallas_call(functools.partial(down_kernel, which, pairs), in_specs=[SM...  14.8 us
    pallas_call x1, Pallas kernels, load_weights(): pl.pallas_call(load_kernel, in_specs=[ANY] * len(weights), out_specs=[VME...  8.07 us
    pallas_call x2, Pallas kernels, finish(): pl.pallas_call(functools.partial(finish_kernel, forward), in_specs=[SMEM]...  5.51 us
    all_to_all x4, waiting for transfers between devices, exchange(): lax.all_to_all(rows, 'expert', split_axis=0, concat_axis=0, tiled=True)  4.86 us
  transfers between devices with their start and end apart: 24, of which 14 were waited for; matrix products, arithmetic and copies ran while one was open for 0% of the time, Pallas kernels for 35%

profile of v2, /device:TPU:0, one launch (start us, length us, event | category | flops | bytes accessed | tf_op | source)
XLA Modules:
  0.0 157.9 jit_solution(7394591665955581864)
XLA Ops:
  0.7 3.1 %shard_map.122 = (bf16[384,1536]{1,0:T(8,128)(2,1)}, bf16[384,64]{1,0:T(8,128)(2,1)}, bf16[384,128]{1,0:T(8,128)(2,1)}, bf16[384,128]{1,0:T(8,128)(2,1)}) custom-call(s32[4,64]{1,0:T(4,128)} %bitcast.50, s32[4,64]{1,0:T(4,128)} %bitcast.51, s32[4,64]{1,0:T(4,128)} %bitcast.52, s32[4,64]{1,0:T(4,128)} %bitcast.53, bf16[64,768]{1,0:T(8,128)(2,1)} %bitcast.37, ...), custom_call_target="tpu_custom_call" | custom-call | tf_op jit(solution)/shard_map/pallas_call | solution.py:81
  3.7 5.7 %all-to-all-start = ((bf16[16,24,1536]{2,1,0:T(8,128)(2,1)}), bf16[16,24,1536]{2,1,0:T(8,128)(2,1)S(1)}, u32[]{:S(2)}, u32[]{:S(2)}) async-start(bf16[16,24,1536]{2,1,0:T(8,128)(2,1)} %bitcast.48), calls=%async_computation | async-start | bytes 2359296 | tf_op jit(solution)/shard_map/all_to_all | solution.py:413
  9.5 4.0 %collective-permute-start.2 = (bf16[64,768]{1,0:T(8,128)(2,1)S(1)}, bf16[64,768]{1,0:T(8,128)(2,1)S(1)}, u32[]{:S(2)}, u32[]{:S(2)}) collective-permute-start(bf16[64,768]{1,0:T(8,128)(2,1)S(1)} %bitcast.32), channel_id=1, source_target_pairs={{0,2},{1,3},{2,0},{3,1},{4,6},{5,7},{6,4},{7,5},{8,10},{9,11},{10,... | collective-permute-start | bytes 294920 | tf_op jit(solution)/shard_map/ppermute | solution.py:35
  16.8 2.9 %collective-permute-done.1.p2 = bf16[64,768]{1,0:T(8,128)(2,1)S(1)} collective-permute-done((bf16[64,768]{1,0:T(8,128)(2,1)S(1)}, bf16[64,768]{1,0:T(8,128)(2,1)S(1)}, u32[]{:S(2)}, u32[]{:S(2)}) %collective-permute-start.1) | collective-permute-done | bytes 98336 | tf_op jit(solution)/shard_map/ppermute | solution.py:35
  20.0 2.7 %shard_map.123 = bf16[384,3072]{1,0:T(8,128)(2,1)} custom-call(s32[4]{0:T(128)S(1)} %and_select_fusion.order, bf16[384,64]{1,0:T(8,128)(2,1)S(1)} %copy-done.7, bf16[64,768]{1,0:T(8,128)(2,1)S(1)} %bitcast.35, bf16[64,768]{1,0:T(8,128)(2,1)S(1)} %collective-permute-done.p1, bf16[64,768]{1,0:T(8,128)(2,1)S(1)} %collective-permute-done.1.p2, ...), custom_call_target="tpu_custom_call" | custom-call | tf_op jit(solution)/shard_map/pallas_call | solution.py:103
  22.7 4.8 %all-to-all-done = bf16[16,24,1536]{2,1,0:T(8,128)(2,1)S(1)} async-done(((bf16[16,24,1536]{2,1,0:T(8,128)(2,1)}), bf16[16,24,1536]{2,1,0:T(8,128)(2,1)S(1)}, u32[]{:S(2)}, u32[]{:S(2)}) %all-to-all-start) | async-done | bytes 1179680 | tf_op jit(solution)/shard_map/all_to_all | solution.py:413
  27.6 3.7 %all-to-all-start.2 = ((bf16[16,24,3072]{2,1,0:T(8,128)(2,1)}), bf16[16,24,3072]{2,1,0:T(8,128)(2,1)S(1)}, u32[]{:S(2)}, u32[]{:S(2)}) async-start(bf16[16,24,3072]{2,1,0:T(8,128)(2,1)} %bitcast.46), calls=%async_computation.2 | async-start | bytes 4718592 | tf_op jit(solution)/shard_map/all_to_all | solution.py:413
  31.4 4.1 %collective-permute-start.4 = (bf16[384,768]{1,0:T(8,128)(2,1)S(1)}, bf16[384,768]{1,0:T(8,128)(2,1)S(1)}, u32[]{:S(2)}, u32[]{:S(2)}) collective-permute-start(bf16[384,768]{1,0:T(8,128)(2,1)S(1)} %get-tuple-element.79.p0), channel_id=1, source_target_pairs={{0,3},{1,0},{2,1},{3,2},{4,7},{5,4},{6,5},{7,6},{8,11},{9,8},{10,9... | collective-permute-start | bytes 1769480 | tf_op jit(solution)/shard_map/ppermute | solution.py:35
  35.5 8.1 %shard_map.124 = (bf16[1344,3072]{1,0:T(8,128)(2,1)S(1)}, bf16[1344,3072]{1,0:T(8,128)(2,1)S(1)}, bf16[1344,3072]{1,0:T(8,128)(2,1)S(1)}, f32[8,128]{1,0:T(8,128)S(1)}) custom-call(bf16[1344,3072]{1,0:T(8,128)(2,1)} %bitcast.40, bf16[1344,3072]{1,0:T(8,128)(2,1)} %bitcast.42, bf16[1344,3072]{1,0:T(8,128)(2,1)} %bitcast.44), custom_call_target="tpu_custom_call" | custom-call | bytes 24772608 | tf_op jit(solution)/shard_map/pallas_call | solution.py:132
  43.6 4.9 %collective-permute-done.4.from_next.p2 = bf16[384,768]{1,0:T(8,128)(2,1)S(1)} collective-permute-done((bf16[384,768]{1,0:T(8,128)(2,1)S(1)}, bf16[384,768]{1,0:T(8,128)(2,1)S(1)}, u32[]{:S(2)}, u32[]{:S(2)}) %collective-permute-start.4) | collective-permute-done | bytes 589856 | tf_op jit(solution)/shard_map/ppermute | solution.py:35
  48.4 3.4 %collective-permute-done.3.from_last.p1 = bf16[384,768]{1,0:T(8,128)(2,1)S(1)} collective-permute-done((bf16[384,768]{1,0:T(8,128)(2,1)S(1)}, bf16[384,768]{1,0:T(8,128)(2,1)S(1)}, u32[]{:S(2)}, u32[]{:S(2)}) %collective-permute-start.3) | collective-permute-done | bytes 589856 | tf_op jit(solution)/shard_map/ppermute | solution.py:35
  52.0 3.2 %collective-permute-start.6 = (bf16[192,768]{1,0:T(8,128)(2,1)S(1)}, bf16[192,768]{1,0:T(8,128)(2,1)S(1)}, u32[]{:S(2)}, u32[]{:S(2)}) collective-permute-start(bf16[192,768]{1,0:T(8,128)(2,1)S(1)} %get-tuple-element.46.refs_2_), channel_id=1, source_target_pairs={{0,3},{1,0},{2,1},{3,2},{4,7},{5,4},{6,5},{7,6},{8,11},{9,8},{10,9... | collective-permute-start | bytes 884744 | tf_op jit(solution)/shard_map/ppermute | solution.py:35
  57.2 6.2 %shard_map.126 = (f32[384,1344]{1,0:T(8,128)S(1)}, f32[384,1344]{1,0:T(8,128)S(1)}) custom-call(s32[4]{0:T(128)S(1)} %and_select_fusion.order, bf16[384,768]{1,0:T(8,128)(2,1)S(1)} %copy-done.2, bf16[384,768]{1,0:T(8,128)(2,1)S(1)} %collective-permute-done.3.from_last.p1, bf16[384,768]{1,0:T(8,128)(2,1)S(1)} %collective-permute-done.4.from_next.p2, ...), custom_call_target="tpu_custom_call" | custom-call | flops 4756340736 | bytes 12386304 | tf_op jit(solution)/shard_map/pallas_call | solution.py:228
  63.5 2.7 %shard_map.127.refs_0_ = bf16[384,1344]{1,0:T(8,128)(2,1)S(1)} custom-call(s32[4]{0:T(128)S(1)} %and_select_fusion.order, bf16[192,768]{1,0:T(8,128)(2,1)S(1)} %collective-permute-done.5.top, bf16[192,768]{1,0:T(8,128)(2,1)S(1)} %collective-permute-done.6.bottom, f32[384,1344]{1,0:T(8,128)S(1)} %get-tuple-element.49.sum_a, ...), custom_call_target="tpu_custom_call" | custom-call | flops 1585446912 | bytes 4128768 | tf_op jit(solution)/shard_map/pallas_call | solution.py:264
  66.2 5.9 %shard_map.128.refs_1_ = bf16[384,3072]{1,0:T(8,128)(2,1)} custom-call(s32[4]{0:T(128)S(1)} %and_select_fusion.order, bf16[384,1344]{1,0:T(8,128)(2,1)S(1)} %shard_map.127.refs_0_, bf16[1344,3072]{1,0:T(8,128)(2,1)S(1)} %get-tuple-element.51.refs_1_), custom_call_target="tpu_custom_call" | custom-call | flops 3170893824 | bytes 8257536 | tf_op jit(solution)/shard_map/pallas_call | solution.py:327
  72.1 5.6 %all-to-all-start.1 = ((bf16[16,24,3072]{2,1,0:T(8,128)(2,1)}), bf16[16,24,3072]{2,1,0:T(8,128)(2,1)}, u32[]{:S(2)}, u32[]{:S(2)}) async-start(bf16[16,24,3072]{2,1,0:T(8,128)(2,1)} %bitcast.30), calls=%async_computation.1 | async-start | bytes 4718592 | tf_op jit(solution)/shard_map/all_to_all | solution.py:413
  80.6 3.2 %collective-permute-start.14 = (bf16[192,768]{1,0:T(8,128)(2,1)S(1)}, bf16[192,768]{1,0:T(8,128)(2,1)S(1)}, u32[]{:S(2)}, u32[]{:S(2)}) collective-permute-start(bf16[192,768]{1,0:T(8,128)(2,1)S(1)} %get-tuple-element.60), channel_id=1, source_target_pairs={{0,3},{1,0},{2,1},{3,2},{4,7},{5,4},{6,5},{7,6},{8,11},{9,8},{10,9... | collective-permute-start | bytes 884744 | tf_op jit(solution)/shard_map/ppermute | solution.py:35
  83.8 10.1 %shard_map.133 = (f32[384,1344]{1,0:T(8,128)S(1)}, f32[384,1344]{1,0:T(8,128)S(1)}, bf16[1344,3072]{1,0:T(8,128)(2,1)S(1)}, bf16[1344,3072]{1,0:T(8,128)(2,1)S(1)}, bf16[1344,3072]{1,0:T(8,128)(2,1)S(1)}) custom-call(s32[4]{0:T(128)S(1)} %and_select_fusion.order, bf16[384,768]{1,0:T(8,128)(2,1)S(1)} %shard_map.132.p0, ...), custom_call_target="tpu_custom_call" | custom-call | flops 4756340736 | bytes 12386304 | tf_op jit(solution)/shard_map/pallas_call | solution.py:228
  93.9 2.9 %shard_map.134 = (f32[384,1344]{1,0:T(8,128)S(1)}, f32[384,1344]{1,0:T(8,128)S(1)}) custom-call(s32[4]{0:T(128)S(1)} %and_select_fusion.order, bf16[192,768]{1,0:T(8,128)(2,1)S(1)} %collective-permute-done.13.top, bf16[192,768]{1,0:T(8,128)(2,1)S(1)} %collective-permute-done.14.bottom, f32[384,1344]{1,0:T(8,128)S(1)} %get-tuple-element.61.sum_a, ...), custom_call_target="tpu_custom_call" | custom-call | flops 1585446912 | bytes 4128768 | tf_op jit(solution)/shard_map/pallas_call | solution.py:264
  96.8 3.8 %shard_map.135 = (bf16[384,1344]{1,0:T(8,128)(2,1)S(1)}, bf16[384,1344]{1,0:T(8,128)(2,1)S(1)}) custom-call(bf16[384,3072]{1,0:T(8,128)(2,1)S(1)} %bitcast.29, f32[384,1344]{1,0:T(8,128)S(1)} %get-tuple-element.65.for_gate, f32[384,1344]{1,0:T(8,128)S(1)} %get-tuple-element.66.for_up, bf16[1344,3072]{1,0:T(8,128)(2,1)S(1)} %get-tuple-element.67.wd), custom_call_target="tpu_custom_call" | custom-call | flops 3170893824 | bytes 8257536 | tf_op jit(solution)/shard_map/pallas_call | solution.py:293
  100.6 2.6 %shard_map.137 = (bf16[192,768]{1,0:T(8,128)(2,1)S(1)}, bf16[192,768]{1,0:T(8,128)(2,1)S(1)}) custom-call(s32[4]{0:T(128)S(1)} %and_select_fusion.order, bf16[384,1344]{1,0:T(8,128)(2,1)S(1)} %get-tuple-element.68.refs_0_, bf16[384,1344]{1,0:T(8,128)(2,1)S(1)} %get-tuple-element.69.refs_1_, bf16[1344,3072]{1,0:T(8,128)(2,1)S(1)} %get-tuple-element.63.wg.refs_2_, ...), custom_call_target="tpu_custom_call" | custom-call | flops 1585446912 | bytes 4128768 | tf_op jit(solution)/shard_map/pallas_call | solution.py:327
  103.3 3.2 %collective-permute-start.16 = (bf16[192,768]{1,0:T(8,128)(2,1)S(1)}, bf16[192,768]{1,0:T(8,128)(2,1)S(1)}, u32[]{:S(2)}, u32[]{:S(2)}) collective-permute-start(bf16[192,768]{1,0:T(8,128)(2,1)S(1)} %get-tuple-element.74), channel_id=1, source_target_pairs={{0,3},{1,0},{2,1},{3,2},{4,7},{5,4},{6,5},{7,6},{8,11},{9,8},{10,9... | collective-permute-start | bytes 884744 | tf_op jit(solution)/shard_map/ppermute | solution.py:35
  106.5 6.3 %shard_map.136 = (bf16[384,768]{1,0:T(8,128)(2,1)S(1)}, bf16[384,768]{1,0:T(8,128)(2,1)S(1)}, f32[384,768]{1,0:T(8,128)S(1)}) custom-call(s32[4]{0:T(128)S(1)} %and_select_fusion.order, bf16[384,1344]{1,0:T(8,128)(2,1)S(1)} %get-tuple-element.68.refs_0_, bf16[384,1344]{1,0:T(8,128)(2,1)S(1)} %get-tuple-element.69.refs_1_, ...), custom_call_target="tpu_custom_call" | custom-call | flops 4756340736 | bytes 12386304 | tf_op jit(solution)/shard_map/pallas_call | solution.py:327
  114.3 3.0 %collective-permute-start.18 = (bf16[384,768]{1,0:T(8,128)(2,1)}, bf16[384,768]{1,0:T(8,128)(2,1)S(1)}, u32[]{:S(2)}, u32[]{:S(2)}) collective-permute-start(bf16[384,768]{1,0:T(8,128)(2,1)} %get-tuple-element.76), channel_id=1, source_target_pairs={{0,3},{1,0},{2,1},{3,2},{4,7},{5,4},{6,5},{7,6},{8,11},{9,8},{10,9... | collective-permute-start | bytes 1769480 | tf_op jit(solution)/shard_map/ppermute | solution.py:35
  120.2 8.9 %collective-permute-done.18.from_next = bf16[384,768]{1,0:T(8,128)(2,1)S(1)} collective-permute-done((bf16[384,768]{1,0:T(8,128)(2,1)}, bf16[384,768]{1,0:T(8,128)(2,1)S(1)}, u32[]{:S(2)}, u32[]{:S(2)}) %collective-permute-start.18) | collective-permute-done | bytes 589856 | tf_op jit(solution)/shard_map/ppermute | solution.py:35
  129.2 3.1 %collective-permute-done.17.from_last = bf16[384,768]{1,0:T(8,128)(2,1)S(1)} collective-permute-done((bf16[384,768]{1,0:T(8,128)(2,1)S(1)}, bf16[384,768]{1,0:T(8,128)(2,1)S(1)}, u32[]{:S(2)}, u32[]{:S(2)}) %collective-permute-start.17) | collective-permute-done | bytes 589856 | tf_op jit(solution)/shard_map/ppermute | solution.py:35
  133.3 5.2 %all-to-all-start.3 = ((bf16[16,24,768]{2,1,0:T(8,128)(2,1)}), bf16[16,24,768]{2,1,0:T(8,128)(2,1)S(1)}, u32[]{:S(2)}, u32[]{:S(2)}) async-start(bf16[16,24,768]{2,1,0:T(8,128)(2,1)} %bitcast.21), calls=%async_computation.3 | async-start | bytes 1179648 | tf_op jit(solution)/shard_map/all_to_all | solution.py:413
  140.6 3.1 %collective-permute-done.7 = bf16[64,768]{1,0:T(8,128)(2,1)S(1)} collective-permute-done((bf16[64,768]{1,0:T(8,128)(2,1)S(1)}, bf16[64,768]{1,0:T(8,128)(2,1)S(1)}, u32[]{:S(2)}, u32[]{:S(2)}) %collective-permute-start.7) | collective-permute-done | bytes 98336 | tf_op jit(solution)/shard_map/ppermute | solution.py:35
  143.8 3.5 %collective-permute-done.8 = bf16[64,768]{1,0:T(8,128)(2,1)S(1)} collective-permute-done((bf16[64,768]{1,0:T(8,128)(2,1)S(1)}, bf16[64,768]{1,0:T(8,128)(2,1)S(1)}, u32[]{:S(2)}, u32[]{:S(2)}) %collective-permute-start.8) | collective-permute-done | bytes 98336 | tf_op jit(solution)/shard_map/ppermute | solution.py:35
  147.3 2.8 %collective-permute-start.10 = (bf16[1,64,768]{2,1,0:T(8,128)(2,1)S(1)}, bf16[1,64,768]{2,1,0:T(8,128)(2,1)S(1)}, u32[]{:S(2)}, u32[]{:S(2)}) collective-permute-start(bf16[1,64,768]{2,1,0:T(8,128)(2,1)S(1)} %fusion), channel_id=1, source_target_pairs={{0,64},{64,0},{1,65},{65,1},{2,66},{66,2},{3,67},{67,3},{4,68},{68... | collective-permute-start | bytes 294920 | tf_op jit(solution)/shard_map/ppermute | solution.py:35
  150.4 2.7 %collective-permute-start.19 = (bf16[1,64,768]{2,1,0:T(8,128)(2,1)S(1)}, bf16[1,64,768]{2,1,0:T(8,128)(2,1)S(1)}, u32[]{:S(2)}, u32[]{:S(2)}) collective-permute-start(bf16[1,64,768]{2,1,0:T(8,128)(2,1)S(1)} %bitcast.39), channel_id=1, source_target_pairs={{0,64},{64,0},{1,65},{65,1},{2,66},{66,2},{3,67},{67,3},{4,68},{68... | collective-permute-start | bytes 294920 | tf_op jit(solution)/shard_map/ppermute | solution.py:35
  153.5 3.1 %collective-permute-done.19 = bf16[1,64,768]{2,1,0:T(8,128)(2,1)S(1)} collective-permute-done((bf16[1,64,768]{2,1,0:T(8,128)(2,1)S(1)}, bf16[1,64,768]{2,1,0:T(8,128)(2,1)S(1)}, u32[]{:S(2)}, u32[]{:S(2)}) %collective-permute-start.19) | collective-permute-done | bytes 98336 | tf_op jit(solution)/shard_map/ppermute | solution.py:35
  (64 shorter events, 18.4 us)
Async XLA Ops:
  0.6 14.8 %copy-start.11 = (s32[4]{0:T(128)S(1)}, s32[4]{0:T(128)}, u32[]{:S(2)}) copy-start(s32[4]{0:T(128)} %constant.21.clone) | copy-start | bytes 52
  0.6 8.8 %copy-start.3 = (bf16[1,64,768]{2,1,0:T(8,128)(2,1)S(1)}, bf16[1,64,768]{2,1,0:T(8,128)(2,1)}, u32[]{:S(2)}) copy-start(bf16[1,64,768]{2,1,0:T(8,128)(2,1)} %param.13) | copy-start | bytes 294916
  3.7 16.2 %copy-start.7 = (bf16[384,64]{1,0:T(8,128)(2,1)S(1)}, bf16[384,64]{1,0:T(8,128)(2,1)}, u32[]{:S(2)}) copy-start(bf16[384,64]{1,0:T(8,128)(2,1)} %get-tuple-element.42.table) | copy-start | bytes 147460
  3.7 23.8 %all-to-all-start = ((bf16[16,24,1536]{2,1,0:T(8,128)(2,1)}), bf16[16,24,1536]{2,1,0:T(8,128)(2,1)S(1)}, u32[]{:S(2)}, u32[]{:S(2)}) async-start(bf16[16,24,1536]{2,1,0:T(8,128)(2,1)} %bitcast.48), calls=%async_computation | async-start | bytes 2359296 | tf_op jit(solution)/shard_map/all_to_all | solution.py:413
  9.5 7.3 %collective-permute-start.2 = (bf16[64,768]{1,0:T(8,128)(2,1)S(1)}, bf16[64,768]{1,0:T(8,128)(2,1)S(1)}, u32[]{:S(2)}, u32[]{:S(2)}) collective-permute-start(bf16[64,768]{1,0:T(8,128)(2,1)S(1)} %bitcast.32), channel_id=1, source_target_pairs={{0,2},{1,3},{2,0},{3,1},{4,6},{5,7},{6,4},{7,5},{8,10},{9,11},{10,... | collective-permute-start | bytes 294920 | tf_op jit(solution)/shard_map/ppermute | solution.py:35
  13.4 6.3 %collective-permute-start.1 = (bf16[64,768]{1,0:T(8,128)(2,1)S(1)}, bf16[64,768]{1,0:T(8,128)(2,1)S(1)}, u32[]{:S(2)}, u32[]{:S(2)}) collective-permute-start(bf16[64,768]{1,0:T(8,128)(2,1)S(1)} %bitcast.33), channel_id=1, source_target_pairs={{0,3},{1,0},{2,1},{3,2},{4,7},{5,4},{6,5},{7,6},{8,11},{9,8},{10,9... | collective-permute-start | bytes 294920 | tf_op jit(solution)/shard_map/ppermute | solution.py:35
  14.2 5.8 %collective-permute-start = (bf16[64,768]{1,0:T(8,128)(2,1)S(1)}, bf16[64,768]{1,0:T(8,128)(2,1)S(1)}, u32[]{:S(2)}, u32[]{:S(2)}) collective-permute-start(bf16[64,768]{1,0:T(8,128)(2,1)S(1)} %bitcast.34), channel_id=1, source_target_pairs={{0,1},{1,2},{2,3},{3,0},{4,5},{5,6},{6,7},{7,4},{8,9},{9,10},{10,1... | collective-permute-start | bytes 294920 | tf_op jit(solution)/shard_map/ppermute | solution.py:35
  27.6 44.5 %all-to-all-start.2 = ((bf16[16,24,3072]{2,1,0:T(8,128)(2,1)}), bf16[16,24,3072]{2,1,0:T(8,128)(2,1)S(1)}, u32[]{:S(2)}, u32[]{:S(2)}) async-start(bf16[16,24,3072]{2,1,0:T(8,128)(2,1)} %bitcast.46), calls=%async_computation.2 | async-start | bytes 4718592 | tf_op jit(solution)/shard_map/all_to_all | solution.py:413
  31.4 17.1 %collective-permute-start.4 = (bf16[384,768]{1,0:T(8,128)(2,1)S(1)}, bf16[384,768]{1,0:T(8,128)(2,1)S(1)}, u32[]{:S(2)}, u32[]{:S(2)}) collective-permute-start(bf16[384,768]{1,0:T(8,128)(2,1)S(1)} %get-tuple-element.79.p0), channel_id=1, source_target_pairs={{0,3},{1,0},{2,1},{3,2},{4,7},{5,4},{6,5},{7,6},{8,11},{9,8},{10,9... | collective-permute-start | bytes 1769480 | tf_op jit(solution)/shard_map/ppermute | solution.py:35
  35.5 16.4 %collective-permute-start.3 = (bf16[384,768]{1,0:T(8,128)(2,1)S(1)}, bf16[384,768]{1,0:T(8,128)(2,1)S(1)}, u32[]{:S(2)}, u32[]{:S(2)}) collective-permute-start(bf16[384,768]{1,0:T(8,128)(2,1)S(1)} %get-tuple-element.79.p0), channel_id=1, source_target_pairs={{0,1},{1,2},{2,3},{3,0},{4,5},{5,6},{6,7},{7,4},{8,9},{9,10},{10,1... | collective-permute-start | bytes 1769480 | tf_op jit(solution)/shard_map/ppermute | solution.py:35
  43.6 13.7 %copy-start.2 = (bf16[384,768]{1,0:T(8,128)(2,1)S(1)}, bf16[384,768]{1,0:T(8,128)(2,1)}, u32[]{:S(2)}) copy-start(bf16[384,768]{1,0:T(8,128)(2,1)} %copy-done.1) | copy-start | bytes 1769476
  51.9 11.6 %collective-permute-start.5 = (bf16[192,768]{1,0:T(8,128)(2,1)S(1)}, bf16[192,768]{1,0:T(8,128)(2,1)S(1)}, u32[]{:S(2)}, u32[]{:S(2)}) collective-permute-start(bf16[192,768]{1,0:T(8,128)(2,1)S(1)} %get-tuple-element.45.refs_1_), channel_id=1, source_target_pairs={{0,1},{1,2},{2,3},{3,0},{4,5},{5,6},{6,7},{7,4},{8,9},{9,10},{10,1... | collective-permute-start | bytes 884744 | tf_op jit(solution)/shard_map/ppermute | solution.py:35
  52.0 11.5 %collective-permute-start.6 = (bf16[192,768]{1,0:T(8,128)(2,1)S(1)}, bf16[192,768]{1,0:T(8,128)(2,1)S(1)}, u32[]{:S(2)}, u32[]{:S(2)}) collective-permute-start(bf16[192,768]{1,0:T(8,128)(2,1)S(1)} %get-tuple-element.46.refs_2_), channel_id=1, source_target_pairs={{0,3},{1,0},{2,1},{3,2},{4,7},{5,4},{6,5},{7,6},{8,11},{9,8},{10,9... | collective-permute-start | bytes 884744 | tf_op jit(solution)/shard_map/ppermute | solution.py:35
  55.2 22.5 %collective-permute-start.12 = (bf16[384,768]{1,0:T(8,128)(2,1)S(1)}, bf16[384,768]{1,0:T(8,128)(2,1)S(1)}, u32[]{:S(2)}, u32[]{:S(2)}) collective-permute-start(bf16[384,768]{1,0:T(8,128)(2,1)S(1)} %shard_map.130.refs_0_), channel_id=1, source_target_pairs={{0,3},{1,0},{2,1},{3,2},{4,7},{5,4},{6,5},{7,6},{8,11},{9,8},{10,9... | collective-permute-start | bytes 1769480 | tf_op jit(solution)/shard_map/ppermute | solution.py:35
  55.2 22.4 %collective-permute-start.11 = (bf16[384,768]{1,0:T(8,128)(2,1)S(1)}, bf16[384,768]{1,0:T(8,128)(2,1)}, u32[]{:S(2)}, u32[]{:S(2)}) collective-permute-start(bf16[384,768]{1,0:T(8,128)(2,1)S(1)} %shard_map.130.refs_0_), channel_id=1, source_target_pairs={{0,1},{1,2},{2,3},{3,0},{4,5},{5,6},{6,7},{7,4},{8,9},{9,10},{10,1... | collective-permute-start | bytes 1769480 | tf_op jit(solution)/shard_map/ppermute | solution.py:35
  72.1 45.2 %all-to-all-start.1 = ((bf16[16,24,3072]{2,1,0:T(8,128)(2,1)}), bf16[16,24,3072]{2,1,0:T(8,128)(2,1)}, u32[]{:S(2)}, u32[]{:S(2)}) async-start(bf16[16,24,3072]{2,1,0:T(8,128)(2,1)} %bitcast.30), calls=%async_computation.1 | async-start | bytes 4718592 | tf_op jit(solution)/shard_map/all_to_all | solution.py:413
  80.5 13.4 %collective-permute-start.13 = (bf16[192,768]{1,0:T(8,128)(2,1)S(1)}, bf16[192,768]{1,0:T(8,128)(2,1)S(1)}, u32[]{:S(2)}, u32[]{:S(2)}) collective-permute-start(bf16[192,768]{1,0:T(8,128)(2,1)S(1)} %get-tuple-element.59), channel_id=1, source_target_pairs={{0,1},{1,2},{2,3},{3,0},{4,5},{5,6},{6,7},{7,4},{8,9},{9,10},{10,1... | collective-permute-start | bytes 884744 | tf_op jit(solution)/shard_map/ppermute | solution.py:35
  80.6 13.3 %collective-permute-start.14 = (bf16[192,768]{1,0:T(8,128)(2,1)S(1)}, bf16[192,768]{1,0:T(8,128)(2,1)S(1)}, u32[]{:S(2)}, u32[]{:S(2)}) collective-permute-start(bf16[192,768]{1,0:T(8,128)(2,1)S(1)} %get-tuple-element.60), channel_id=1, source_target_pairs={{0,3},{1,0},{2,1},{3,2},{4,7},{5,4},{6,5},{7,6},{8,11},{9,8},{10,9... | collective-permute-start | bytes 884744 | tf_op jit(solution)/shard_map/ppermute | solution.py:35
  103.2 10.2 %collective-permute-start.15 = (bf16[192,768]{1,0:T(8,128)(2,1)S(1)}, bf16[192,768]{1,0:T(8,128)(2,1)S(1)}, u32[]{:S(2)}, u32[]{:S(2)}) collective-permute-start(bf16[192,768]{1,0:T(8,128)(2,1)S(1)} %get-tuple-element.73), channel_id=1, source_target_pairs={{0,1},{1,2},{2,3},{3,0},{4,5},{5,6},{6,7},{7,4},{8,9},{9,10},{10,1... | collective-permute-start | bytes 884744 | tf_op jit(solution)/shard_map/ppermute | solution.py:35
  103.3 14.0 %copy-start.5 = (bf16[1,64,768]{2,1,0:T(8,128)(2,1)S(1)}, bf16[1,64,768]{2,1,0:T(8,128)(2,1)}, u32[]{:S(2)}) copy-start(bf16[1,64,768]{2,1,0:T(8,128)(2,1)} %param.11) | copy-start | bytes 294916
  103.3 14.0 %copy-start.6 = (bf16[384,128]{1,0:T(8,128)(2,1)S(1)}, bf16[384,128]{1,0:T(8,128)(2,1)}, u32[]{:S(2)}) copy-start(bf16[384,128]{1,0:T(8,128)(2,1)} %get-tuple-element.40.table) | copy-start | bytes 294916
  103.3 10.1 %collective-permute-start.16 = (bf16[192,768]{1,0:T(8,128)(2,1)S(1)}, bf16[192,768]{1,0:T(8,128)(2,1)S(1)}, u32[]{:S(2)}, u32[]{:S(2)}) collective-permute-start(bf16[192,768]{1,0:T(8,128)(2,1)S(1)} %get-tuple-element.74), channel_id=1, source_target_pairs={{0,3},{1,0},{2,1},{3,2},{4,7},{5,4},{6,5},{7,6},{8,11},{9,8},{10,9... | collective-permute-start | bytes 884744 | tf_op jit(solution)/shard_map/ppermute | solution.py:35
  114.3 14.8 %collective-permute-start.18 = (bf16[384,768]{1,0:T(8,128)(2,1)}, bf16[384,768]{1,0:T(8,128)(2,1)S(1)}, u32[]{:S(2)}, u32[]{:S(2)}) collective-permute-start(bf16[384,768]{1,0:T(8,128)(2,1)} %get-tuple-element.76), channel_id=1, source_target_pairs={{0,3},{1,0},{2,1},{3,2},{4,7},{5,4},{6,5},{7,6},{8,11},{9,8},{10,9... | collective-permute-start | bytes 1769480 | tf_op jit(solution)/shard_map/ppermute | solution.py:35
  117.3 15.0 %collective-permute-start.17 = (bf16[384,768]{1,0:T(8,128)(2,1)S(1)}, bf16[384,768]{1,0:T(8,128)(2,1)S(1)}, u32[]{:S(2)}, u32[]{:S(2)}) collective-permute-start(bf16[384,768]{1,0:T(8,128)(2,1)S(1)} %get-tuple-element.75), channel_id=1, source_target_pairs={{0,1},{1,2},{2,3},{3,0},{4,5},{5,6},{6,7},{7,4},{8,9},{9,10},{10,1... | collective-permute-start | bytes 1769480 | tf_op jit(solution)/shard_map/ppermute | solution.py:35
  132.3 17.9 %copy-start.4 = (bf16[1,64,768]{2,1,0:T(8,128)(2,1)S(1)}, bf16[1,64,768]{2,1,0:T(8,128)(2,1)}, u32[]{:S(2)}) copy-start(bf16[1,64,768]{2,1,0:T(8,128)(2,1)} %param.13) | copy-start | bytes 294916
  132.3 17.9 %copy-start.8 = (bf16[384,128]{1,0:T(8,128)(2,1)S(1)}, bf16[384,128]{1,0:T(8,128)(2,1)}, u32[]{:S(2)}) copy-start(bf16[384,128]{1,0:T(8,128)(2,1)} %get-tuple-element.56.table) | copy-start | bytes 294916
  133.3 16.9 %all-to-all-start.3 = ((bf16[16,24,768]{2,1,0:T(8,128)(2,1)}), bf16[16,24,768]{2,1,0:T(8,128)(2,1)S(1)}, u32[]{:S(2)}, u32[]{:S(2)}) async-start(bf16[16,24,768]{2,1,0:T(8,128)(2,1)} %bitcast.21), calls=%async_computation.3 | async-start | bytes 1179648 | tf_op jit(solution)/shard_map/all_to_all | solution.py:413
  138.5 5.2 %collective-permute-start.7 = (bf16[64,768]{1,0:T(8,128)(2,1)S(1)}, bf16[64,768]{1,0:T(8,128)(2,1)S(1)}, u32[]{:S(2)}, u32[]{:S(2)}) collective-permute-start(bf16[64,768]{1,0:T(8,128)(2,1)S(1)} %copy-done.10), channel_id=1, source_target_pairs={{0,3},{1,0},{2,1},{3,2},{4,7},{5,4},{6,5},{7,6},{8,11},{9,8},{10,9... | collective-permute-start | bytes 294920 | tf_op jit(solution)/shard_map/ppermute | solution.py:35
  139.1 8.2 %collective-permute-start.8 = (bf16[64,768]{1,0:T(8,128)(2,1)S(1)}, bf16[64,768]{1,0:T(8,128)(2,1)S(1)}, u32[]{:S(2)}, u32[]{:S(2)}) collective-permute-start(bf16[64,768]{1,0:T(8,128)(2,1)S(1)} %get-tuple-element.54), channel_id=1, source_target_pairs={{0,1},{1,2},{2,3},{3,0},{4,5},{5,6},{6,7},{7,4},{8,9},{9,10},{10,1... | collective-permute-start | bytes 294920 | tf_op jit(solution)/shard_map/ppermute | solution.py:35
  140.6 6.6 %collective-permute-start.9 = (bf16[64,768]{1,0:T(8,128)(2,1)S(1)}, bf16[64,768]{1,0:T(8,128)(2,1)S(1)}, u32[]{:S(2)}, u32[]{:S(2)}) collective-permute-start(bf16[64,768]{1,0:T(8,128)(2,1)S(1)} %get-tuple-element.55), channel_id=1, source_target_pairs={{0,2},{1,3},{2,0},{3,1},{4,6},{5,7},{6,4},{7,5},{8,10},{9,11},{10,... | collective-permute-start | bytes 294920 | tf_op jit(solution)/shard_map/ppermute | solution.py:35
  147.3 6.2 %collective-permute-start.10 = (bf16[1,64,768]{2,1,0:T(8,128)(2,1)S(1)}, bf16[1,64,768]{2,1,0:T(8,128)(2,1)S(1)}, u32[]{:S(2)}, u32[]{:S(2)}) collective-permute-start(bf16[1,64,768]{2,1,0:T(8,128)(2,1)S(1)} %fusion), channel_id=1, source_target_pairs={{0,64},{64,0},{1,65},{65,1},{2,66},{66,2},{3,67},{67,3},{4,68},{68... | collective-permute-start | bytes 294920 | tf_op jit(solution)/shard_map/ppermute | solution.py:35
  150.4 6.2 %collective-permute-start.19 = (bf16[1,64,768]{2,1,0:T(8,128)(2,1)S(1)}, bf16[1,64,768]{2,1,0:T(8,128)(2,1)S(1)}, u32[]{:S(2)}, u32[]{:S(2)}) collective-permute-start(bf16[1,64,768]{2,1,0:T(8,128)(2,1)S(1)} %bitcast.39), channel_id=1, source_target_pairs={{0,64},{64,0},{1,65},{65,1},{2,66},{66,2},{3,67},{67,3},{4,68},{68... | collective-permute-start | bytes 294920 | tf_op jit(solution)/shard_map/ppermute | solution.py:35
  (4 other events, 16.5 us)

commit v3 on v2

--- a/solution.py
+++ b/solution.py
@@ -14,7 +14,7 @@
 ANY = pl.BlockSpec(memory_space=pl.ANY)
 
 
-def params(mebibytes=12):
+def params(mebibytes=8):
     return pltpu.CompilerParams(vmem_limit_bytes=mebibytes * 1024 * 1024)
 
 
@@ -189,14 +189,40 @@
     return sums
 
 
-def begin_kernel(order, p0, p1, p2, wg, wu, sum_a, sum_b):
+def begin_kernel(first_entry, count, order, *refs):
+    pieces, (wg, wu), earlier, (sum_a, sum_b, mark) = refs[:count], refs[count : count + 2], refs[count + 2 : -3], refs[-3:]
+    mark[...] = jnp.zeros_like(mark)
     for start, size in tiles(wg.shape[0]):
         part = slice(start, start + size)
-        sum_a[:, part], sum_b[:, part] = piece_sums(order, 0, (p0, p1, p2), wg, wu, part)
-
-
-def begin_loading_kernel(order, p0, p1, p2, wg, wu, wd, sum_a, sum_b, near_g, near_u, near_d, semaphores):
+        a, b = piece_sums(order, first_entry, pieces, wg, wu, part)
+        if earlier:
+            a += earlier[0][:, part]
+            b += earlier[1][:, part]
+        sum_a[:, part] = a
+        sum_b[:, part] = b
+
+
+def begin(order, first_entry, pieces, wg, wu, earlier):
+    rows, quarter = pieces[0].shape
+    units = wg.shape[0]
+    count = len(pieces)
+    return pl.pallas_call(
+        functools.partial(begin_kernel, first_entry, count),
+        in_specs=[SMEM] + [VMEM] * (count + 2 + len(earlier)),
+        out_specs=[VMEM] * 3,
+        out_shape=[pltpu.VMEM((rows, units), F32)] * 2 + [jax.ShapeDtypeStruct((8, 128), F32)],
+        compiler_params=params(),
+        cost_estimate=pl.CostEstimate(
+            flops=4 * count * rows * quarter * units, bytes_accessed=4 * count * units * quarter, transcendentals=0
+        ),
+    )(order, *pieces, *[near(array) for array in (wg, wu, *earlier)])
+
+
+def begin_loading_kernel(
+    order, p0, p1, p2, wg, wu, wd, sum_a, sum_b, near_g, near_u, near_d, rows, row_waits, semaphores
+):
     spans = load_spans(wg.shape[0])
+    row_copies = [pltpu.make_async_copy(piece, rows.at[n], row_waits.at[n]) for n, piece in enumerate((p0, p1, p2))]
     copies = []
     for p, (start, size) in enumerate(spans):
         span = pl.ds(start, size)
@@ -207,8 +233,10 @@
             ]
         )
     copies.append([pltpu.make_async_copy(wd, near_d, semaphores.at[len(spans), 0])])
-    for copy in copies[0] + copies[1]:
+    for copy in row_copies + copies[0] + copies[1]:
         copy.start()
+    for copy in row_copies:
+        copy.wait()
     for p, (begin, length) in enumerate(spans):
         for copy in copies[p]:
             copy.wait()
@@ -217,89 +245,131 @@
                 copy.start()
         for start, size in tiles(length):
             part = slice(begin + start, begin + start + size)
-            sum_a[:, part], sum_b[:, part] = piece_sums(order, 0, (p0, p1, p2), near_g, near_u, part)
+            sum_a[:, part], sum_b[:, part] = piece_sums(
+                order, 0, [rows.at[n] for n in range(3)], near_g, near_u, part
+            )
     copies[-1][0].wait()
 
 
-def begin(order, pieces, weights):
-    loading = len(weights) == 3
+def begin_loading(order, pieces, weights):
     rows, quarter = pieces[0].shape
     units = weights[0].shape[0]
     return pl.pallas_call(
-        begin_loading_kernel if loading else begin_kernel,
-        in_specs=[SMEM] + [VMEM] * 3 + [ANY if loading else VMEM] * len(weights),
-        out_specs=[VMEM] * (5 if loading else 2),
-        out_shape=[pltpu.VMEM((rows, units), F32)] * 2
-        + ([pltpu.VMEM(w.shape, w.dtype) for w in weights] if loading else []),
-        scratch_shapes=[pltpu.SemaphoreType.DMA((len(load_spans(units)) + 1, 2))] if loading else [],
+        begin_loading_kernel,
+        in_specs=[SMEM] + [ANY] * 6,
+        out_specs=[VMEM] * 5,
+        out_shape=[pltpu.VMEM((rows, units), F32)] * 2 + [pltpu.VMEM(w.shape, w.dtype) for w in weights],
+        scratch_shapes=[
+            pltpu.VMEM((3, rows, quarter), BF16),
+            pltpu.SemaphoreType.DMA((3,)),
+            pltpu.SemaphoreType.DMA((len(load_spans(units)) + 1, 2)),
+        ],
         compiler_params=params(),
         cost_estimate=pl.CostEstimate(
             flops=12 * rows * quarter * units, bytes_accessed=12 * units * quarter, transcendentals=0
         ),
-    )(order, *pieces, *[(far if loading else near)(w) for w in weights])
-
-
-def finish_kernel(forward, order, top, bottom, sum_a, sum_b, wg, wu, *outs):
-    rows = outs[-1]
+    )(order, *pieces, *[far(w) for w in weights])
+
+
+def finish_kernel(order, top, bottom, sum_a, sum_b, wg, wu, hidden, opposite):
     half = top.shape[0]
-    rows[:half] = top[...]
-    rows[half:] = bottom[...]
+    opposite[:half] = top[...]
+    opposite[half:] = bottom[...]
     for start, size in tiles(wg.shape[0]):
         part = slice(start, start + size)
-        a, b = piece_sums(order, 3, (rows,), wg, wu, part)
+        a, b = piece_sums(order, 3, (opposite,), wg, wu, part)
+        a += sum_a[:, part]
+        b += sum_b[:, part]
+        hidden[:, part] = (a * jax.nn.sigmoid(a) * b).astype(BF16)
+
+
+def finish(order, halves, sums, wg, wu):
+    rows, units = sums[0].shape
+    quarter = halves[0].shape[1]
+    return pl.pallas_call(
+        finish_kernel,
+        in_specs=[SMEM] + [VMEM] * 6,
+        out_specs=VMEM,
+        out_shape=pltpu.VMEM((rows, units), BF16),
+        scratch_shapes=[pltpu.VMEM((rows, quarter), BF16)],
+        compiler_params=params(),
+        cost_estimate=pl.CostEstimate(
+            flops=4 * rows * quarter * units, bytes_accessed=4 * units * quarter, transcendentals=rows * units
+        ),
+    )(order, *halves, *[near(array) for array in (*sums, wg, wu)])
+
+
+def load_spans(units):
+    cuts = [0, min(256, units), min(512, units), min(896, units), units]
+    return [(low, high - low) for low, high in zip(cuts, cuts[1:]) if high > low]
+
+
+def middle_kernel(order, top, bottom, sum_a, sum_b, c, wg, wu, wd, da, db, result_top, result_bottom, opposite):
+    half, quarter = top.shape
+    opposite[:half] = top[...]
+    opposite[half:] = bottom[...]
+    for start, size in tiles(wg.shape[0]):
+        part = slice(start, start + size)
+        a, b = piece_sums(order, 3, (opposite,), wg, wu, part)
         a += sum_a[:, part]
         b += sum_b[:, part]
         q = jax.nn.sigmoid(a)
-        if forward:
-            outs[0][:, part] = (a * q * b).astype(BF16)
-        else:
-            outs[0][:, part] = b * q * (1.0 + a * (1.0 - q))
-            outs[1][:, part] = a * q
-
-
-def finish(forward, order, halves, sums, wg, wu):
+        dh = contract_last(c[...], wd[part, :])
+        da[:, part] = (dh * (b * q * (1.0 + a * (1.0 - q)))).astype(BF16)
+        db[:, part] = (dh * (a * q)).astype(BF16)
+    slots = columns(order[3], quarter)
+    result = jnp.dot(da[...], wg[:, slots], preferred_element_type=F32)
+    result += jnp.dot(db[...], wu[:, slots], preferred_element_type=F32)
+    result_top[...] = result[:half].astype(BF16)
+    result_bottom[...] = result[half:].astype(BF16)
+
+
+def middle(order, halves, sums, c, weights):
     rows, units = sums[0].shape
-    quarter = halves[0].shape[1]
-    outs = [pltpu.VMEM((rows, units), BF16)] if forward else [pltpu.VMEM((rows, units), F32)] * 2
-    return pl.pallas_call(
-        functools.partial(finish_kernel, forward),
-        in_specs=[SMEM] + [VMEM] * 6,
-        out_specs=[VMEM] * len(outs),
-        out_shape=outs,
+    half, quarter = halves[0].shape
+    result = jax.ShapeDtypeStruct((half, quarter), BF16)
+    return pl.pallas_call(
+        middle_kernel,
+        in_specs=[SMEM] + [VMEM] * 8,
+        out_specs=[VMEM] * 4,
+        out_shape=[pltpu.VMEM((rows, units), BF16)] * 2 + [result] * 2,
         scratch_shapes=[pltpu.VMEM((rows, quarter), BF16)],
         compiler_params=params(),
         cost_estimate=pl.CostEstimate(
-            flops=4 * rows * quarter * units, bytes_accessed=4 * units * quarter, transcendentals=rows * units
-        ),
-    )(order, *halves, *[near(array) for array in (*sums, wg, wu)])
-
-
-def load_spans(units):
-    cuts = [0, min(256, units), min(768, units), units]
-    return [(low, high - low) for low, high in zip(cuts, cuts[1:]) if high > low]
-
-
-def grads_kernel(c, for_gate, for_up, wd, da, db):
-    for start, size in tiles(wd.shape[0]):
-        part = slice(start, start + size)
-        dh = contract_last(c[...], wd[part, :])
-        da[:, part] = (dh * for_gate[:, part]).astype(BF16)
-        db[:, part] = (dh * for_up[:, part]).astype(BF16)
-
-
-def hidden_grads(c, for_gate, for_up, wd):
-    rows, features = c.shape
-    units = wd.shape[0]
-    return pl.pallas_call(
-        grads_kernel,
-        in_specs=[VMEM] * 4,
-        out_specs=[VMEM] * 2,
-        out_shape=[pltpu.VMEM((rows, units), BF16)] * 2,
-        compiler_params=params(),
-        cost_estimate=pl.CostEstimate(
-            flops=2 * rows * features * units, bytes_accessed=2 * units * features, transcendentals=0
-        ),
-    )(c, near(for_gate), near(for_up), near(wd))
+            flops=16 * rows * quarter * units, bytes_accessed=16 * units * quarter, transcendentals=rows * units
+        ),
+    )(order, *halves, *[near(array) for array in sums], c, *[near(array) for array in weights])
+
+
+def whole_kernel(order, act, weight, out, mark, results, semaphores):
+    quarter = results.shape[-1]
+    copies = []
+    for n in range(4):
+        slots = slice(n * quarter, (n + 1) * quarter)
+        results[n] = jnp.dot(act[...], weight[:, slots], preferred_element_type=F32).astype(BF16)
+        copies.append(
+            pltpu.make_async_copy(results.at[n], out.at[:, pl.ds(n * quarter, quarter)], semaphores.at[n])
+        )
+        copies[n].start()
+    mark[...] = jnp.zeros_like(mark)
+    for copy in copies:
+        copy.wait()
+
+
+def whole_result(order, act, weight):
+    rows, units = act.shape
+    features = weight.shape[1]
+    return pl.pallas_call(
+        whole_kernel,
+        in_specs=[SMEM] + [VMEM] * 2,
+        out_specs=[ANY, VMEM],
+        out_shape=[pltpu.HBM((rows, features), BF16), jax.ShapeDtypeStruct((8, 128), F32)],
+        scratch_shapes=[pltpu.VMEM((4, rows, features // 4), BF16), pltpu.SemaphoreType.DMA((4,))],
+        compiler_params=params(),
+        cost_estimate=pl.CostEstimate(
+            flops=2 * rows * units * features, bytes_accessed=2 * units * features, transcendentals=0
+        ),
+    )(order, near(act), near(weight))
 
 
 def down_kernel(which, pairs, order, *refs):
@@ -310,14 +380,7 @@
         total = functools.reduce(
             jnp.add, [jnp.dot(a[...], w[:, slots], preferred_element_type=F32) for a, w in zip(acts, weights)]
         )
-        if len(which) == 4:
-            outs[0][:, slots] = total.astype(outs[0].dtype)
-        elif len(which) == 1:
-            half = outs[0].shape[0]
-            outs[0][...] = total[:half].astype(outs[0].dtype)
-            outs[1][...] = total[half:].astype(outs[1].dtype)
-        else:
-            outs[n][...] = total.astype(outs[n].dtype)
+        outs[n][...] = total.astype(outs[n].dtype)
 
 
 def down_projections(order, which, acts, weights, outs):
@@ -350,12 +413,10 @@
     out[...] = (own[...] + from_last[...].astype(F32) + from_next[...].astype(F32)).astype(BF16)
 
 
-def summed_over_tensor(order, acts, weights, earlier):
+def summed_over_tensor(order, top, bottom, acts, weights, earlier):
     rows = acts[0].shape[0]
     quarter = weights[0].shape[1] // 4
     whole = jax.ShapeDtypeStruct((rows, quarter), BF16)
-    half = jax.ShapeDtypeStruct((rows // 2, quarter), BF16)
-    top, bottom = down_projections(order, (3,), acts, weights, [half, half])
     up = shift(top, "tensor", 1)
     down = shift(bottom, "tensor", -1)
     kept = [pltpu.VMEM(whole.shape, BF16)] * 2 + [pltpu.VMEM(whole.shape, F32)]
@@ -434,23 +495,22 @@
     rows_c = exchange(after(send_c, f0, x0))
     f_last, f_next = shift(f0, "tensor", 1), shift(f0, "tensor", -1)
     near_g, near_u, near_d, loaded = load_weights((wg, wu, wd))
+    *sums, _ = begin(order, 0, (f0,), near_g, near_u, ())
     f_top, f_bottom = halves(f_last, f_next, loaded)
     f_opposite = shift(f_top, "tensor", 1), shift(f_bottom, "tensor", -1)
-    x0 = held(x0, f_top, f_bottom)
+    *sums, begun = begin(order, 1, (f_last, f_next), near_g, near_u, sums)
+    x0 = held(x0, f_top, f_bottom, begun)
     x_next, x_last = shift(x0, "tensor", -1), shift(x0, "tensor", 1)
     x_top, x_bottom = halves(x_last, x_next)
     x_opposite = shift(x_top, "tensor", 1), shift(x_bottom, "tensor", -1)
 
-    sums = begin(order, (f0, f_last, f_next), (near_g, near_u))
-    (hidden,) = finish(True, order, f_opposite, sums, near_g, near_u)
-    whole = pltpu.HBM((hidden.shape[0], wd.shape[1]), BF16)
-    (part_f,) = down_projections(order, (0, 1, 2, 3), (hidden,), (near_d,), [whole])
+    hidden = finish(order, f_opposite, sums, near_g, near_u)
+    part_f, sent = whole_result(order, hidden, near_d)
     back_f = exchange(part_f)
-    *sums, near_g, near_u, near_d = begin(order, (held(x0, part_f), x_last, x_next), (wg, wu, wd))
-    for_gate, for_up = finish(False, order, x_opposite, sums, near_g, near_u)
-    da, db = hidden_grads(rows_c, for_gate, for_up, near_d)
+    *sums, near_g, near_u, near_d = begin_loading(order, (held(x0, sent), x_last, x_next), (wg, wu, wd))
+    da, db, top, bottom = middle(order, x_opposite, sums, rows_c, (near_g, near_u, near_d))
     mixed_f = mixed_over_tensor(order, mix_f, back_f, f)
-    share_b = summed_over_tensor(order, (da, db), (near_g, near_u), mixed_f)
+    share_b = summed_over_tensor(order, top, bottom, (da, db), (near_g, near_u), mixed_f)
     out_f = total_over_tensor(*mixed_f)
     out_b = mixed(mix_b, exchange(share_b), c)
     return shift(out_f[None], "pipe", 1), shift(out_b[None], "pipe", -1)

time: 159 us -> 153 us (0.962)
  waiting for transfers between devices: 40.4 us -> 34.7 us
  local copies, waits for them, and re-layouts: 3.73 us -> 1.4 us
    pallas_call x5 -> x6, Pallas kernels: 25.7 us -> 35 us  [the longest x1 9.94 us: begin_loading(): pl.pallas_call(begin_loading_kernel, in_specs=[SMEM] + [ANY] * 6, out_spe...]
    pallas_call x3 -> x1, Pallas kernels: 14.8 us -> 6.27 us  [down_projections(): pl.pallas_call(functools.partial(down_kernel, which, pairs), in_specs=[SM...]
    ppermute x20, waiting for transfers between devices: 35.5 us -> 30.1 us  [shift(): lax.ppermute(shard, axis, [(i, (i + by) % length) for i in range(length)])]
    unnamed x26 -> x18, local copies, waits for them, and re-layouts: 3.65 us -> 1.32 us
  transfers between devices with their start and end apart: 24 -> 24, of which waited for: 14 -> 13; matrix products, arithmetic and copies ran while one was open for 0% -> 0% of each run, Pallas kernels for 35% -> 37%
where the time goes in v3:
time: 153 us; the launch traced here: 152 us
  Pallas kernels  60.9 us (40%)
  starting transfers between devices  54.3 us (35%)
  waiting for transfers between devices  34.7 us (23%)
    ppermute x20, starting transfers between devices, shift(): lax.ppermute(shard, axis, [(i, (i + by) % length) for i in range(length)])  34.1 us
    ppermute x20, waiting for transfers between devices, shift(): lax.ppermute(shard, axis, [(i, (i + by) % length) for i in range(length)])  30.1 us
    all_to_all x4, starting transfers between devices, exchange(): lax.all_to_all(rows, 'expert', split_axis=0, concat_axis=0, tiled=True)  20.3 us
    pallas_call x1, Pallas kernels, begin_loading(): pl.pallas_call(begin_loading_kernel, in_specs=[SMEM] + [ANY] * 6, out_spe...  9.94 us
    pallas_call x1, Pallas kernels, middle(): pl.pallas_call(middle_kernel, in_specs=[SMEM] + [VMEM] * 8, out_specs=[VM...  9.56 us
    pallas_call x1, Pallas kernels, load_weights(): pl.pallas_call(load_kernel, in_specs=[ANY] * len(weights), out_specs=[VME...  8.07 us
    pallas_call x2, Pallas kernels, begin(): pl.pallas_call(functools.partial(begin_kernel, first_entry, count), in_sp...  7.53 us
    pallas_call x1, Pallas kernels, down_projections(): pl.pallas_call(functools.partial(down_kernel, which, pairs), in_specs=[SM...  6.27 us
  transfers between devices with their start and end apart: 24, of which 13 were waited for; matrix products, arithmetic and copies ran while one was open for 0% of the time, Pallas kernels for 37%

profile of v3, /device:TPU:0, one launch (start us, length us, event | category | flops | bytes accessed | tf_op | source)
XLA Modules:
  0.0 152.2 jit_solution(17238320259244439628)
XLA Ops:
  0.7 3.1 %shard_map.122 = (bf16[384,1536]{1,0:T(8,128)(2,1)}, bf16[384,64]{1,0:T(8,128)(2,1)}, bf16[384,128]{1,0:T(8,128)(2,1)}, bf16[384,128]{1,0:T(8,128)(2,1)}) custom-call(s32[4,64]{1,0:T(4,128)} %bitcast.50, s32[4,64]{1,0:T(4,128)} %bitcast.51, s32[4,64]{1,0:T(4,128)} %bitcast.52, s32[4,64]{1,0:T(4,128)} %bitcast.53, bf16[64,768]{1,0:T(8,128)(2,1)} %bitcast.36, ...), custom_call_target="tpu_custom_call" | custom-call | tf_op jit(solution)/shard_map/pallas_call | solution.py:81
  3.7 5.7 %all-to-all-start = ((bf16[16,24,1536]{2,1,0:T(8,128)(2,1)}), bf16[16,24,1536]{2,1,0:T(8,128)(2,1)S(1)}, u32[]{:S(2)}, u32[]{:S(2)}) async-start(bf16[16,24,1536]{2,1,0:T(8,128)(2,1)} %bitcast.48), calls=%async_computation | async-start | bytes 2359296 | tf_op jit(solution)/shard_map/all_to_all | solution.py:474
  9.5 2.0 %collective-permute-start = (bf16[64,768]{1,0:T(8,128)(2,1)S(1)}, bf16[64,768]{1,0:T(8,128)(2,1)S(1)}, u32[]{:S(2)}, u32[]{:S(2)}) collective-permute-start(bf16[64,768]{1,0:T(8,128)(2,1)S(1)} %bitcast.31), channel_id=1, source_target_pairs={{0,1},{1,2},{2,3},{3,0},{4,5},{5,6},{6,7},{7,4},{8,9},{9,10},{10,1... | collective-permute-start | bytes 294920 | tf_op jit(solution)/shard_map/ppermute | solution.py:35
  11.5 2.2 %collective-permute-start.1 = (bf16[64,768]{1,0:T(8,128)(2,1)S(1)}, bf16[64,768]{1,0:T(8,128)(2,1)S(1)}, u32[]{:S(2)}, u32[]{:S(2)}) collective-permute-start(bf16[64,768]{1,0:T(8,128)(2,1)S(1)} %bitcast.32), channel_id=1, source_target_pairs={{0,3},{1,0},{2,1},{3,2},{4,7},{5,4},{6,5},{7,6},{8,11},{9,8},{10,9... | collective-permute-start | bytes 294920 | tf_op jit(solution)/shard_map/ppermute | solution.py:35
  20.3 2.8 %shard_map.123 = bf16[384,3072]{1,0:T(8,128)(2,1)} custom-call(s32[4]{0:T(128)S(1)} %and_select_fusion.order, bf16[384,64]{1,0:T(8,128)(2,1)S(1)} %copy-done.4, bf16[64,768]{1,0:T(8,128)(2,1)S(1)} %bitcast.34, bf16[64,768]{1,0:T(8,128)(2,1)S(1)} %collective-permute-done.p1, bf16[64,768]{1,0:T(8,128)(2,1)S(1)} %collective-permute-done.1.p2, ...), custom_call_target="tpu_custom_call" | custom-call | tf_op jit(solution)/shard_map/pallas_call | solution.py:103
  23.0 4.5 %all-to-all-done = bf16[16,24,1536]{2,1,0:T(8,128)(2,1)S(1)} async-done(((bf16[16,24,1536]{2,1,0:T(8,128)(2,1)}), bf16[16,24,1536]{2,1,0:T(8,128)(2,1)S(1)}, u32[]{:S(2)}, u32[]{:S(2)}) %all-to-all-start) | async-done | bytes 1179680 | tf_op jit(solution)/shard_map/all_to_all | solution.py:474
  27.6 3.7 %all-to-all-start.2 = ((bf16[16,24,3072]{2,1,0:T(8,128)(2,1)}), bf16[16,24,3072]{2,1,0:T(8,128)(2,1)S(1)}, u32[]{:S(2)}, u32[]{:S(2)}) async-start(bf16[16,24,3072]{2,1,0:T(8,128)(2,1)} %bitcast.45), calls=%async_computation.2 | async-start | bytes 4718592 | tf_op jit(solution)/shard_map/all_to_all | solution.py:474
  31.4 2.0 %collective-permute-start.3 = (bf16[384,768]{1,0:T(8,128)(2,1)S(1)}, bf16[384,768]{1,0:T(8,128)(2,1)S(1)}, u32[]{:S(2)}, u32[]{:S(2)}) collective-permute-start(bf16[384,768]{1,0:T(8,128)(2,1)S(1)} %get-tuple-element.85.refs_0_), channel_id=1, source_target_pairs={{0,1},{1,2},{2,3},{3,0},{4,5},{5,6},{6,7},{7,4},{8,9},{9,10},{10,1... | collective-permute-start | bytes 1769480 | tf_op jit(solution)/shard_map/ppermute | solution.py:35
  33.3 2.2 %collective-permute-start.4 = (bf16[384,768]{1,0:T(8,128)(2,1)S(1)}, bf16[384,768]{1,0:T(8,128)(2,1)S(1)}, u32[]{:S(2)}, u32[]{:S(2)}) collective-permute-start(bf16[384,768]{1,0:T(8,128)(2,1)S(1)} %get-tuple-element.85.refs_0_), channel_id=1, source_target_pairs={{0,3},{1,0},{2,1},{3,2},{4,7},{5,4},{6,5},{7,6},{8,11},{9,8},{10,9... | collective-permute-start | bytes 1769480 | tf_op jit(solution)/shard_map/ppermute | solution.py:35
  35.5 8.1 %shard_map.124 = (bf16[1344,3072]{1,0:T(8,128)(2,1)S(1)}, bf16[1344,3072]{1,0:T(8,128)(2,1)S(1)}, bf16[1344,3072]{1,0:T(8,128)(2,1)S(1)}, f32[8,128]{1,0:T(8,128)S(1)}) custom-call(bf16[1344,3072]{1,0:T(8,128)(2,1)} %bitcast.39, bf16[1344,3072]{1,0:T(8,128)(2,1)} %bitcast.41, bf16[1344,3072]{1,0:T(8,128)(2,1)} %bitcast.43), custom_call_target="tpu_custom_call" | custom-call | bytes 24772608 | tf_op jit(solution)/shard_map/pallas_call | solution.py:132
  43.6 3.1 %shard_map.126 = (f32[384,1344]{1,0:T(8,128)S(1)}, f32[384,1344]{1,0:T(8,128)S(1)}, f32[8,128]{1,0:T(8,128)}) custom-call(s32[4]{0:T(128)S(1)} %and_select_fusion.order, bf16[384,768]{1,0:T(8,128)(2,1)S(1)} %get-tuple-element.85.refs_0_, bf16[1344,3072]{1,0:T(8,128)(2,1)S(1)} %get-tuple-element.50.refs_1_.refs_2_.wg, ...), custom_call_target="tpu_custom_call" | custom-call | flops 1585446912 | bytes 4128768 | tf_op jit(solution)/shard_map/pallas_call | solution.py:209
  46.7 2.5 %collective-permute-done.3.from_last.refs_0_ = bf16[384,768]{1,0:T(8,128)(2,1)S(1)} collective-permute-done((bf16[384,768]{1,0:T(8,128)(2,1)S(1)}, bf16[384,768]{1,0:T(8,128)(2,1)S(1)}, u32[]{:S(2)}, u32[]{:S(2)}) %collective-permute-start.3) | collective-permute-done | bytes 589856 | tf_op jit(solution)/shard_map/ppermute | solution.py:35
  52.5 4.5 %shard_map.127 = (f32[384,1344]{1,0:T(8,128)S(1)}, f32[384,1344]{1,0:T(8,128)S(1)}, f32[8,128]{1,0:T(8,128)S(1)}) custom-call(s32[4]{0:T(128)S(1)} %and_select_fusion.order, bf16[384,768]{1,0:T(8,128)(2,1)S(1)} %collective-permute-done.3.from_last.refs_0_, bf16[384,768]{1,0:T(8,128)(2,1)S(1)} %collective-permute-done.4.from_next.refs_1_, ...), custom_call_target="tpu_custom_call" | custom-call | flops 3170893824 | bytes 8257536 | tf_op jit(solution)/shard_map/pallas_call | solution.py:209
  57.1 3.2 %collective-permute-start.12 = (bf16[384,768]{1,0:T(8,128)(2,1)S(1)}, bf16[384,768]{1,0:T(8,128)(2,1)}, u32[]{:S(2)}, u32[]{:S(2)}) collective-permute-start(bf16[384,768]{1,0:T(8,128)(2,1)S(1)} %shard_map.131.refs_0_), channel_id=1, source_target_pairs={{0,3},{1,0},{2,1},{3,2},{4,7},{5,4},{6,5},{7,6},{8,11},{9,8},{10,9... | collective-permute-start | bytes 1769480 | tf_op jit(solution)/shard_map/ppermute | solution.py:35
  60.3 2.7 %shard_map.128.act = bf16[384,1344]{1,0:T(8,128)(2,1)S(1)} custom-call(s32[4]{0:T(128)S(1)} %and_select_fusion.order, bf16[192,768]{1,0:T(8,128)(2,1)S(1)} %collective-permute-done.5.top, bf16[192,768]{1,0:T(8,128)(2,1)S(1)} %collective-permute-done.6.bottom, f32[384,1344]{1,0:T(8,128)S(1)} %get-tuple-element.54.sum_a, ...), custom_call_target="tpu_custom_call" | custom-call | flops 1585446912 | bytes 4128768 | tf_op jit(solution)/shard_map/pallas_call | solution.py:289
  63.0 5.3 %shard_map.129 = (bf16[384,3072]{1,0:T(8,128)(2,1)}, f32[8,128]{1,0:T(8,128)S(1)}) custom-call(s32[4]{0:T(128)S(1)} %and_select_fusion.order, bf16[384,1344]{1,0:T(8,128)(2,1)S(1)} %shard_map.128.act, bf16[1344,3072]{1,0:T(8,128)(2,1)S(1)} %get-tuple-element.56.weight), custom_call_target="tpu_custom_call" | custom-call | flops 3170893824 | bytes 8257536 | tf_op jit(solution)/shard_map/pallas_call | solution.py:362
  68.3 5.6 %all-to-all-start.1 = ((bf16[16,24,3072]{2,1,0:T(8,128)(2,1)}), bf16[16,24,3072]{2,1,0:T(8,128)(2,1)}, u32[]{:S(2)}, u32[]{:S(2)}) async-start(bf16[16,24,3072]{2,1,0:T(8,128)(2,1)} %bitcast.47), calls=%async_computation.1 | async-start | bytes 4718592 | tf_op jit(solution)/shard_map/all_to_all | solution.py:474
  75.1 3.2 %collective-permute-start.14 = (bf16[192,768]{1,0:T(8,128)(2,1)S(1)}, bf16[192,768]{1,0:T(8,128)(2,1)S(1)}, u32[]{:S(2)}, u32[]{:S(2)}) collective-permute-start(bf16[192,768]{1,0:T(8,128)(2,1)S(1)} %get-tuple-element.65), channel_id=1, source_target_pairs={{0,3},{1,0},{2,1},{3,2},{4,7},{5,4},{6,5},{7,6},{8,11},{9,8},{10,9... | collective-permute-start | bytes 884744 | tf_op jit(solution)/shard_map/ppermute | solution.py:35
  78.4 9.9 %shard_map.134 = (f32[384,1344]{1,0:T(8,128)S(1)}, f32[384,1344]{1,0:T(8,128)S(1)}, bf16[1344,3072]{1,0:T(8,128)(2,1)S(1)}, bf16[1344,3072]{1,0:T(8,128)(2,1)S(1)}, bf16[1344,3072]{1,0:T(8,128)(2,1)S(1)}) custom-call(s32[4]{0:T(128)S(1)} %and_select_fusion.order, bf16[384,768]{1,0:T(8,128)(2,1)S(1)} %shard_map.133.p0, ...), custom_call_target="tpu_custom_call" | custom-call | flops 4756340736 | bytes 12386304 | tf_op jit(solution)/shard_map/pallas_call | solution.py:257
  88.3 9.6 %shard_map.135 = (bf16[384,1344]{1,0:T(8,128)(2,1)S(1)}, bf16[384,1344]{1,0:T(8,128)(2,1)S(1)}, bf16[192,768]{1,0:T(8,128)(2,1)S(1)}, bf16[192,768]{1,0:T(8,128)(2,1)S(1)}) custom-call(s32[4]{0:T(128)S(1)} %and_select_fusion.order, bf16[192,768]{1,0:T(8,128)(2,1)S(1)} %collective-permute-done.13.top, bf16[192,768]{1,0:T(8,128)(2,1)S(1)} %collective-permute-done.14.bottom, ...), custom_call_target="tpu_custom_call" | custom-call | flops 6341787648 | bytes 16515072 | tf_op jit(solution)/shard_map/pallas_call | solution.py:331
  98.0 3.2 %collective-permute-start.16 = (bf16[192,768]{1,0:T(8,128)(2,1)S(1)}, bf16[192,768]{1,0:T(8,128)(2,1)S(1)}, u32[]{:S(2)}, u32[]{:S(2)}) collective-permute-start(bf16[192,768]{1,0:T(8,128)(2,1)S(1)} %get-tuple-element.80), channel_id=1, source_target_pairs={{0,3},{1,0},{2,1},{3,2},{4,7},{5,4},{6,5},{7,6},{8,11},{9,8},{10,9... | collective-permute-start | bytes 884744 | tf_op jit(solution)/shard_map/ppermute | solution.py:35
  101.2 6.3 %shard_map.136 = (bf16[384,768]{1,0:T(8,128)(2,1)S(1)}, bf16[384,768]{1,0:T(8,128)(2,1)S(1)}, f32[384,768]{1,0:T(8,128)S(1)}) custom-call(s32[4]{0:T(128)S(1)} %and_select_fusion.order, bf16[384,1344]{1,0:T(8,128)(2,1)S(1)} %get-tuple-element.74.refs_0_, bf16[384,1344]{1,0:T(8,128)(2,1)S(1)} %get-tuple-element.75.refs_1_, ...), custom_call_target="tpu_custom_call" | custom-call | flops 4756340736 | bytes 12386304 | tf_op jit(solution)/shard_map/pallas_call | solution.py:390
  108.8 3.0 %collective-permute-start.18 = (bf16[384,768]{1,0:T(8,128)(2,1)}, bf16[384,768]{1,0:T(8,128)(2,1)S(1)}, u32[]{:S(2)}, u32[]{:S(2)}) collective-permute-start(bf16[384,768]{1,0:T(8,128)(2,1)} %get-tuple-element.82), channel_id=1, source_target_pairs={{0,3},{1,0},{2,1},{3,2},{4,7},{5,4},{6,5},{7,6},{8,11},{9,8},{10,9... | collective-permute-start | bytes 1769480 | tf_op jit(solution)/shard_map/ppermute | solution.py:35
  111.8 2.3 %shard_map.130 = (f32[64,768]{1,0:T(8,128)S(1)}, bf16[64,768]{1,0:T(8,128)(2,1)S(1)}, bf16[64,768]{1,0:T(8,128)(2,1)S(1)}, bf16[64,768]{1,0:T(8,128)(2,1)S(1)}) custom-call(s32[4]{0:T(128)S(1)} %and_select_fusion.order, bf16[384,128]{1,0:T(8,128)(2,1)S(1)} %copy-done.3, bf16[384,3072]{1,0:T(8,128)(2,1)} %bitcast.17.back, bf16[64,768]{1,0:T(8,128)(2,1)S(1)} %bitcast.37), custom_call_target="tpu_custom_call" | custom-call | tf_op jit(solution)/shard_map/pallas_call | solution.py:458
  114.1 9.3 %collective-permute-done.18.from_next = bf16[384,768]{1,0:T(8,128)(2,1)S(1)} collective-permute-done((bf16[384,768]{1,0:T(8,128)(2,1)}, bf16[384,768]{1,0:T(8,128)(2,1)S(1)}, u32[]{:S(2)}, u32[]{:S(2)}) %collective-permute-start.18) | collective-permute-done | bytes 589856 | tf_op jit(solution)/shard_map/ppermute | solution.py:35
  123.5 3.1 %collective-permute-done.17.from_last = bf16[384,768]{1,0:T(8,128)(2,1)S(1)} collective-permute-done((bf16[384,768]{1,0:T(8,128)(2,1)S(1)}, bf16[384,768]{1,0:T(8,128)(2,1)S(1)}, u32[]{:S(2)}, u32[]{:S(2)}) %collective-permute-start.17) | collective-permute-done | bytes 589856 | tf_op jit(solution)/shard_map/ppermute | solution.py:35
  127.6 5.2 %all-to-all-start.3 = ((bf16[16,24,768]{2,1,0:T(8,128)(2,1)}), bf16[16,24,768]{2,1,0:T(8,128)(2,1)S(1)}, u32[]{:S(2)}, u32[]{:S(2)}) async-start(bf16[16,24,768]{2,1,0:T(8,128)(2,1)} %bitcast.21), calls=%async_computation.3 | async-start | bytes 1179648 | tf_op jit(solution)/shard_map/all_to_all | solution.py:474
  134.9 3.5 %collective-permute-done.7 = bf16[64,768]{1,0:T(8,128)(2,1)S(1)} collective-permute-done((bf16[64,768]{1,0:T(8,128)(2,1)}, bf16[64,768]{1,0:T(8,128)(2,1)S(1)}, u32[]{:S(2)}, u32[]{:S(2)}) %collective-permute-start.7) | collective-permute-done | bytes 98336 | tf_op jit(solution)/shard_map/ppermute | solution.py:35
  138.4 3.0 %collective-permute-done.8 = bf16[64,768]{1,0:T(8,128)(2,1)S(1)} collective-permute-done((bf16[64,768]{1,0:T(8,128)(2,1)S(1)}, bf16[64,768]{1,0:T(8,128)(2,1)S(1)}, u32[]{:S(2)}, u32[]{:S(2)}) %collective-permute-start.8) | collective-permute-done | bytes 98336 | tf_op jit(solution)/shard_map/ppermute | solution.py:35
  141.5 2.8 %collective-permute-start.10 = (bf16[1,64,768]{2,1,0:T(8,128)(2,1)S(1)}, bf16[1,64,768]{2,1,0:T(8,128)(2,1)S(1)}, u32[]{:S(2)}, u32[]{:S(2)}) collective-permute-start(bf16[1,64,768]{2,1,0:T(8,128)(2,1)S(1)} %fusion), channel_id=1, source_target_pairs={{0,64},{64,0},{1,65},{65,1},{2,66},{66,2},{3,67},{67,3},{4,68},{68... | collective-permute-start | bytes 294920 | tf_op jit(solution)/shard_map/ppermute | solution.py:35
  144.7 2.8 %collective-permute-start.19 = (bf16[1,64,768]{2,1,0:T(8,128)(2,1)S(1)}, bf16[1,64,768]{2,1,0:T(8,128)(2,1)S(1)}, u32[]{:S(2)}, u32[]{:S(2)}) collective-permute-start(bf16[1,64,768]{2,1,0:T(8,128)(2,1)S(1)} %bitcast.38), channel_id=1, source_target_pairs={{0,64},{64,0},{1,65},{65,1},{2,66},{66,2},{3,67},{67,3},{4,68},{68... | collective-permute-start | bytes 294920 | tf_op jit(solution)/shard_map/ppermute | solution.py:35
  147.7 3.2 %collective-permute-done.19 = bf16[1,64,768]{2,1,0:T(8,128)(2,1)S(1)} collective-permute-done((bf16[1,64,768]{2,1,0:T(8,128)(2,1)S(1)}, bf16[1,64,768]{2,1,0:T(8,128)(2,1)S(1)}, u32[]{:S(2)}, u32[]{:S(2)}) %collective-permute-start.19) | collective-permute-done | bytes 98336 | tf_op jit(solution)/shard_map/ppermute | solution.py:35
  (55 shorter events, 17.8 us)
Async XLA Ops:
  0.6 14.8 %copy-start.7 = (s32[4]{0:T(128)S(1)}, s32[4]{0:T(128)}, u32[]{:S(2)}) copy-start(s32[4]{0:T(128)} %constant.21.clone) | copy-start | bytes 52
  0.6 8.8 %copy-start = (bf16[1,64,768]{2,1,0:T(8,128)(2,1)S(1)}, bf16[1,64,768]{2,1,0:T(8,128)(2,1)}, u32[]{:S(2)}) copy-start(bf16[1,64,768]{2,1,0:T(8,128)(2,1)} %param.13) | copy-start | bytes 294916
  3.7 16.5 %copy-start.4 = (bf16[384,64]{1,0:T(8,128)(2,1)S(1)}, bf16[384,64]{1,0:T(8,128)(2,1)}, u32[]{:S(2)}) copy-start(bf16[384,64]{1,0:T(8,128)(2,1)} %get-tuple-element.45.table) | copy-start | bytes 147460
  3.7 23.8 %all-to-all-start = ((bf16[16,24,1536]{2,1,0:T(8,128)(2,1)}), bf16[16,24,1536]{2,1,0:T(8,128)(2,1)S(1)}, u32[]{:S(2)}, u32[]{:S(2)}) async-start(bf16[16,24,1536]{2,1,0:T(8,128)(2,1)} %bitcast.48), calls=%async_computation | async-start | bytes 2359296 | tf_op jit(solution)/shard_map/all_to_all | solution.py:474
  9.5 7.5 %collective-permute-start = (bf16[64,768]{1,0:T(8,128)(2,1)S(1)}, bf16[64,768]{1,0:T(8,128)(2,1)S(1)}, u32[]{:S(2)}, u32[]{:S(2)}) collective-permute-start(bf16[64,768]{1,0:T(8,128)(2,1)S(1)} %bitcast.31), channel_id=1, source_target_pairs={{0,1},{1,2},{2,3},{3,0},{4,5},{5,6},{6,7},{7,4},{8,9},{9,10},{10,1... | collective-permute-start | bytes 294920 | tf_op jit(solution)/shard_map/ppermute | solution.py:35
  11.5 7.0 %collective-permute-start.1 = (bf16[64,768]{1,0:T(8,128)(2,1)S(1)}, bf16[64,768]{1,0:T(8,128)(2,1)S(1)}, u32[]{:S(2)}, u32[]{:S(2)}) collective-permute-start(bf16[64,768]{1,0:T(8,128)(2,1)S(1)} %bitcast.32), channel_id=1, source_target_pairs={{0,3},{1,0},{2,1},{3,2},{4,7},{5,4},{6,5},{7,6},{8,11},{9,8},{10,9... | collective-permute-start | bytes 294920 | tf_op jit(solution)/shard_map/ppermute | solution.py:35
  13.7 6.6 %collective-permute-start.2 = (bf16[64,768]{1,0:T(8,128)(2,1)S(1)}, bf16[64,768]{1,0:T(8,128)(2,1)S(1)}, u32[]{:S(2)}, u32[]{:S(2)}) collective-permute-start(bf16[64,768]{1,0:T(8,128)(2,1)S(1)} %bitcast.33), channel_id=1, source_target_pairs={{0,2},{1,3},{2,0},{3,1},{4,6},{5,7},{6,4},{7,5},{8,10},{9,11},{10,... | collective-permute-start | bytes 294920 | tf_op jit(solution)/shard_map/ppermute | solution.py:35
  27.6 40.7 %all-to-all-start.2 = ((bf16[16,24,3072]{2,1,0:T(8,128)(2,1)}), bf16[16,24,3072]{2,1,0:T(8,128)(2,1)S(1)}, u32[]{:S(2)}, u32[]{:S(2)}) async-start(bf16[16,24,3072]{2,1,0:T(8,128)(2,1)} %bitcast.45), calls=%async_computation.2 | async-start | bytes 4718592 | tf_op jit(solution)/shard_map/all_to_all | solution.py:474
  31.4 17.8 %collective-permute-start.3 = (bf16[384,768]{1,0:T(8,128)(2,1)S(1)}, bf16[384,768]{1,0:T(8,128)(2,1)S(1)}, u32[]{:S(2)}, u32[]{:S(2)}) collective-permute-start(bf16[384,768]{1,0:T(8,128)(2,1)S(1)} %get-tuple-element.85.refs_0_), channel_id=1, source_target_pairs={{0,1},{1,2},{2,3},{3,0},{4,5},{5,6},{6,7},{7,4},{8,9},{9,10},{10,1... | collective-permute-start | bytes 1769480 | tf_op jit(solution)/shard_map/ppermute | solution.py:35
  33.3 15.8 %collective-permute-start.4 = (bf16[384,768]{1,0:T(8,128)(2,1)S(1)}, bf16[384,768]{1,0:T(8,128)(2,1)S(1)}, u32[]{:S(2)}, u32[]{:S(2)}) collective-permute-start(bf16[384,768]{1,0:T(8,128)(2,1)S(1)} %get-tuple-element.85.refs_0_), channel_id=1, source_target_pairs={{0,3},{1,0},{2,1},{3,2},{4,7},{5,4},{6,5},{7,6},{8,11},{9,8},{10,9... | collective-permute-start | bytes 1769480 | tf_op jit(solution)/shard_map/ppermute | solution.py:35
  49.2 11.1 %collective-permute-start.5 = (bf16[192,768]{1,0:T(8,128)(2,1)S(1)}, bf16[192,768]{1,0:T(8,128)(2,1)S(1)}, u32[]{:S(2)}, u32[]{:S(2)}) collective-permute-start(bf16[192,768]{1,0:T(8,128)(2,1)S(1)} %get-tuple-element.48.refs_1_), channel_id=1, source_target_pairs={{0,1},{1,2},{2,3},{3,0},{4,5},{5,6},{6,7},{7,4},{8,9},{9,10},{10,1... | collective-permute-start | bytes 884744 | tf_op jit(solution)/shard_map/ppermute | solution.py:35
  50.5 9.8 %collective-permute-start.6 = (bf16[192,768]{1,0:T(8,128)(2,1)S(1)}, bf16[192,768]{1,0:T(8,128)(2,1)S(1)}, u32[]{:S(2)}, u32[]{:S(2)}) collective-permute-start(bf16[192,768]{1,0:T(8,128)(2,1)S(1)} %get-tuple-element.49.refs_2_), channel_id=1, source_target_pairs={{0,3},{1,0},{2,1},{3,2},{4,7},{5,4},{6,5},{7,6},{8,11},{9,8},{10,9... | collective-permute-start | bytes 884744 | tf_op jit(solution)/shard_map/ppermute | solution.py:35
  57.0 16.9 %collective-permute-start.11 = (bf16[384,768]{1,0:T(8,128)(2,1)S(1)}, bf16[384,768]{1,0:T(8,128)(2,1)S(1)}, u32[]{:S(2)}, u32[]{:S(2)}) collective-permute-start(bf16[384,768]{1,0:T(8,128)(2,1)S(1)} %shard_map.131.refs_0_), channel_id=1, source_target_pairs={{0,1},{1,2},{2,3},{3,0},{4,5},{5,6},{6,7},{7,4},{8,9},{9,10},{10,1... | collective-permute-start | bytes 1769480 | tf_op jit(solution)/shard_map/ppermute | solution.py:35
  57.1 16.8 %collective-permute-start.12 = (bf16[384,768]{1,0:T(8,128)(2,1)S(1)}, bf16[384,768]{1,0:T(8,128)(2,1)}, u32[]{:S(2)}, u32[]{:S(2)}) collective-permute-start(bf16[384,768]{1,0:T(8,128)(2,1)S(1)} %shard_map.131.refs_0_), channel_id=1, source_target_pairs={{0,3},{1,0},{2,1},{3,2},{4,7},{5,4},{6,5},{7,6},{8,11},{9,8},{10,9... | collective-permute-start | bytes 1769480 | tf_op jit(solution)/shard_map/ppermute | solution.py:35
  68.3 43.5 %all-to-all-start.1 = ((bf16[16,24,3072]{2,1,0:T(8,128)(2,1)}), bf16[16,24,3072]{2,1,0:T(8,128)(2,1)}, u32[]{:S(2)}, u32[]{:S(2)}) async-start(bf16[16,24,3072]{2,1,0:T(8,128)(2,1)} %bitcast.47), calls=%async_computation.1 | async-start | bytes 4718592 | tf_op jit(solution)/shard_map/all_to_all | solution.py:474
  75.0 13.3 %collective-permute-start.13 = (bf16[192,768]{1,0:T(8,128)(2,1)S(1)}, bf16[192,768]{1,0:T(8,128)(2,1)S(1)}, u32[]{:S(2)}, u32[]{:S(2)}) collective-permute-start(bf16[192,768]{1,0:T(8,128)(2,1)S(1)} %get-tuple-element.64), channel_id=1, source_target_pairs={{0,1},{1,2},{2,3},{3,0},{4,5},{5,6},{6,7},{7,4},{8,9},{9,10},{10,1... | collective-permute-start | bytes 884744 | tf_op jit(solution)/shard_map/ppermute | solution.py:35
  75.1 13.2 %collective-permute-start.14 = (bf16[192,768]{1,0:T(8,128)(2,1)S(1)}, bf16[192,768]{1,0:T(8,128)(2,1)S(1)}, u32[]{:S(2)}, u32[]{:S(2)}) collective-permute-start(bf16[192,768]{1,0:T(8,128)(2,1)S(1)} %get-tuple-element.65), channel_id=1, source_target_pairs={{0,3},{1,0},{2,1},{3,2},{4,7},{5,4},{6,5},{7,6},{8,11},{9,8},{10,9... | collective-permute-start | bytes 884744 | tf_op jit(solution)/shard_map/ppermute | solution.py:35
  97.9 10.0 %collective-permute-start.15 = (bf16[192,768]{1,0:T(8,128)(2,1)S(1)}, bf16[192,768]{1,0:T(8,128)(2,1)S(1)}, u32[]{:S(2)}, u32[]{:S(2)}) collective-permute-start(bf16[192,768]{1,0:T(8,128)(2,1)S(1)} %get-tuple-element.79), channel_id=1, source_target_pairs={{0,1},{1,2},{2,3},{3,0},{4,5},{5,6},{6,7},{7,4},{8,9},{9,10},{10,1... | collective-permute-start | bytes 884744 | tf_op jit(solution)/shard_map/ppermute | solution.py:35
  98.0 9.9 %collective-permute-start.16 = (bf16[192,768]{1,0:T(8,128)(2,1)S(1)}, bf16[192,768]{1,0:T(8,128)(2,1)S(1)}, u32[]{:S(2)}, u32[]{:S(2)}) collective-permute-start(bf16[192,768]{1,0:T(8,128)(2,1)S(1)} %get-tuple-element.80), channel_id=1, source_target_pairs={{0,3},{1,0},{2,1},{3,2},{4,7},{5,4},{6,5},{7,6},{8,11},{9,8},{10,9... | collective-permute-start | bytes 884744 | tf_op jit(solution)/shard_map/ppermute | solution.py:35
  101.2 10.6 %copy-start.2 = (bf16[1,64,768]{2,1,0:T(8,128)(2,1)S(1)}, bf16[1,64,768]{2,1,0:T(8,128)(2,1)}, u32[]{:S(2)}) copy-start(bf16[1,64,768]{2,1,0:T(8,128)(2,1)} %param.11) | copy-start | bytes 294916
  101.2 10.6 %copy-start.3 = (bf16[384,128]{1,0:T(8,128)(2,1)S(1)}, bf16[384,128]{1,0:T(8,128)(2,1)}, u32[]{:S(2)}) copy-start(bf16[384,128]{1,0:T(8,128)(2,1)} %get-tuple-element.43.table) | copy-start | bytes 294916
  108.8 14.6 %collective-permute-start.18 = (bf16[384,768]{1,0:T(8,128)(2,1)}, bf16[384,768]{1,0:T(8,128)(2,1)S(1)}, u32[]{:S(2)}, u32[]{:S(2)}) collective-permute-start(bf16[384,768]{1,0:T(8,128)(2,1)} %get-tuple-element.82), channel_id=1, source_target_pairs={{0,3},{1,0},{2,1},{3,2},{4,7},{5,4},{6,5},{7,6},{8,11},{9,8},{10,9... | collective-permute-start | bytes 1769480 | tf_op jit(solution)/shard_map/ppermute | solution.py:35
  111.8 14.8 %collective-permute-start.17 = (bf16[384,768]{1,0:T(8,128)(2,1)S(1)}, bf16[384,768]{1,0:T(8,128)(2,1)S(1)}, u32[]{:S(2)}, u32[]{:S(2)}) collective-permute-start(bf16[384,768]{1,0:T(8,128)(2,1)S(1)} %get-tuple-element.81), channel_id=1, source_target_pairs={{0,1},{1,2},{2,3},{3,0},{4,5},{5,6},{6,7},{7,4},{8,9},{9,10},{10,1... | collective-permute-start | bytes 1769480 | tf_op jit(solution)/shard_map/ppermute | solution.py:35
  114.1 13.4 %copy-start.6 = (bf16[64,768]{1,0:T(8,128)(2,1)}, bf16[64,768]{1,0:T(8,128)(2,1)S(1)}, u32[]{:S(2)}) copy-start(bf16[64,768]{1,0:T(8,128)(2,1)S(1)} %get-tuple-element.59) | copy-start | bytes 294916
  126.6 17.9 %copy-start.1 = (bf16[1,64,768]{2,1,0:T(8,128)(2,1)S(1)}, bf16[1,64,768]{2,1,0:T(8,128)(2,1)}, u32[]{:S(2)}) copy-start(bf16[1,64,768]{2,1,0:T(8,128)(2,1)} %param.13) | copy-start | bytes 294916
  126.6 17.9 %copy-start.5 = (bf16[384,128]{1,0:T(8,128)(2,1)S(1)}, bf16[384,128]{1,0:T(8,128)(2,1)}, u32[]{:S(2)}) copy-start(bf16[384,128]{1,0:T(8,128)(2,1)} %get-tuple-element.62.table) | copy-start | bytes 294916
  127.6 16.9 %all-to-all-start.3 = ((bf16[16,24,768]{2,1,0:T(8,128)(2,1)}), bf16[16,24,768]{2,1,0:T(8,128)(2,1)S(1)}, u32[]{:S(2)}, u32[]{:S(2)}) async-start(bf16[16,24,768]{2,1,0:T(8,128)(2,1)} %bitcast.21), calls=%async_computation.3 | async-start | bytes 1179648 | tf_op jit(solution)/shard_map/all_to_all | solution.py:474
  132.8 5.6 %collective-permute-start.7 = (bf16[64,768]{1,0:T(8,128)(2,1)}, bf16[64,768]{1,0:T(8,128)(2,1)S(1)}, u32[]{:S(2)}, u32[]{:S(2)}) collective-permute-start(bf16[64,768]{1,0:T(8,128)(2,1)} %copy-done.6), channel_id=1, source_target_pairs={{0,3},{1,0},{2,1},{3,2},{4,7},{5,4},{6,5},{7,6},{8,11},{9,8},{10,9... | collective-permute-start | bytes 294920 | tf_op jit(solution)/shard_map/ppermute | solution.py:35
  133.4 8.1 %collective-permute-start.8 = (bf16[64,768]{1,0:T(8,128)(2,1)S(1)}, bf16[64,768]{1,0:T(8,128)(2,1)S(1)}, u32[]{:S(2)}, u32[]{:S(2)}) collective-permute-start(bf16[64,768]{1,0:T(8,128)(2,1)S(1)} %get-tuple-element.60), channel_id=1, source_target_pairs={{0,1},{1,2},{2,3},{3,0},{4,5},{5,6},{6,7},{7,4},{8,9},{9,10},{10,1... | collective-permute-start | bytes 294920 | tf_op jit(solution)/shard_map/ppermute | solution.py:35
  134.9 6.5 %collective-permute-start.9 = (bf16[64,768]{1,0:T(8,128)(2,1)S(1)}, bf16[64,768]{1,0:T(8,128)(2,1)S(1)}, u32[]{:S(2)}, u32[]{:S(2)}) collective-permute-start(bf16[64,768]{1,0:T(8,128)(2,1)S(1)} %get-tuple-element.61), channel_id=1, source_target_pairs={{0,2},{1,3},{2,0},{3,1},{4,6},{5,7},{6,4},{7,5},{8,10},{9,11},{10,... | collective-permute-start | bytes 294920 | tf_op jit(solution)/shard_map/ppermute | solution.py:35
  141.5 6.2 %collective-permute-start.10 = (bf16[1,64,768]{2,1,0:T(8,128)(2,1)S(1)}, bf16[1,64,768]{2,1,0:T(8,128)(2,1)S(1)}, u32[]{:S(2)}, u32[]{:S(2)}) collective-permute-start(bf16[1,64,768]{2,1,0:T(8,128)(2,1)S(1)} %fusion), channel_id=1, source_target_pairs={{0,64},{64,0},{1,65},{65,1},{2,66},{66,2},{3,67},{67,3},{4,68},{68... | collective-permute-start | bytes 294920 | tf_op jit(solution)/shard_map/ppermute | solution.py:35
  144.7 6.2 %collective-permute-start.19 = (bf16[1,64,768]{2,1,0:T(8,128)(2,1)S(1)}, bf16[1,64,768]{2,1,0:T(8,128)(2,1)S(1)}, u32[]{:S(2)}, u32[]{:S(2)}) collective-permute-start(bf16[1,64,768]{2,1,0:T(8,128)(2,1)S(1)} %bitcast.38), channel_id=1, source_target_pairs={{0,64},{64,0},{1,65},{65,1},{2,66},{66,2},{3,67},{67,3},{4,68},{68... | collective-permute-start | bytes 294920 | tf_op jit(solution)/shard_map/ppermute | solution.py:35

commit v4 on v3

--- a/solution.py
+++ b/solution.py
@@ -372,62 +372,75 @@
     )(order, near(act), near(weight))
 
 
-def down_kernel(which, pairs, order, *refs):
-    acts, weights, outs = refs[:pairs], refs[pairs : 2 * pairs], refs[2 * pairs :]
-    quarter = weights[0].shape[1] // 4
-    for n, entry in enumerate(which):
-        slots = columns(order[entry], quarter)
-        total = functools.reduce(
-            jnp.add, [jnp.dot(a[...], w[:, slots], preferred_element_type=F32) for a, w in zip(acts, weights)]
-        )
-        outs[n][...] = total.astype(outs[n].dtype)
-
-
-def down_projections(order, which, acts, weights, outs):
+def sides_kernel(order, da, db, wg, wu, next_top, next_bottom, last_top, last_bottom):
+    half, quarter = next_top.shape
+    for entry, top, bottom in ((2, next_top, next_bottom), (1, last_top, last_bottom)):
+        result = feature_slice(order[entry], (da, db), (wg, wu), quarter).astype(BF16)
+        top[...] = result[:half]
+        bottom[...] = result[half:]
+
+
+def own_kernel(order, da, db, wg, wu, own):
+    own[...] = feature_slice(order[0], (da, db), (wg, wu), own.shape[1])
+
+
+def feature_slice(place, acts, weights, quarter):
+    slots = columns(place, quarter)
+    return functools.reduce(
+        jnp.add, [jnp.dot(a[...], w[:, slots], preferred_element_type=F32) for a, w in zip(acts, weights)]
+    )
+
+
+def result_slices(kernel, order, acts, weights, slices, outs):
     rows, units = acts[0].shape
     quarter = weights[0].shape[1] // 4
-    pairs = len(acts)
-    return pl.pallas_call(
-        functools.partial(down_kernel, which, pairs),
-        in_specs=[SMEM] + [VMEM] * (2 * pairs),
+    return pl.pallas_call(
+        kernel,
+        in_specs=[SMEM] + [VMEM] * 4,
         out_specs=[VMEM] * len(outs),
         out_shape=outs,
         compiler_params=params(),
         cost_estimate=pl.CostEstimate(
-            flops=2 * len(which) * pairs * rows * units * quarter,
-            bytes_accessed=2 * len(which) * pairs * units * quarter,
-            transcendentals=0,
+            flops=4 * slices * rows * units * quarter, bytes_accessed=4 * slices * units * quarter, transcendentals=0
         ),
     )(order, *[near(array) for array in (*acts, *weights)])
 
 
-def passed_kernel(to_next, to_last, up, down, next_sum, last_sum):
-    half = up.shape[0]
-    next_sum[:half] = (to_next[:half].astype(F32) + up[...].astype(F32)).astype(BF16)
-    next_sum[half:] = to_next[half:]
-    last_sum[:half] = to_last[:half]
-    last_sum[half:] = (to_last[half:].astype(F32) + down[...].astype(F32)).astype(BF16)
-
-
-def total_kernel(own, from_last, from_next, out):
-    out[...] = (own[...] + from_last[...].astype(F32) + from_next[...].astype(F32)).astype(BF16)
+def passed_kernel(next_top, last_bottom, up, down, next_sum, last_sum):
+    next_sum[...] = (next_top[...].astype(F32) + up[...].astype(F32)).astype(BF16)
+    last_sum[...] = (last_bottom[...].astype(F32) + down[...].astype(F32)).astype(BF16)
+
+
+def total_kernel(own, last_top, last_bottom, next_top, next_bottom, out):
+    half = last_top.shape[0]
+    tops = last_top[...].astype(F32) + next_top[...].astype(F32)
+    bottoms = last_bottom[...].astype(F32) + next_bottom[...].astype(F32)
+    out[:half] = (own[:half] + tops).astype(BF16)
+    out[half:] = (own[half:] + bottoms).astype(BF16)
 
 
 def summed_over_tensor(order, top, bottom, acts, weights, earlier):
     rows = acts[0].shape[0]
     quarter = weights[0].shape[1] // 4
-    whole = jax.ShapeDtypeStruct((rows, quarter), BF16)
+    half = jax.ShapeDtypeStruct((rows // 2, quarter), BF16)
+    kept = pltpu.VMEM(half.shape, BF16)
     up = shift(top, "tensor", 1)
     down = shift(bottom, "tensor", -1)
-    kept = [pltpu.VMEM(whole.shape, BF16)] * 2 + [pltpu.VMEM(whole.shape, F32)]
-    to_next, to_last, own = down_projections(order, (2, 1, 0), acts, weights, kept)
-    to_next, to_last = pl.pallas_call(passed_kernel, out_shape=[whole, whole], compiler_params=params())(
-        near(to_next), near(to_last), up, down
+    next_top, next_bottom, last_top, last_bottom = result_slices(
+        sides_kernel, order, acts, weights, 2, [kept, half, half, kept]
     )
-    from_last = shift(to_next, "tensor", 1)
-    from_next = shift(to_last, "tensor", -1)
-    from_next = after(from_next, *earlier)
-    return pl.pallas_call(total_kernel, out_shape=whole, compiler_params=params())(near(own), from_last, from_next)
+    from_last_bottom = shift(next_bottom, "tensor", 1)
+    from_next_top = shift(last_top, "tensor", -1)
+    (own,) = result_slices(own_kernel, order, acts, weights, 1, [pltpu.VMEM((rows, quarter), F32)])
+    next_top, last_bottom = pl.pallas_call(passed_kernel, out_shape=[half, half], compiler_params=params())(
+        near(next_top), near(last_bottom), up, down
+    )
+    from_last_top = shift(next_top, "tensor", 1)
+    from_next_bottom = shift(last_bottom, "tensor", -1)
+    from_next_bottom = after(from_next_bottom, *earlier)
+    return pl.pallas_call(
+        total_kernel, out_shape=jax.ShapeDtypeStruct((rows, quarter), BF16), compiler_params=params()
+    )(near(own), from_last_top, from_last_bottom, from_next_top, from_next_bottom)
 
 
 def mix(table, back):

time: 153 us -> 153 us (level)
  waiting for transfers between devices: 34.7 us -> 30.7 us
  starting transfers between devices: 54.3 us -> 57.6 us
    ppermute x20 -> x22, waiting for transfers between devices: 30.1 us -> 26.1 us  [shift(): lax.ppermute(shard, axis, [(i, (i + by) % length) for i in range(length)])]
    ppermute x20 -> x22, starting transfers between devices: 34.1 us -> 37.3 us  [shift(): lax.ppermute(shard, axis, [(i, (i + by) % length) for i in range(length)])]
    pallas_call x3 -> x4, Pallas kernels: 8.22 us -> 8.87 us  [the longest x2 6.95 us: result_slices(): pl.pallas_call(kernel, in_specs=[SMEM] + [VMEM] * 4, out_specs=[VMEM] * l...]
  transfers between devices with their start and end apart: 24 -> 26, of which waited for: 13 -> 14; matrix products, arithmetic and copies ran while one was open for 0% -> 0% of each run, Pallas kernels for 37% -> 38%
where the time goes in v4:
time: 153 us; the launch traced here: 152 us
  Pallas kernels  61.6 us (40%)
  starting transfers between devices  57.6 us (38%)
  waiting for transfers between devices  30.7 us (20%)
    ppermute x22, starting transfers between devices, shift(): lax.ppermute(shard, axis, [(i, (i + by) % length) for i in range(length)])  37.3 us
    ppermute x22, waiting for transfers between devices, shift(): lax.ppermute(shard, axis, [(i, (i + by) % length) for i in range(length)])  26.1 us
    all_to_all x4, starting transfers between devices, exchange(): lax.all_to_all(rows, 'expert', split_axis=0, concat_axis=0, tiled=True)  20.3 us
    pallas_call x1, Pallas kernels, begin_loading(): pl.pallas_call(begin_loading_kernel, in_specs=[SMEM] + [ANY] * 6, out_spe...  9.93 us
    pallas_call x1, Pallas kernels, middle(): pl.pallas_call(middle_kernel, in_specs=[SMEM] + [VMEM] * 8, out_specs=[VM...  9.52 us
    pallas_call x1, Pallas kernels, load_weights(): pl.pallas_call(load_kernel, in_specs=[ANY] * len(weights), out_specs=[VME...  8.07 us
    pallas_call x2, Pallas kernels, begin(): pl.pallas_call(functools.partial(begin_kernel, first_entry, count), in_sp...  7.57 us
    pallas_call x2, Pallas kernels, result_slices(): pl.pallas_call(kernel, in_specs=[SMEM] + [VMEM] * 4, out_specs=[VMEM] * l...  6.95 us
  transfers between devices with their start and end apart: 26, of which 14 were waited for; matrix products, arithmetic and copies ran while one was open for 0% of the time, Pallas kernels for 38%

profile of v4, /device:TPU:0, one launch (start us, length us, event | category | flops | bytes accessed | tf_op | source)
XLA Modules:
  0.0 152.2 jit_solution(4371784585874230491)
XLA Ops:
  0.7 3.1 %shard_map.122 = (bf16[384,1536]{1,0:T(8,128)(2,1)}, bf16[384,64]{1,0:T(8,128)(2,1)}, bf16[384,128]{1,0:T(8,128)(2,1)}, bf16[384,128]{1,0:T(8,128)(2,1)}) custom-call(s32[4,64]{1,0:T(4,128)} %bitcast.50, s32[4,64]{1,0:T(4,128)} %bitcast.51, s32[4,64]{1,0:T(4,128)} %bitcast.52, s32[4,64]{1,0:T(4,128)} %bitcast.53, bf16[64,768]{1,0:T(8,128)(2,1)} %bitcast.36, ...), custom_call_target="tpu_custom_call" | custom-call | tf_op jit(solution)/shard_map/pallas_call | solution.py:81
  3.8 5.7 %all-to-all-start = ((bf16[16,24,1536]{2,1,0:T(8,128)(2,1)}), bf16[16,24,1536]{2,1,0:T(8,128)(2,1)S(1)}, u32[]{:S(2)}, u32[]{:S(2)}) async-start(bf16[16,24,1536]{2,1,0:T(8,128)(2,1)} %bitcast.48), calls=%async_computation | async-start | bytes 2359296 | tf_op jit(solution)/shard_map/all_to_all | solution.py:487
  11.5 2.2 %collective-permute-start.1 = (bf16[64,768]{1,0:T(8,128)(2,1)S(1)}, bf16[64,768]{1,0:T(8,128)(2,1)S(1)}, u32[]{:S(2)}, u32[]{:S(2)}) collective-permute-start(bf16[64,768]{1,0:T(8,128)(2,1)S(1)} %bitcast.32), channel_id=1, source_target_pairs={{0,3},{1,0},{2,1},{3,2},{4,7},{5,4},{6,5},{7,6},{8,11},{9,8},{10,9... | collective-permute-start | bytes 294920 | tf_op jit(solution)/shard_map/ppermute | solution.py:35
  20.3 2.8 %shard_map.123 = bf16[384,3072]{1,0:T(8,128)(2,1)} custom-call(s32[4]{0:T(128)S(1)} %and_select_fusion.order, bf16[384,64]{1,0:T(8,128)(2,1)S(1)} %copy-done.4, bf16[64,768]{1,0:T(8,128)(2,1)S(1)} %bitcast.34, bf16[64,768]{1,0:T(8,128)(2,1)S(1)} %collective-permute-done.p1, bf16[64,768]{1,0:T(8,128)(2,1)S(1)} %collective-permute-done.1.p2, ...), custom_call_target="tpu_custom_call" | custom-call | tf_op jit(solution)/shard_map/pallas_call | solution.py:103
  23.1 4.5 %all-to-all-done = bf16[16,24,1536]{2,1,0:T(8,128)(2,1)S(1)} async-done(((bf16[16,24,1536]{2,1,0:T(8,128)(2,1)}), bf16[16,24,1536]{2,1,0:T(8,128)(2,1)S(1)}, u32[]{:S(2)}, u32[]{:S(2)}) %all-to-all-start) | async-done | bytes 1179680 | tf_op jit(solution)/shard_map/all_to_all | solution.py:487
  27.6 3.7 %all-to-all-start.2 = ((bf16[16,24,3072]{2,1,0:T(8,128)(2,1)}), bf16[16,24,3072]{2,1,0:T(8,128)(2,1)S(1)}, u32[]{:S(2)}, u32[]{:S(2)}) async-start(bf16[16,24,3072]{2,1,0:T(8,128)(2,1)} %bitcast.45), calls=%async_computation.2 | async-start | bytes 4718592 | tf_op jit(solution)/shard_map/all_to_all | solution.py:487
  35.6 8.1 %shard_map.124 = (bf16[1344,3072]{1,0:T(8,128)(2,1)S(1)}, bf16[1344,3072]{1,0:T(8,128)(2,1)S(1)}, bf16[1344,3072]{1,0:T(8,128)(2,1)S(1)}, f32[8,128]{1,0:T(8,128)S(1)}) custom-call(bf16[1344,3072]{1,0:T(8,128)(2,1)} %bitcast.39, bf16[1344,3072]{1,0:T(8,128)(2,1)} %bitcast.41, bf16[1344,3072]{1,0:T(8,128)(2,1)} %bitcast.43), custom_call_target="tpu_custom_call" | custom-call | bytes 24772608 | tf_op jit(solution)/shard_map/pallas_call | solution.py:132
  43.7 3.1 %shard_map.126 = (f32[384,1344]{1,0:T(8,128)S(1)}, f32[384,1344]{1,0:T(8,128)S(1)}, f32[8,128]{1,0:T(8,128)}) custom-call(s32[4]{0:T(128)S(1)} %and_select_fusion.order, bf16[384,768]{1,0:T(8,128)(2,1)S(1)} %get-tuple-element.87.refs_0_, bf16[1344,3072]{1,0:T(8,128)(2,1)S(1)} %get-tuple-element.51.refs_1_.refs_2_.wg, ...), custom_call_target="tpu_custom_call" | custom-call | flops 1585446912 | bytes 4128768 | tf_op jit(solution)/shard_map/pallas_call | solution.py:209
  46.7 2.5 %collective-permute-done.3.from_last.refs_0_ = bf16[384,768]{1,0:T(8,128)(2,1)S(1)} collective-permute-done((bf16[384,768]{1,0:T(8,128)(2,1)S(1)}, bf16[384,768]{1,0:T(8,128)(2,1)S(1)}, u32[]{:S(2)}, u32[]{:S(2)}) %collective-permute-start.3) | collective-permute-done | bytes 589856 | tf_op jit(solution)/shard_map/ppermute | solution.py:35
  52.6 4.5 %shard_map.127 = (f32[384,1344]{1,0:T(8,128)S(1)}, f32[384,1344]{1,0:T(8,128)S(1)}, f32[8,128]{1,0:T(8,128)S(1)}) custom-call(s32[4]{0:T(128)S(1)} %and_select_fusion.order, bf16[384,768]{1,0:T(8,128)(2,1)S(1)} %collective-permute-done.3.from_last.refs_0_, bf16[384,768]{1,0:T(8,128)(2,1)S(1)} %collective-permute-done.4.from_next.refs_1_, ...), custom_call_target="tpu_custom_call" | custom-call | flops 3170893824 | bytes 8257536 | tf_op jit(solution)/shard_map/pallas_call | solution.py:209
  57.2 3.2 %collective-permute-start.12 = (bf16[384,768]{1,0:T(8,128)(2,1)S(1)}, bf16[384,768]{1,0:T(8,128)(2,1)}, u32[]{:S(2)}, u32[]{:S(2)}) collective-permute-start(bf16[384,768]{1,0:T(8,128)(2,1)S(1)} %shard_map.131.refs_0_), channel_id=1, source_target_pairs={{0,3},{1,0},{2,1},{3,2},{4,7},{5,4},{6,5},{7,6},{8,11},{9,8},{10,9... | collective-permute-start | bytes 1769480 | tf_op jit(solution)/shard_map/ppermute | solution.py:35
  60.4 2.7 %shard_map.128.act = bf16[384,1344]{1,0:T(8,128)(2,1)S(1)} custom-call(s32[4]{0:T(128)S(1)} %and_select_fusion.order, bf16[192,768]{1,0:T(8,128)(2,1)S(1)} %collective-permute-done.5.top, bf16[192,768]{1,0:T(8,128)(2,1)S(1)} %collective-permute-done.6.bottom, f32[384,1344]{1,0:T(8,128)S(1)} %get-tuple-element.55.sum_a, ...), custom_call_target="tpu_custom_call" | custom-call | flops 1585446912 | bytes 4128768 | tf_op jit(solution)/shard_map/pallas_call | solution.py:289
  63.0 5.3 %shard_map.129 = (bf16[384,3072]{1,0:T(8,128)(2,1)}, f32[8,128]{1,0:T(8,128)S(1)}) custom-call(s32[4]{0:T(128)S(1)} %and_select_fusion.order, bf16[384,1344]{1,0:T(8,128)(2,1)S(1)} %shard_map.128.act, bf16[1344,3072]{1,0:T(8,128)(2,1)S(1)} %get-tuple-element.57.weight), custom_call_target="tpu_custom_call" | custom-call | flops 3170893824 | bytes 8257536 | tf_op jit(solution)/shard_map/pallas_call | solution.py:362
  68.3 5.6 %all-to-all-start.1 = ((bf16[16,24,3072]{2,1,0:T(8,128)(2,1)}), bf16[16,24,3072]{2,1,0:T(8,128)(2,1)}, u32[]{:S(2)}, u32[]{:S(2)}) async-start(bf16[16,24,3072]{2,1,0:T(8,128)(2,1)} %bitcast.47), calls=%async_computation.1 | async-start | bytes 4718592 | tf_op jit(solution)/shard_map/all_to_all | solution.py:487
  75.2 3.2 %collective-permute-start.14 = (bf16[192,768]{1,0:T(8,128)(2,1)S(1)}, bf16[192,768]{1,0:T(8,128)(2,1)S(1)}, u32[]{:S(2)}, u32[]{:S(2)}) collective-permute-start(bf16[192,768]{1,0:T(8,128)(2,1)S(1)} %get-tuple-element.66), channel_id=1, source_target_pairs={{0,3},{1,0},{2,1},{3,2},{4,7},{5,4},{6,5},{7,6},{8,11},{9,8},{10,9... | collective-permute-start | bytes 884744 | tf_op jit(solution)/shard_map/ppermute | solution.py:35
  78.4 9.9 %shard_map.134 = (f32[384,1344]{1,0:T(8,128)S(1)}, f32[384,1344]{1,0:T(8,128)S(1)}, bf16[1344,3072]{1,0:T(8,128)(2,1)S(1)}, bf16[1344,3072]{1,0:T(8,128)(2,1)S(1)}, bf16[1344,3072]{1,0:T(8,128)(2,1)S(1)}) custom-call(s32[4]{0:T(128)S(1)} %and_select_fusion.order, bf16[384,768]{1,0:T(8,128)(2,1)S(1)} %shard_map.133.p0, ...), custom_call_target="tpu_custom_call" | custom-call | flops 4756340736 | bytes 12386304 | tf_op jit(solution)/shard_map/pallas_call | solution.py:257
  88.4 9.5 %shard_map.135 = (bf16[384,1344]{1,0:T(8,128)(2,1)S(1)}, bf16[384,1344]{1,0:T(8,128)(2,1)S(1)}, bf16[192,768]{1,0:T(8,128)(2,1)S(1)}, bf16[192,768]{1,0:T(8,128)(2,1)S(1)}) custom-call(s32[4]{0:T(128)S(1)} %and_select_fusion.order, bf16[192,768]{1,0:T(8,128)(2,1)S(1)} %collective-permute-done.13.top, bf16[192,768]{1,0:T(8,128)(2,1)S(1)} %collective-permute-done.14.bottom, ...), custom_call_target="tpu_custom_call" | custom-call | flops 6341787648 | bytes 16515072 | tf_op jit(solution)/shard_map/pallas_call | solution.py:331
  98.0 3.2 %collective-permute-start.16 = (bf16[192,768]{1,0:T(8,128)(2,1)S(1)}, bf16[192,768]{1,0:T(8,128)(2,1)S(1)}, u32[]{:S(2)}, u32[]{:S(2)}) collective-permute-start(bf16[192,768]{1,0:T(8,128)(2,1)S(1)} %get-tuple-element.80), channel_id=1, source_target_pairs={{0,3},{1,0},{2,1},{3,2},{4,7},{5,4},{6,5},{7,6},{8,11},{9,8},{10,9... | collective-permute-start | bytes 884744 | tf_op jit(solution)/shard_map/ppermute | solution.py:35
  101.2 4.4 %shard_map.137 = (bf16[192,768]{1,0:T(8,128)(2,1)S(1)}, bf16[192,768]{1,0:T(8,128)(2,1)S(1)}, bf16[192,768]{1,0:T(8,128)(2,1)S(1)}, bf16[192,768]{1,0:T(8,128)(2,1)S(1)}) custom-call(s32[4]{0:T(128)S(1)} %and_select_fusion.order, bf16[384,1344]{1,0:T(8,128)(2,1)S(1)} %get-tuple-element.75.da, bf16[384,1344]{1,0:T(8,128)(2,1)S(1)} %get-tuple-element.76.db, ...), custom_call_target="tpu_custom_call" | custom-call | flops 3170893824 | bytes 8257536 | tf_op jit(solution)/shard_map/pallas_call | solution.py:397
  105.6 2.2 %collective-permute-done.15.up = bf16[192,768]{1,0:T(8,128)(2,1)S(1)} collective-permute-done((bf16[192,768]{1,0:T(8,128)(2,1)S(1)}, bf16[192,768]{1,0:T(8,128)(2,1)S(1)}, u32[]{:S(2)}, u32[]{:S(2)}) %collective-permute-start.15) | collective-permute-done | bytes 294944 | tf_op jit(solution)/shard_map/ppermute | solution.py:35
  108.8 3.0 %collective-permute-start.20 = (bf16[192,768]{1,0:T(8,128)(2,1)}, bf16[192,768]{1,0:T(8,128)(2,1)S(1)}, u32[]{:S(2)}, u32[]{:S(2)}) collective-permute-start(bf16[192,768]{1,0:T(8,128)(2,1)} %get-tuple-element.84), channel_id=1, source_target_pairs={{0,3},{1,0},{2,1},{3,2},{4,7},{5,4},{6,5},{7,6},{8,11},{9,8},{10,9... | collective-permute-start | bytes 884744 | tf_op jit(solution)/shard_map/ppermute | solution.py:35
  111.7 3.2 %collective-permute-start.19 = (bf16[192,768]{1,0:T(8,128)(2,1)S(1)}, bf16[192,768]{1,0:T(8,128)(2,1)S(1)}, u32[]{:S(2)}, u32[]{:S(2)}) collective-permute-start(bf16[192,768]{1,0:T(8,128)(2,1)S(1)} %get-tuple-element.83), channel_id=1, source_target_pairs={{0,3},{1,0},{2,1},{3,2},{4,7},{5,4},{6,5},{7,6},{8,11},{9,8},{10,9... | collective-permute-start | bytes 884744 | tf_op jit(solution)/shard_map/ppermute | solution.py:35
  115.0 2.5 %shard_map.136.own = f32[384,768]{1,0:T(8,128)S(1)} custom-call(s32[4]{0:T(128)S(1)} %and_select_fusion.order, bf16[384,1344]{1,0:T(8,128)(2,1)S(1)} %get-tuple-element.75.da, bf16[384,1344]{1,0:T(8,128)(2,1)S(1)} %get-tuple-element.76.db, bf16[1344,3072]{1,0:T(8,128)(2,1)S(1)} %get-tuple-element.72.wg, bf16[1344,3072]{1,0:T(8,128)(2,1)S(1)} %get-tuple-element.73.wu), custom_call_target="tpu_custom_call" | custom-call | flops 1585446912 | bytes 4128768 | tf_op jit(solution)/shard_map/pallas_call | solution.py:397
  117.5 2.3 %shard_map.130 = (f32[64,768]{1,0:T(8,128)S(1)}, bf16[64,768]{1,0:T(8,128)(2,1)S(1)}, bf16[64,768]{1,0:T(8,128)(2,1)S(1)}, bf16[64,768]{1,0:T(8,128)(2,1)S(1)}) custom-call(s32[4]{0:T(128)S(1)} %and_select_fusion.order, bf16[384,128]{1,0:T(8,128)(2,1)S(1)} %copy-done.3, bf16[384,3072]{1,0:T(8,128)(2,1)} %bitcast.17.back, bf16[64,768]{1,0:T(8,128)(2,1)S(1)} %bitcast.37), custom_call_target="tpu_custom_call" | custom-call | tf_op jit(solution)/shard_map/pallas_call | solution.py:471
  119.9 3.0 %collective-permute-done.18.last_bottom = bf16[192,768]{1,0:T(8,128)(2,1)S(1)} collective-permute-done((bf16[192,768]{1,0:T(8,128)(2,1)S(1)}, bf16[192,768]{1,0:T(8,128)(2,1)S(1)}, u32[]{:S(2)}, u32[]{:S(2)}) %collective-permute-start.18) | collective-permute-done | bytes 294944 | tf_op jit(solution)/shard_map/ppermute | solution.py:35
  123.3 3.2 %collective-permute-done.17.last_top = bf16[192,768]{1,0:T(8,128)(2,1)S(1)} collective-permute-done((bf16[192,768]{1,0:T(8,128)(2,1)}, bf16[192,768]{1,0:T(8,128)(2,1)S(1)}, u32[]{:S(2)}, u32[]{:S(2)}) %collective-permute-start.17) | collective-permute-done | bytes 294944 | tf_op jit(solution)/shard_map/ppermute | solution.py:35
  127.5 5.3 %all-to-all-start.3 = ((bf16[16,24,768]{2,1,0:T(8,128)(2,1)}), bf16[16,24,768]{2,1,0:T(8,128)(2,1)S(1)}, u32[]{:S(2)}, u32[]{:S(2)}) async-start(bf16[16,24,768]{2,1,0:T(8,128)(2,1)} %bitcast.21), calls=%async_computation.3 | async-start | bytes 1179648 | tf_op jit(solution)/shard_map/all_to_all | solution.py:487
  134.9 3.5 %collective-permute-done.7 = bf16[64,768]{1,0:T(8,128)(2,1)S(1)} collective-permute-done((bf16[64,768]{1,0:T(8,128)(2,1)}, bf16[64,768]{1,0:T(8,128)(2,1)S(1)}, u32[]{:S(2)}, u32[]{:S(2)}) %collective-permute-start.7) | collective-permute-done | bytes 98336 | tf_op jit(solution)/shard_map/ppermute | solution.py:35
  138.4 3.0 %collective-permute-done.8 = bf16[64,768]{1,0:T(8,128)(2,1)S(1)} collective-permute-done((bf16[64,768]{1,0:T(8,128)(2,1)S(1)}, bf16[64,768]{1,0:T(8,128)(2,1)S(1)}, u32[]{:S(2)}, u32[]{:S(2)}) %collective-permute-start.8) | collective-permute-done | bytes 98336 | tf_op jit(solution)/shard_map/ppermute | solution.py:35
  141.5 2.8 %collective-permute-start.10 = (bf16[1,64,768]{2,1,0:T(8,128)(2,1)S(1)}, bf16[1,64,768]{2,1,0:T(8,128)(2,1)S(1)}, u32[]{:S(2)}, u32[]{:S(2)}) collective-permute-start(bf16[1,64,768]{2,1,0:T(8,128)(2,1)S(1)} %fusion), channel_id=1, source_target_pairs={{0,64},{64,0},{1,65},{65,1},{2,66},{66,2},{3,67},{67,3},{4,68},{68... | collective-permute-start | bytes 294920 | tf_op jit(solution)/shard_map/ppermute | solution.py:35
  144.7 2.8 %collective-permute-start.21 = (bf16[1,64,768]{2,1,0:T(8,128)(2,1)S(1)}, bf16[1,64,768]{2,1,0:T(8,128)(2,1)S(1)}, u32[]{:S(2)}, u32[]{:S(2)}) collective-permute-start(bf16[1,64,768]{2,1,0:T(8,128)(2,1)S(1)} %bitcast.38), channel_id=1, source_target_pairs={{0,64},{64,0},{1,65},{65,1},{2,66},{66,2},{3,67},{67,3},{4,68},{68... | collective-permute-start | bytes 294920 | tf_op jit(solution)/shard_map/ppermute | solution.py:35
  147.7 3.2 %collective-permute-done.21 = bf16[1,64,768]{2,1,0:T(8,128)(2,1)S(1)} collective-permute-done((bf16[1,64,768]{2,1,0:T(8,128)(2,1)S(1)}, bf16[1,64,768]{2,1,0:T(8,128)(2,1)S(1)}, u32[]{:S(2)}, u32[]{:S(2)}) %collective-permute-start.21) | collective-permute-done | bytes 98336 | tf_op jit(solution)/shard_map/ppermute | solution.py:35
  (60 shorter events, 24.0 us)
Async XLA Ops:
  0.6 14.8 %copy-start.7 = (s32[4]{0:T(128)S(1)}, s32[4]{0:T(128)}, u32[]{:S(2)}) copy-start(s32[4]{0:T(128)} %constant.21.clone) | copy-start | bytes 52
  0.6 8.9 %copy-start = (bf16[1,64,768]{2,1,0:T(8,128)(2,1)S(1)}, bf16[1,64,768]{2,1,0:T(8,128)(2,1)}, u32[]{:S(2)}) copy-start(bf16[1,64,768]{2,1,0:T(8,128)(2,1)} %param.13) | copy-start | bytes 294916
  3.8 16.5 %copy-start.4 = (bf16[384,64]{1,0:T(8,128)(2,1)S(1)}, bf16[384,64]{1,0:T(8,128)(2,1)}, u32[]{:S(2)}) copy-start(bf16[384,64]{1,0:T(8,128)(2,1)} %get-tuple-element.46.table) | copy-start | bytes 147460
  3.8 23.8 %all-to-all-start = ((bf16[16,24,1536]{2,1,0:T(8,128)(2,1)}), bf16[16,24,1536]{2,1,0:T(8,128)(2,1)S(1)}, u32[]{:S(2)}, u32[]{:S(2)}) async-start(bf16[16,24,1536]{2,1,0:T(8,128)(2,1)} %bitcast.48), calls=%async_computation | async-start | bytes 2359296 | tf_op jit(solution)/shard_map/all_to_all | solution.py:487
  9.5 7.5 %collective-permute-start = (bf16[64,768]{1,0:T(8,128)(2,1)S(1)}, bf16[64,768]{1,0:T(8,128)(2,1)S(1)}, u32[]{:S(2)}, u32[]{:S(2)}) collective-permute-start(bf16[64,768]{1,0:T(8,128)(2,1)S(1)} %bitcast.31), channel_id=1, source_target_pairs={{0,1},{1,2},{2,3},{3,0},{4,5},{5,6},{6,7},{7,4},{8,9},{9,10},{10,1... | collective-permute-start | bytes 294920 | tf_op jit(solution)/shard_map/ppermute | solution.py:35
  11.5 7.0 %collective-permute-start.1 = (bf16[64,768]{1,0:T(8,128)(2,1)S(1)}, bf16[64,768]{1,0:T(8,128)(2,1)S(1)}, u32[]{:S(2)}, u32[]{:S(2)}) collective-permute-start(bf16[64,768]{1,0:T(8,128)(2,1)S(1)} %bitcast.32), channel_id=1, source_target_pairs={{0,3},{1,0},{2,1},{3,2},{4,7},{5,4},{6,5},{7,6},{8,11},{9,8},{10,9... | collective-permute-start | bytes 294920 | tf_op jit(solution)/shard_map/ppermute | solution.py:35
  13.7 6.6 %collective-permute-start.2 = (bf16[64,768]{1,0:T(8,128)(2,1)S(1)}, bf16[64,768]{1,0:T(8,128)(2,1)S(1)}, u32[]{:S(2)}, u32[]{:S(2)}) collective-permute-start(bf16[64,768]{1,0:T(8,128)(2,1)S(1)} %bitcast.33), channel_id=1, source_target_pairs={{0,2},{1,3},{2,0},{3,1},{4,6},{5,7},{6,4},{7,5},{8,10},{9,11},{10,... | collective-permute-start | bytes 294920 | tf_op jit(solution)/shard_map/ppermute | solution.py:35
  27.6 40.7 %all-to-all-start.2 = ((bf16[16,24,3072]{2,1,0:T(8,128)(2,1)}), bf16[16,24,3072]{2,1,0:T(8,128)(2,1)S(1)}, u32[]{:S(2)}, u32[]{:S(2)}) async-start(bf16[16,24,3072]{2,1,0:T(8,128)(2,1)} %bitcast.45), calls=%async_computation.2 | async-start | bytes 4718592 | tf_op jit(solution)/shard_map/all_to_all | solution.py:487
  31.4 17.8 %collective-permute-start.3 = (bf16[384,768]{1,0:T(8,128)(2,1)S(1)}, bf16[384,768]{1,0:T(8,128)(2,1)S(1)}, u32[]{:S(2)}, u32[]{:S(2)}) collective-permute-start(bf16[384,768]{1,0:T(8,128)(2,1)S(1)} %get-tuple-element.87.refs_0_), channel_id=1, source_target_pairs={{0,1},{1,2},{2,3},{3,0},{4,5},{5,6},{6,7},{7,4},{8,9},{9,10},{10,1... | collective-permute-start | bytes 1769480 | tf_op jit(solution)/shard_map/ppermute | solution.py:35
  33.4 15.8 %collective-permute-start.4 = (bf16[384,768]{1,0:T(8,128)(2,1)S(1)}, bf16[384,768]{1,0:T(8,128)(2,1)S(1)}, u32[]{:S(2)}, u32[]{:S(2)}) collective-permute-start(bf16[384,768]{1,0:T(8,128)(2,1)S(1)} %get-tuple-element.87.refs_0_), channel_id=1, source_target_pairs={{0,3},{1,0},{2,1},{3,2},{4,7},{5,4},{6,5},{7,6},{8,11},{9,8},{10,9... | collective-permute-start | bytes 1769480 | tf_op jit(solution)/shard_map/ppermute | solution.py:35
  49.3 11.1 %collective-permute-start.5 = (bf16[192,768]{1,0:T(8,128)(2,1)S(1)}, bf16[192,768]{1,0:T(8,128)(2,1)S(1)}, u32[]{:S(2)}, u32[]{:S(2)}) collective-permute-start(bf16[192,768]{1,0:T(8,128)(2,1)S(1)} %get-tuple-element.49.refs_1_), channel_id=1, source_target_pairs={{0,1},{1,2},{2,3},{3,0},{4,5},{5,6},{6,7},{7,4},{8,9},{9,10},{10,1... | collective-permute-start | bytes 884744 | tf_op jit(solution)/shard_map/ppermute | solution.py:35
  50.6 9.8 %collective-permute-start.6 = (bf16[192,768]{1,0:T(8,128)(2,1)S(1)}, bf16[192,768]{1,0:T(8,128)(2,1)S(1)}, u32[]{:S(2)}, u32[]{:S(2)}) collective-permute-start(bf16[192,768]{1,0:T(8,128)(2,1)S(1)} %get-tuple-element.50.refs_2_), channel_id=1, source_target_pairs={{0,3},{1,0},{2,1},{3,2},{4,7},{5,4},{6,5},{7,6},{8,11},{9,8},{10,9... | collective-permute-start | bytes 884744 | tf_op jit(solution)/shard_map/ppermute | solution.py:35
  57.0 16.9 %collective-permute-start.11 = (bf16[384,768]{1,0:T(8,128)(2,1)S(1)}, bf16[384,768]{1,0:T(8,128)(2,1)S(1)}, u32[]{:S(2)}, u32[]{:S(2)}) collective-permute-start(bf16[384,768]{1,0:T(8,128)(2,1)S(1)} %shard_map.131.refs_0_), channel_id=1, source_target_pairs={{0,1},{1,2},{2,3},{3,0},{4,5},{5,6},{6,7},{7,4},{8,9},{9,10},{10,1... | collective-permute-start | bytes 1769480 | tf_op jit(solution)/shard_map/ppermute | solution.py:35
  57.2 16.8 %collective-permute-start.12 = (bf16[384,768]{1,0:T(8,128)(2,1)S(1)}, bf16[384,768]{1,0:T(8,128)(2,1)}, u32[]{:S(2)}, u32[]{:S(2)}) collective-permute-start(bf16[384,768]{1,0:T(8,128)(2,1)S(1)} %shard_map.131.refs_0_), channel_id=1, source_target_pairs={{0,3},{1,0},{2,1},{3,2},{4,7},{5,4},{6,5},{7,6},{8,11},{9,8},{10,9... | collective-permute-start | bytes 1769480 | tf_op jit(solution)/shard_map/ppermute | solution.py:35
  68.3 49.2 %all-to-all-start.1 = ((bf16[16,24,3072]{2,1,0:T(8,128)(2,1)}), bf16[16,24,3072]{2,1,0:T(8,128)(2,1)}, u32[]{:S(2)}, u32[]{:S(2)}) async-start(bf16[16,24,3072]{2,1,0:T(8,128)(2,1)} %bitcast.47), calls=%async_computation.1 | async-start | bytes 4718592 | tf_op jit(solution)/shard_map/all_to_all | solution.py:487
  75.1 13.3 %collective-permute-start.13 = (bf16[192,768]{1,0:T(8,128)(2,1)S(1)}, bf16[192,768]{1,0:T(8,128)(2,1)S(1)}, u32[]{:S(2)}, u32[]{:S(2)}) collective-permute-start(bf16[192,768]{1,0:T(8,128)(2,1)S(1)} %get-tuple-element.65), channel_id=1, source_target_pairs={{0,1},{1,2},{2,3},{3,0},{4,5},{5,6},{6,7},{7,4},{8,9},{9,10},{10,1... | collective-permute-start | bytes 884744 | tf_op jit(solution)/shard_map/ppermute | solution.py:35
  75.2 13.2 %collective-permute-start.14 = (bf16[192,768]{1,0:T(8,128)(2,1)S(1)}, bf16[192,768]{1,0:T(8,128)(2,1)S(1)}, u32[]{:S(2)}, u32[]{:S(2)}) collective-permute-start(bf16[192,768]{1,0:T(8,128)(2,1)S(1)} %get-tuple-element.66), channel_id=1, source_target_pairs={{0,3},{1,0},{2,1},{3,2},{4,7},{5,4},{6,5},{7,6},{8,11},{9,8},{10,9... | collective-permute-start | bytes 884744 | tf_op jit(solution)/shard_map/ppermute | solution.py:35
  97.9 10.0 %collective-permute-start.15 = (bf16[192,768]{1,0:T(8,128)(2,1)S(1)}, bf16[192,768]{1,0:T(8,128)(2,1)S(1)}, u32[]{:S(2)}, u32[]{:S(2)}) collective-permute-start(bf16[192,768]{1,0:T(8,128)(2,1)S(1)} %get-tuple-element.79), channel_id=1, source_target_pairs={{0,1},{1,2},{2,3},{3,0},{4,5},{5,6},{6,7},{7,4},{8,9},{9,10},{10,1... | collective-permute-start | bytes 884744 | tf_op jit(solution)/shard_map/ppermute | solution.py:35
  98.0 9.9 %collective-permute-start.16 = (bf16[192,768]{1,0:T(8,128)(2,1)S(1)}, bf16[192,768]{1,0:T(8,128)(2,1)S(1)}, u32[]{:S(2)}, u32[]{:S(2)}) collective-permute-start(bf16[192,768]{1,0:T(8,128)(2,1)S(1)} %get-tuple-element.80), channel_id=1, source_target_pairs={{0,3},{1,0},{2,1},{3,2},{4,7},{5,4},{6,5},{7,6},{8,11},{9,8},{10,9... | collective-permute-start | bytes 884744 | tf_op jit(solution)/shard_map/ppermute | solution.py:35
  108.8 11.1 %collective-permute-start.20 = (bf16[192,768]{1,0:T(8,128)(2,1)}, bf16[192,768]{1,0:T(8,128)(2,1)S(1)}, u32[]{:S(2)}, u32[]{:S(2)}) collective-permute-start(bf16[192,768]{1,0:T(8,128)(2,1)} %get-tuple-element.84), channel_id=1, source_target_pairs={{0,3},{1,0},{2,1},{3,2},{4,7},{5,4},{6,5},{7,6},{8,11},{9,8},{10,9... | collective-permute-start | bytes 884744 | tf_op jit(solution)/shard_map/ppermute | solution.py:35
  111.7 11.2 %collective-permute-start.18 = (bf16[192,768]{1,0:T(8,128)(2,1)S(1)}, bf16[192,768]{1,0:T(8,128)(2,1)S(1)}, u32[]{:S(2)}, u32[]{:S(2)}) collective-permute-start(bf16[192,768]{1,0:T(8,128)(2,1)S(1)} %get-tuple-element.82), channel_id=1, source_target_pairs={{0,1},{1,2},{2,3},{3,0},{4,5},{5,6},{6,7},{7,4},{8,9},{9,10},{10,1... | collective-permute-start | bytes 884744 | tf_op jit(solution)/shard_map/ppermute | solution.py:35
  111.7 11.5 %collective-permute-start.19 = (bf16[192,768]{1,0:T(8,128)(2,1)S(1)}, bf16[192,768]{1,0:T(8,128)(2,1)S(1)}, u32[]{:S(2)}, u32[]{:S(2)}) collective-permute-start(bf16[192,768]{1,0:T(8,128)(2,1)S(1)} %get-tuple-element.83), channel_id=1, source_target_pairs={{0,3},{1,0},{2,1},{3,2},{4,7},{5,4},{6,5},{7,6},{8,11},{9,8},{10,9... | collective-permute-start | bytes 884744 | tf_op jit(solution)/shard_map/ppermute | solution.py:35
  115.0 11.5 %collective-permute-start.17 = (bf16[192,768]{1,0:T(8,128)(2,1)}, bf16[192,768]{1,0:T(8,128)(2,1)S(1)}, u32[]{:S(2)}, u32[]{:S(2)}) collective-permute-start(bf16[192,768]{1,0:T(8,128)(2,1)} %get-tuple-element.81), channel_id=1, source_target_pairs={{0,1},{1,2},{2,3},{3,0},{4,5},{5,6},{6,7},{7,4},{8,9},{9,10},{10,1... | collective-permute-start | bytes 884744 | tf_op jit(solution)/shard_map/ppermute | solution.py:35
  119.8 7.7 %copy-start.6 = (bf16[64,768]{1,0:T(8,128)(2,1)}, bf16[64,768]{1,0:T(8,128)(2,1)S(1)}, u32[]{:S(2)}) copy-start(bf16[64,768]{1,0:T(8,128)(2,1)S(1)} %get-tuple-element.60) | copy-start | bytes 294916
  119.9 24.5 %copy-start.1 = (bf16[1,64,768]{2,1,0:T(8,128)(2,1)S(1)}, bf16[1,64,768]{2,1,0:T(8,128)(2,1)}, u32[]{:S(2)}) copy-start(bf16[1,64,768]{2,1,0:T(8,128)(2,1)} %param.13) | copy-start | bytes 294916
  119.9 24.5 %copy-start.5 = (bf16[384,128]{1,0:T(8,128)(2,1)S(1)}, bf16[384,128]{1,0:T(8,128)(2,1)}, u32[]{:S(2)}) copy-start(bf16[384,128]{1,0:T(8,128)(2,1)} %get-tuple-element.63.table) | copy-start | bytes 294916
  127.5 16.9 %all-to-all-start.3 = ((bf16[16,24,768]{2,1,0:T(8,128)(2,1)}), bf16[16,24,768]{2,1,0:T(8,128)(2,1)S(1)}, u32[]{:S(2)}, u32[]{:S(2)}) async-start(bf16[16,24,768]{2,1,0:T(8,128)(2,1)} %bitcast.21), calls=%async_computation.3 | async-start | bytes 1179648 | tf_op jit(solution)/shard_map/all_to_all | solution.py:487
  132.8 5.6 %collective-permute-start.7 = (bf16[64,768]{1,0:T(8,128)(2,1)}, bf16[64,768]{1,0:T(8,128)(2,1)S(1)}, u32[]{:S(2)}, u32[]{:S(2)}) collective-permute-start(bf16[64,768]{1,0:T(8,128)(2,1)} %copy-done.6), channel_id=1, source_target_pairs={{0,3},{1,0},{2,1},{3,2},{4,7},{5,4},{6,5},{7,6},{8,11},{9,8},{10,9... | collective-permute-start | bytes 294920 | tf_op jit(solution)/shard_map/ppermute | solution.py:35
  133.3 8.1 %collective-permute-start.8 = (bf16[64,768]{1,0:T(8,128)(2,1)S(1)}, bf16[64,768]{1,0:T(8,128)(2,1)S(1)}, u32[]{:S(2)}, u32[]{:S(2)}) collective-permute-start(bf16[64,768]{1,0:T(8,128)(2,1)S(1)} %get-tuple-element.61), channel_id=1, source_target_pairs={{0,1},{1,2},{2,3},{3,0},{4,5},{5,6},{6,7},{7,4},{8,9},{9,10},{10,1... | collective-permute-start | bytes 294920 | tf_op jit(solution)/shard_map/ppermute | solution.py:35
  134.9 6.5 %collective-permute-start.9 = (bf16[64,768]{1,0:T(8,128)(2,1)S(1)}, bf16[64,768]{1,0:T(8,128)(2,1)S(1)}, u32[]{:S(2)}, u32[]{:S(2)}) collective-permute-start(bf16[64,768]{1,0:T(8,128)(2,1)S(1)} %get-tuple-element.62), channel_id=1, source_target_pairs={{0,2},{1,3},{2,0},{3,1},{4,6},{5,7},{6,4},{7,5},{8,10},{9,11},{10,... | collective-permute-start | bytes 294920 | tf_op jit(solution)/shard_map/ppermute | solution.py:35
  141.5 6.2 %collective-permute-start.10 = (bf16[1,64,768]{2,1,0:T(8,128)(2,1)S(1)}, bf16[1,64,768]{2,1,0:T(8,128)(2,1)S(1)}, u32[]{:S(2)}, u32[]{:S(2)}) collective-permute-start(bf16[1,64,768]{2,1,0:T(8,128)(2,1)S(1)} %fusion), channel_id=1, source_target_pairs={{0,64},{64,0},{1,65},{65,1},{2,66},{66,2},{3,67},{67,3},{4,68},{68... | collective-permute-start | bytes 294920 | tf_op jit(solution)/shard_map/ppermute | solution.py:35
  144.7 6.2 %collective-permute-start.21 = (bf16[1,64,768]{2,1,0:T(8,128)(2,1)S(1)}, bf16[1,64,768]{2,1,0:T(8,128)(2,1)S(1)}, u32[]{:S(2)}, u32[]{:S(2)}) collective-permute-start(bf16[1,64,768]{2,1,0:T(8,128)(2,1)S(1)} %bitcast.38), channel_id=1, source_target_pairs={{0,64},{64,0},{1,65},{65,1},{2,66},{66,2},{3,67},{67,3},{4,68},{68... | collective-permute-start | bytes 294920 | tf_op jit(solution)/shard_map/ppermute | solution.py:35
  (2 other events, 5.1 us)
